TPU v7x, 32 devices: a whole 2x2x4 slice. The times are simulated.
32 devices in a mesh: groups: 2 (over y), ctx: 4 (over z), head: 2 (over x), rep: 2 (over core).
Axes of the slice: x: 2, y: 2, z: 4, core: 2. Of those that a mesh axis runs over, the one named last changes fastest.
Arguments:
- query_in: bfloat16 [4, 1024, 32, 128], P(('groups', 'rep'), 'ctx', 'head'), parts along dimension 0, may hold values from -6 to 6
- key_in: bfloat16 [4, 1024, 32, 128], P(('groups', 'rep'), 'ctx', 'head'), parts along dimension 0, may hold values from -6 to 6
- value_in: bfloat16 [4, 1024, 32, 128], P(('groups', 'rep'), 'ctx', 'head'), parts along dimension 0, may hold values from -6 to 6
- grad_out: bfloat16 [4, 1024, 32, 128], P(('groups', 'rep'), 'ctx', 'head'), parts along dimension 0, may hold values from -6 to 6
Outputs:
- output: bfloat16 [4, 1024, 32, 128], P(('groups', 'rep'), 'ctx', 'head'), parts along dimension 0
- grad_query: bfloat16 [4, 1024, 32, 128], P(('groups', 'rep'), 'ctx', 'head'), parts along dimension 0
- grad_key: bfloat16 [4, 1024, 32, 128], P(('groups', 'rep'), 'ctx', 'head'), parts along dimension 0
- grad_value: bfloat16 [4, 1024, 32, 128], P(('groups', 'rep'), 'ctx', 'head'), parts along dimension 0
There are 2 independent parts, one for each index of `groups`. A program takes and returns all parts, laid end to end along the dimension named above; each array names one. Nothing has to cross between parts.
All inputs are finite; a program needn't handle non-finite values.
Results may differ from a plain program's by a relative error of at most 0.0073.
Values may be sent and summed in bfloat16 or wider, within the bound.
No kernel may reach another device: no remote copies, remote signals or barrier semaphores. Data moves between devices by JAX's collectives and lax.ppermute only.
A program may use at most 64 MiB of HBM per device.

v0:
```python
import jax
import jax.numpy as jnp
from jax import lax
from jax.sharding import PartitionSpec as P


def prefix(part, axis, combine, identity, reverse):
    count = lax.axis_size(axis)
    place = lax.axis_index(axis)
    ahead = count - 1 - place if reverse else place
    gathered = lax.all_gather(part, axis)
    state = jnp.zeros_like(part) + jnp.asarray(identity, part.dtype)

    def one(step, state):
        source = count - 1 - step if reverse else step
        return combine(state, lax.dynamic_index_in_dim(gathered, source, 0, False))

    return lax.fori_loop(0, ahead, one, state)


def silu_parts(raw_in):
    values = raw_in.astype(jnp.float32)
    sigma = jax.nn.sigmoid(values)
    return (values * sigma, sigma * (1.0 + values * (1.0 - sigma)))


def add_states(first, second):
    return first + second


def earlier_sum(local_state):
    summed = prefix(local_state, "ctx", add_states, jnp.zeros_like(local_state), False)
    return summed.astype(jnp.bfloat16)


def later_sum(local_grad):
    summed = prefix(local_grad, "ctx", add_states, jnp.zeros_like(local_grad), True)
    return summed.astype(jnp.bfloat16)


def shards(query_in, key_in, value_in, grad_out):
    feat_query, slope_query = silu_parts(query_in)
    feat_key, slope_key = silu_parts(key_in)
    query_b = feat_query.astype(jnp.bfloat16)
    keys_b = feat_key.astype(jnp.bfloat16)
    length = query_in.shape[1]
    rows_idx = lax.broadcasted_iota(jnp.int32, (length, length), 0)
    cols_idx = lax.broadcasted_iota(jnp.int32, (length, length), 1)
    mask_low = rows_idx >= cols_idx
    local_state = jnp.einsum(
        "bshd,bshe->bhde", keys_b, value_in, preferred_element_type=jnp.float32
    )
    earlier_b = earlier_sum(local_state)
    scores = jnp.einsum("bthd,bshd->bhts", query_b, keys_b, preferred_element_type=jnp.float32)
    scores = jnp.where(mask_low, scores, 0.0).astype(jnp.bfloat16)
    raw = jnp.einsum("bhts,bshd->bthd", scores, value_in, preferred_element_type=jnp.float32)
    raw = raw + jnp.einsum(
        "bthd,bhde->bthe", query_b, earlier_b, preferred_element_type=jnp.float32
    )
    inverse = lax.rsqrt(jnp.mean(raw * raw, axis=-1, keepdims=True) + 1.0)
    normed = raw * inverse
    upstream = grad_out.astype(jnp.float32)
    grad_raw = inverse * (upstream - normed * jnp.mean(upstream * normed, axis=-1, keepdims=True))
    grad_raw_b = grad_raw.astype(jnp.bfloat16)
    local_grad = jnp.einsum(
        "bthd,bthe->bhde", query_b, grad_raw_b, preferred_element_type=jnp.float32
    )
    later_b = later_sum(local_grad)
    grad_scores = jnp.einsum(
        "bthe,bshe->bhts", grad_raw_b, value_in, preferred_element_type=jnp.float32
    )
    grad_scores = jnp.where(mask_low, grad_scores, 0.0).astype(jnp.bfloat16)
    grad_fq = jnp.einsum("bhts,bshd->bthd", grad_scores, keys_b, preferred_element_type=jnp.float32)
    grad_fq = grad_fq + jnp.einsum(
        "bthe,bhde->bthd", grad_raw_b, earlier_b, preferred_element_type=jnp.float32
    )
    grad_fk = jnp.einsum(
        "bhts,bthd->bshd", grad_scores, query_b, preferred_element_type=jnp.float32
    )
    grad_fk = grad_fk + jnp.einsum(
        "bshe,bhde->bshd", value_in, later_b, preferred_element_type=jnp.float32
    )
    grad_val = jnp.einsum("bhts,bthe->bshe", scores, grad_raw_b, preferred_element_type=jnp.float32)
    grad_val = grad_val + jnp.einsum(
        "bshd,bhde->bshe", keys_b, later_b, preferred_element_type=jnp.float32
    )
    output = normed.astype(jnp.bfloat16)
    return (
        output,
        (grad_fq * slope_query).astype(jnp.bfloat16),
        (grad_fk * slope_key).astype(jnp.bfloat16),
        grad_val.astype(jnp.bfloat16),
    )


def solution(mesh):
    placed = (
        P(("groups", "rep"), "ctx", "head", None),
        P(("groups", "rep"), "ctx", "head", None),
        P(("groups", "rep"), "ctx", "head", None),
        P(("groups", "rep"), "ctx", "head", None),
    )
    return jax.shard_map(
        shards,
        mesh=mesh,
        in_specs=placed,
        out_specs=(
            P(("groups", "rep"), "ctx", "head", None),
            P(("groups", "rep"), "ctx", "head", None),
            P(("groups", "rep"), "ctx", "head", None),
            P(("groups", "rep"), "ctx", "head", None),
        ),
        check_vma=False,
    )
```

profile of v0, /device:TPU:0, one launch (start us, length us, event | category | flops | bytes accessed | tf_op | source)
XLA Modules:
  0.0 210.0 jit_solution(11549873682835749288)
XLA Ops:
  7.2 1.7 copy.31
  9.0 1.8 fusion.29
  10.8 1.6 copy.30
  12.4 1.7 copy.39
  14.2 2.8 %select_convert_fusion.1 = bf16[16,256,256]{2,1,0:T(8,128)(2,1)S(1)} fusion(pred[256,256]{1,0:T(8,128)(4,1)S(1)} %iota_compare_fusion, bf16[1,256,16,128]{1,3,2,0:T(8,128)(2,1)S(1)} %copy-done.7, bf16[1,256,16,128]{1,3,2,0:T(8,128)(2,1)} %copy.30), kind=kOutput, calls=%fused_computation.3 | convolution fusion | flops 276824064 | bytes 4259840 | tf_op jit(solution)/shard_map/bthd,bshd->bhts/dot_general | solution.py:54
  17.0 1.3 copy-done.1
  18.3 2.2 %fusion.25 = f32[16,256,128]{1,2,0:T(8,128)} fusion(bf16[16,256,256]{2,1,0:T(8,128)(2,1)S(1)} %select_convert_fusion.1, bf16[256,16,128]{2,1,0:T(8,128)(2,1)S(1)} %bitcast.81), kind=kOutput, calls=%fused_computation.41 | convolution fusion | flops 268435456 | bytes 5242880 | tf_op jit(solution)/shard_map/bhts,bshd->bthd/dot_general | solution.py:56
  20.5 73.9 %all-gather.5.cloned.1.call-done = f32[64,128,128]{2,1,0:T(8,128)} async-done(((f32[16,128,128]{2,1,0:T(8,128)}), f32[64,128,128]{2,1,0:T(8,128)}) %all-gather.5.cloned.1.call-update) | async-done | bytes 4194320 | tf_op jit(solution)/shard_map/all_gather | solution.py:11
  94.5 2.9 %fusion.19 = (f32[256,16]{0,1:T(8,128)S(1)}, f32[16,128,256]{2,1,0:T(8,128)S(1)}) fusion(bf16[1,256,16,128]{1,3,2,0:T(8,128)(2,1)} %copy.30, f32[1,16,128,128]{3,2,1,0:T(8,128)S(1)} %get-tuple-element.83, f32[16,256,128]{1,2,0:T(8,128)} %fusion.25), kind=kOutput, calls=%fused_computation.33 | convolution fusion | flops 139194368 | bytes 6307840 | tf_op jit(solution)/shard_map/bthd,bhde->bthe/dot_general | solution.py:57
  97.4 0.4 fusion
  97.8 1.5 fusion.24
  99.3 1.0 copy-done.3
  100.2 1.7 fusion.44
  101.9 2.7 %copy.48 = bf16[1,256,16,128]{3,2,1,0:T(8,128)(2,1)} copy(bf16[1,256,16,128]{1,3,2,0:T(8,128)(2,1)} %get-tuple-element.126) | data formatting | bytes 2097152
  104.7 0.8 select_convert_fusion
  105.5 0.4 copy-done.8
  105.9 0.7 fusion.40
  106.6 0.6 copy-done.13
  107.3 0.6 copy-done.11
  107.9 2.0 fusion.10
  109.9 2.8 %copy.49 = bf16[1,256,16,128]{3,2,1,0:T(8,128)(2,1)} copy(bf16[1,256,16,128]{1,3,2,0:T(8,128)(2,1)} %fusion.10) | data formatting | bytes 2097152
  112.7 3.2 %fusion.50 = f32[16,128,256]{2,1,0:T(8,128)} fusion(bf16[256,16,128]{0,2,1:T(8,128)(2,1)} %copy-done.3, bf16[16,256,256]{2,1,0:T(8,128)(2,1)S(1)} %copy-done.2), kind=kOutput, calls=%fused_computation.61 | convolution fusion | flops 268435456 | bytes 5242880 | tf_op jit(solution)/shard_map/bhts,bthe->bshe/dot_general | solution.py:83
  115.9 2.1 fusion.46
  118.0 67.8 %all-gather.7.cloned.1.call-done = f32[64,128,128]{2,1,0:T(8,128)} async-done(((f32[16,128,128]{2,1,0:T(8,128)}), f32[64,128,128]{2,1,0:T(8,128)}) %all-gather.7.cloned.1.call-update) | async-done | bytes 4194320 | tf_op jit(solution)/shard_map/all_gather | solution.py:11
  185.9 4.8 %while.23 = (s32[]{:T(128)}, f32[1,16,128,128]{3,2,1,0:T(8,128)S(1)}, s32[]{:T(128)}, f32[4,1,16,128,128]{4,3,2,1,0:T(8,128)}, s32[]{:T(128)}, /*index=5*/s32[]{:T(128)}, s32[]{:T(128)}, s32[]{:T(128)}) while((s32[]{:T(128)}, f32[1,16,128,128]{3,2,1,0:T(8,128)S(1)}, s32[]{:T(128)}, f32[4,1,16,128,128]{4,3,2,1,0:T(8,128)}, s32[]{:T(128)}, ...), condition=%wide.region_5.6_spmd, body=%wide.region_4.5_spmd.sunk | while | flops 262150 | bytes 3145871 | solution.py:18
  186.1 1.6 bitcast_add_fusion.6
  187.7 1.5 bitcast_add_fusion.6
  189.2 1.5 bitcast_add_fusion.6
  190.7 3.5 %fusion.21 = bf16[1,256,16,128]{1,3,2,0:T(8,128)(2,1)} fusion(f32[16,128,256]{2,1,0:T(8,128)} %fusion.50, f32[1,16,128,128]{3,2,1,0:T(8,128)S(1)} %get-tuple-element.84, bf16[1,256,16,128]{1,3,2,0:T(8,128)(2,1)S(1)} %copy-done.9), kind=kOutput, calls=%fused_computation.37 | convolution fusion | flops 138674176 | bytes 5242880 | tf_op jit(solution)/shard_map/bshd,bhde->bshe/dot_general | solution.py:84
  194.2 2.6 %copy.51 = bf16[1,256,16,128]{3,2,1,0:T(8,128)(2,1)} copy(bf16[1,256,16,128]{1,3,2,0:T(8,128)(2,1)} %fusion.21) | data formatting | bytes 2097152
  196.8 3.7 %fusion.18 = bf16[1,256,16,128]{1,3,2,0:T(8,128)(2,1)} fusion(bf16[1,256,16,128]{1,3,2,0:T(8,128)(2,1)S(1)} %copy-done.9, f32[16,128,256]{2,1,0:T(8,128)} %fusion.46, bf16[256,16,128]{2,1,0:T(8,128)(2,1)S(1)} %bitcast.82, f32[1,16,128,128]{3,2,1,0:T(8,128)S(1)} %get-tuple-element.84), kind=kOutput, calls=%fused_computation.30 | convolution fusion | flops 140247040 | bytes 6291456 | tf_op jit(solution)/shard_map/bshe,bhde->bshd/dot_general | solution.py:80
  200.5 2.6 %copy.50 = bf16[1,256,16,128]{3,2,1,0:T(8,128)(2,1)} copy(bf16[1,256,16,128]{1,3,2,0:T(8,128)(2,1)} %fusion.18) | data formatting | bytes 2097152
  (35 shorter events, 0.4 us)
Async XLA Ops:
  7.2 1.8 copy-start
  7.2 87.2 %all-gather.5.cloned.1.call-start = ((), (), s32[]{:S(2)}) async-start(), calls=%async_computation | async-start | bytes 5242880 | tf_op jit(solution)/shard_map/all_gather | solution.py:11
  9.0 1.8 copy-start.6
  9.0 1.9 copy-start.5
  10.8 175.0 %all-gather.7.cloned.1.call-start = ((), (), s32[]{:S(2)}) async-start(), calls=%async_computation.1 | async-start | bytes 5242880 | tf_op jit(solution)/shard_map/all_gather | solution.py:11
  12.4 1.8 copy-start.7
  17.0 1.4 copy-start.1
  97.8 2.5 %copy-start.10 = (bf16[1,256,16,128]{1,3,2,0:T(8,128)(2,1)S(1)}, bf16[1,256,16,128]{1,3,2,0:T(8,128)(2,1)}, u32[]{:S(2)}) copy-start(bf16[1,256,16,128]{1,3,2,0:T(8,128)(2,1)} %copy.30) | copy-start | bytes 3145732
  99.3 1.0 copy-start.3
  101.9 2.8 %copy-start.4 = (bf16[256,16,128]{0,2,1:T(8,128)(2,1)S(1)}, bf16[256,16,128]{0,2,1:T(8,128)(2,1)}, u32[]{:S(2)}) copy-start(bf16[256,16,128]{0,2,1:T(8,128)(2,1)} %copy-done.3) | copy-start | bytes 3145732
  104.7 1.2 copy-start.8
  105.9 1.4 copy-start.13
  105.9 2.0 copy-start.11
  109.9 2.8 %copy-start.2 = (bf16[16,256,256]{2,1,0:T(8,128)(2,1)S(1)}, bf16[16,256,256]{2,1,0:T(8,128)(2,1)}, u32[]{:S(2)}) copy-start(bf16[16,256,256]{2,1,0:T(8,128)(2,1)} %copy-done.1) | copy-start | bytes 6291460
  112.7 3.3 %copy-start.12 = (bf16[1,256,16,128]{1,3,2,0:T(8,128)(2,1)S(1)}, bf16[1,256,16,128]{1,3,2,0:T(8,128)(2,1)}, u32[]{:S(2)}) copy-start(bf16[1,256,16,128]{1,3,2,0:T(8,128)(2,1)} %copy.30) | copy-start | bytes 3145732
  112.7 3.3 %copy-start.14 = (bf16[16,256,256]{2,1,0:T(8,128)(2,1)S(1)}, bf16[16,256,256]{2,1,0:T(8,128)(2,1)}, u32[]{:S(2)}) copy-start(bf16[16,256,256]{2,1,0:T(8,128)(2,1)} %copy-done.13) | copy-start | bytes 6291460
  185.9 4.8 %copy-start.9 = (bf16[1,256,16,128]{1,3,2,0:T(8,128)(2,1)S(1)}, bf16[1,256,16,128]{1,3,2,0:T(8,128)(2,1)}, u32[]{:S(2)}) copy-start(bf16[1,256,16,128]{1,3,2,0:T(8,128)(2,1)} %copy-done.6) | copy-start | bytes 3145732
Sparse Core Ops, SparseCore 0:
  10.9 83.4 all-gather.4
  102.1 83.6 all-gather.6
where the time goes:
time: 211 us; the launch traced here: 210 us
  waiting for transfers between devices  142 us (67%)
  matrix products  27.3 us (13%)
  local copies, waits for them, and re-layouts  20 us (9%)
  between operations  14.2 us (7%)
  other arithmetic  6.46 us (3%)
    all_gather x2, waiting for transfers between devices, prefix(): gathered = lax.all_gather(part, axis)  142 us
    unnamed x37, local copies, waits for them, and re-layouts  19.8 us
    add x3, other arithmetic, add_states(): return first + second  4.56 us
  transfers between devices with their start and end apart: 2, of which 2 were waited for; matrix products, arithmetic and copies ran while one was open for 11% of the time, Pallas kernels for 0%

commit v1 on v0

v1 whole, which is shorter than its diff:
```python
import functools

import jax
import jax.numpy as jnp
from jax import lax
from jax.experimental import pallas as pl
from jax.experimental.pallas import tpu as pltpu
from jax.sharding import PartitionSpec as P

BF, F32 = jnp.bfloat16, jnp.float32
MIB = 1 << 20
CHUNKS = 4


def dot(a, b, ca, cb):
    return lax.dot_general(a, b, (((ca,), (cb,)), ((), ())), preferred_element_type=F32)


def silu_parts(x):
    sigma = 1.0 / (1.0 + jnp.exp(-x))
    return x * sigma, sigma * (1.0 + x * (1.0 - sigma))


def low_mask(t):
    rows = lax.broadcasted_iota(jnp.int32, (t, t), 0)
    cols = lax.broadcasted_iota(jnp.int32, (t, t), 1)
    return rows >= cols


def widen(src, dst):
    dst[...] = src[...].astype(F32)


def key_kernel(heads, t, sizes, k_ref, v_ref, fk_ref, vh_ref, slope_ref, *rest):
    states, (k32, v32) = rest[: len(sizes)], rest[len(sizes) :]
    widen(k_ref, k32)
    widen(v_ref, v32)
    base = 0
    for state_ref, size in zip(states, sizes):

        def one(i, carry, base=base, state_ref=state_ref):
            h = base + i
            kh = k32[pl.ds(h, t, stride=heads), :]
            feat, slope = silu_parts(kh)
            feat = feat.astype(BF)
            vh = v32[pl.ds(h, t, stride=heads), :].astype(BF)
            fk_ref[h] = feat
            vh_ref[h] = vh
            slope_ref[h] = slope
            state_ref[i] = dot(feat, vh, 0, 0).astype(BF)
            return carry

        lax.fori_loop(0, size, one, 0)
        base += size


def query_kernel(heads, t, q_ref, g_ref, fk_ref, vh_ref, fq_ref, gh_ref, slope_ref, score_ref, raw_ref, q32, g32):
    widen(q_ref, q32)
    widen(g_ref, g32)

    def one(h, carry):
        qh = q32[pl.ds(h, t, stride=heads), :]
        feat, slope = silu_parts(qh)
        feat = feat.astype(BF)
        fq_ref[h] = feat
        slope_ref[h] = slope
        gh_ref[h] = g32[pl.ds(h, t, stride=heads), :].astype(BF)
        scores = jnp.where(low_mask(t), dot(feat, fk_ref[h], 1, 1), 0.0).astype(BF)
        score_ref[h] = scores
        raw_ref[h] = dot(scores, vh_ref[h], 1, 0)
        return carry

    lax.fori_loop(0, heads, one, 0)


def norm_kernel(base, size, parts, fq_ref, gh_ref, raw_ref, *rest):
    got, (normed_ref, grad_raw_ref, earlier_ref, grad_ref) = rest[:parts], rest[parts:]

    def one(i, carry):
        h = base + i
        earlier = got[0][i].astype(F32)
        for part in got[1:]:
            earlier = earlier + part[i].astype(F32)
        earlier = earlier.astype(BF)
        earlier_ref[i] = earlier
        fq = fq_ref[h]
        raw = raw_ref[h] + dot(fq, earlier, 1, 0)
        inverse = lax.rsqrt(jnp.mean(raw * raw, axis=-1, keepdims=True) + 1.0)
        normed = raw * inverse
        up = gh_ref[h].astype(F32)
        grad = inverse * (up - normed * jnp.mean(up * normed, axis=-1, keepdims=True))
        grad = grad.astype(BF)
        normed_ref[i] = normed.astype(BF)
        grad_raw_ref[i] = grad
        grad_ref[i] = dot(fq, grad, 0, 0).astype(BF)
        return carry

    lax.fori_loop(0, size, one, 0)


def back_kernel(base, size, t, fq_ref, fk_ref, vh_ref, slope_ref, score_ref, grad_raw_ref, earlier_ref, gq_ref, gk_ref, gv_ref):
    def one(i, carry):
        h = base + i
        grad = grad_raw_ref[i]
        fq = fq_ref[h]
        grad_scores = jnp.where(low_mask(t), dot(grad, vh_ref[h], 1, 1), 0.0).astype(BF)
        gfq = dot(grad_scores, fk_ref[h], 1, 0) + dot(grad, earlier_ref[i], 1, 1)
        gq_ref[i] = (gfq * slope_ref[h]).astype(BF)
        gk_ref[i] = dot(grad_scores, fq, 0, 0)
        gv_ref[i] = dot(score_ref[h], grad, 0, 0)
        return carry

    lax.fori_loop(0, size, one, 0)


def gather_kernel(heads, t, sizes, count, *refs):
    ins, outs, scratch = refs[: count * len(sizes)], refs[count * len(sizes) : -1], refs[-1]
    for a in range(count):
        base = 0
        for c, size in enumerate(sizes):
            piece = ins[a * len(sizes) + c]

            def one(i, carry, base=base, piece=piece):
                scratch[pl.ds(base + i, t, stride=heads), :] = piece[i].astype(F32)
                return carry

            lax.fori_loop(0, size, one, 0)
            base += size
        outs[a][...] = scratch[...].astype(BF)


def last_kernel(heads, t, sizes, parts, fk_ref, vh_ref, slope_ref, *refs):
    m = len(sizes)
    gks, gvs, refs = refs[:m], refs[m : 2 * m], refs[2 * m :]
    got, (gk_ref, gv_ref, k32, v32) = refs[: parts * m], refs[parts * m :]
    base = 0
    for c, size in enumerate(sizes):
        mine = got[c * parts : (c + 1) * parts]

        def one(i, carry, base=base, mine=mine, gk=gks[c], gv=gvs[c]):
            h = base + i
            later = mine[0][i].astype(F32)
            for part in mine[1:]:
                later = later + part[i].astype(F32)
            later = later.astype(BF)
            gfk = gk[i] + dot(vh_ref[h], later, 1, 1)
            k32[pl.ds(h, t, stride=heads), :] = gfk * slope_ref[h]
            v32[pl.ds(h, t, stride=heads), :] = gv[i] + dot(fk_ref[h], later, 1, 0)
            return carry

        lax.fori_loop(0, size, one, 0)
        base += size
    gk_ref[...] = k32[...].astype(BF)
    gv_ref[...] = v32[...].astype(BF)


def call(body, outs, scratch, args, flops, name):
    moved = sum(a.size * a.dtype.itemsize for a in args)
    return pl.pallas_call(
        body,
        out_shape=outs,
        scratch_shapes=scratch,
        compiler_params=pltpu.CompilerParams(vmem_limit_bytes=40 * MIB),
        cost_estimate=pl.CostEstimate(flops=flops, bytes_accessed=moved, transcendentals=0),
        name=name,
    )(*args)


def chain(part, n, reverse):
    got = []
    running = part
    for hop in range(n - 1):
        pair = (n - 1 - hop, n - 2 - hop) if reverse else (hop, hop + 1)
        received = lax.ppermute(running, "ctx", [pair])
        got.append(received)
        running = (part.astype(F32) + received.astype(F32)).astype(BF)
    return got


def shards(n, query_in, key_in, value_in, grad_out):
    _, t, heads, d = query_in.shape
    m = min(CHUNKS, heads)
    sizes = [heads // m + (1 if c < heads % m else 0) for c in range(m)]
    bases = [sum(sizes[:c]) for c in range(m)]
    q, k, v, g = (a.reshape(t * heads, d) for a in (query_in, key_in, value_in, grad_out))
    S = jax.ShapeDtypeStruct
    whole = lambda dt: S((heads, t, d), dt)
    flat = S((t * heads, d), BF)
    wide = pltpu.VMEM((t * heads, d), F32)
    mm = 2 * t * d * d

    fk, vh, slope_k, *states = call(
        functools.partial(key_kernel, heads, t, sizes),
        [whole(BF), whole(BF), whole(F32)] + [S((s, d, d), BF) for s in sizes],
        [wide, wide], (k, v), heads * mm, "key",
    )
    ups = [chain(s, n, False) for s in states]
    fq, gh, slope_q, scores, raw = call(
        functools.partial(query_kernel, heads, t),
        [whole(BF), whole(BF), whole(F32), S((heads, t, t), BF), whole(F32)],
        [wide, wide], (q, g, fk, vh), heads * mm * 4, "query",
    )
    normed, gqs, gks, gvs, downs = [], [], [], [], []
    for c in range(m):
        s = sizes[c]
        piece = lambda dt: S((s, t, d), dt)
        nb, grad_raw, earlier, grad = call(
            functools.partial(norm_kernel, bases[c], s, n - 1),
            [piece(BF), piece(BF), S((s, d, d), BF), S((s, d, d), BF)],
            [], (fq, gh, raw, *ups[c]), s * mm * 2, "norm",
        )
        normed.append(nb)
        downs.append(chain(grad, n, True))
        gq, gk, gv = call(
            functools.partial(back_kernel, bases[c], s, t),
            [piece(BF), piece(F32), piece(F32)],
            [], (fq, fk, vh, slope_q, scores, grad_raw, earlier), s * mm * 9, "back",
        )
        gqs.append(gq)
        gks.append(gk)
        gvs.append(gv)
    output, grad_query = call(
        functools.partial(gather_kernel, heads, t, sizes, 2),
        [flat, flat], [wide], (*normed, *gqs), heads * mm, "gather",
    )
    grad_key, grad_value = call(
        functools.partial(last_kernel, heads, t, sizes, n - 1),
        [flat, flat], [wide, wide],
        (fk, vh, slope_k, *gks, *gvs, *[r for down in downs for r in down]), heads * mm * 2, "last",
    )
    return tuple(a.reshape(1, t, heads, d) for a in (output, grad_query, grad_key, grad_value))


def solution(mesh):
    placed = P(("groups", "rep"), "ctx", "head", None)
    return jax.shard_map(
        functools.partial(shards, mesh.shape["ctx"]),
        mesh=mesh,
        in_specs=(placed,) * 4,
        out_specs=(placed,) * 4,
        check_vma=False,
    )
```

time: 211 us -> 81.4 us (0.39)
  the two profiles are of different devices: /device:TPU:0 before, /device:TPU:8 now
where the time goes in v1:
time: 81.4 us; the launch traced here: 80.9 us
  Pallas kernels  36.6 us (45%)
  starting transfers between devices  26.1 us (32%)
  waiting for transfers between devices  14.1 us (17%)
  local copies, waits for them, and re-layouts  2.45 us (3%)
  between operations  1.13 us (1%)
    pallas_call x12, Pallas kernels, call(): pl.pallas_call(body, out_shape=outs, scratch_shapes=scratch, compiler_par...  36.6 us
    ppermute x24, starting transfers between devices, chain(): received = lax.ppermute(running, 'ctx', [pair])  26.1 us
    ppermute x24, waiting for transfers between devices, chain(): received = lax.ppermute(running, 'ctx', [pair])  14.1 us
    unnamed x8, local copies, waits for them, and re-layouts  2.45 us
  transfers between devices with their start and end apart: 24, of which 7 were waited for; matrix products, arithmetic and copies ran while one was open for 1% of the time, Pallas kernels for 32%

profile of v1, /device:TPU:8, one launch (start us, length us, event | category | flops | bytes accessed | tf_op | source)
XLA Modules:
  0.0 80.9 jit_solution(6238302963401194620)
XLA Ops:
  3.1 4.6 %key.1 = (bf16[16,256,128]{2,1,0:T(8,128)(2,1)S(1)}, bf16[16,256,128]{2,1,0:T(8,128)(2,1)S(1)}, f32[16,256,128]{2,1,0:T(8,128)S(1)}, bf16[4,128,128]{2,1,0:T(8,1...) custom-call(bf16[4096,128]{1,0:T(8,128)(2,1)S(1)} %bitcast.8, ...), custom_call_target="tpu_custom_call" | custom-call | flops 134217728 | bytes 2097152 | tf_op jit(solution)/shard_map/key/pallas_call | solution.py:159
  7.7 1.3 %collective-permute-start = (bf16[4,128,128]{2,1,0:T(8,128)(2,1)S(1)}, bf16[4,128,128]{2,1,0:T(8,128)(2,1)S(1)}, u32[]{:S(2)}, u32[]{:S(2)}) collective-permute-start(bf16[4,128,128]{2,1,0:T(8,128)(2,1)S(1)} %get-tuple-element.53), channel_id=1, source_target_pairs={{0,4},{1,5},{2,6},{3,7},{16,20},{17,21},{18,22},{19,23}} | collective-permute-start | bytes 393224 | tf_op jit(solution)/shard_map/ppermute | solution.py:174
  9.0 1.3 %collective-permute-start.3 = (bf16[4,128,128]{2,1,0:T(8,128)(2,1)S(1)}, bf16[4,128,128]{2,1,0:T(8,128)(2,1)S(1)}, u32[]{:S(2)}, u32[]{:S(2)}) collective-permute-start(bf16[4,128,128]{2,1,0:T(8,128)(2,1)S(1)} %get-tuple-element.55), channel_id=1, source_target_pairs={{0,4},{1,5},{2,6},{3,7},{16,20},{17,21},{18,22},{19,23}} | collective-permute-start | bytes 393224 | tf_op jit(solution)/shard_map/ppermute | solution.py:174
  10.3 1.3 %collective-permute-start.6 = (bf16[4,128,128]{2,1,0:T(8,128)(2,1)S(1)}, bf16[4,128,128]{2,1,0:T(8,128)(2,1)S(1)}, u32[]{:S(2)}, u32[]{:S(2)}) collective-permute-start(bf16[4,128,128]{2,1,0:T(8,128)(2,1)S(1)} %get-tuple-element.57), channel_id=1, source_target_pairs={{0,4},{1,5},{2,6},{3,7},{16,20},{17,21},{18,22},{19,23}} | collective-permute-start | bytes 393224 | tf_op jit(solution)/shard_map/ppermute | solution.py:174
  11.6 1.3 %collective-permute-start.9 = (bf16[4,128,128]{2,1,0:T(8,128)(2,1)S(1)}, bf16[4,128,128]{2,1,0:T(8,128)(2,1)S(1)}, u32[]{:S(2)}, u32[]{:S(2)}) collective-permute-start(bf16[4,128,128]{2,1,0:T(8,128)(2,1)S(1)} %get-tuple-element.59), channel_id=1, source_target_pairs={{0,4},{1,5},{2,6},{3,7},{16,20},{17,21},{18,22},{19,23}} | collective-permute-start | bytes 393224 | tf_op jit(solution)/shard_map/ppermute | solution.py:174
  12.9 6.7 %query.1 = (bf16[16,256,128]{2,1,0:T(8,128)(2,1)S(1)}, bf16[16,256,128]{2,1,0:T(8,128)(2,1)S(1)}, f32[16,256,128]{2,1,0:T(8,128)S(1)}, bf16[16,256,256]{2,1,0:T(8,128)(2,1)S(1)}, f32[16,256,128]{2,1,0:T(8,128)S(1)}) custom-call(bf16[4096,128]{1,0:T(8,128)(2,1)S(1)} %bitcast.10, bf16[4096,128]{1,0:T(8,128)(2,1)S(1)} %bitcast.11, ...), custom_call_target="tpu_custom_call" | custom-call | flops 536870912 | bytes 4194304 | tf_op jit(solution)/shard_map/query/pallas_call | solution.py:159
  19.7 1.3 %collective-permute-start.1 = (bf16[4,128,128]{2,1,0:T(8,128)(2,1)S(1)}, bf16[4,128,128]{2,1,0:T(8,128)(2,1)S(1)}, u32[]{:S(2)}, u32[]{:S(2)}) collective-permute-start(bf16[4,128,128]{2,1,0:T(8,128)(2,1)S(1)} %fusion), channel_id=1, source_target_pairs={{4,8},{5,9},{6,10},{7,11},{20,24},{21,25},{22,26},{23,27}} | collective-permute-start | bytes 393224 | tf_op jit(solution)/shard_map/ppermute | solution.py:174
  21.1 1.3 %collective-permute-start.4 = (bf16[4,128,128]{2,1,0:T(8,128)(2,1)S(1)}, bf16[4,128,128]{2,1,0:T(8,128)(2,1)S(1)}, u32[]{:S(2)}, u32[]{:S(2)}) collective-permute-start(bf16[4,128,128]{2,1,0:T(8,128)(2,1)S(1)} %fusion.2), channel_id=1, source_target_pairs={{4,8},{5,9},{6,10},{7,11},{20,24},{21,25},{22,26},{23,27}} | collective-permute-start | bytes 393224 | tf_op jit(solution)/shard_map/ppermute | solution.py:174
  22.4 1.3 %collective-permute-start.7 = (bf16[4,128,128]{2,1,0:T(8,128)(2,1)S(1)}, bf16[4,128,128]{2,1,0:T(8,128)(2,1)S(1)}, u32[]{:S(2)}, u32[]{:S(2)}) collective-permute-start(bf16[4,128,128]{2,1,0:T(8,128)(2,1)S(1)} %fusion.4), channel_id=1, source_target_pairs={{4,8},{5,9},{6,10},{7,11},{20,24},{21,25},{22,26},{23,27}} | collective-permute-start | bytes 393224 | tf_op jit(solution)/shard_map/ppermute | solution.py:174
  23.8 1.3 %collective-permute-start.10 = (bf16[4,128,128]{2,1,0:T(8,128)(2,1)S(1)}, bf16[4,128,128]{2,1,0:T(8,128)(2,1)S(1)}, u32[]{:S(2)}, u32[]{:S(2)}) collective-permute-start(bf16[4,128,128]{2,1,0:T(8,128)(2,1)S(1)} %fusion.6), channel_id=1, source_target_pairs={{4,8},{5,9},{6,10},{7,11},{20,24},{21,25},{22,26},{23,27}} | collective-permute-start | bytes 393224 | tf_op jit(solution)/shard_map/ppermute | solution.py:174
  25.8 1.8 %collective-permute-done.4.rest_1_ = bf16[4,128,128]{2,1,0:T(8,128)(2,1)S(1)} collective-permute-done((bf16[4,128,128]{2,1,0:T(8,128)(2,1)S(1)}, bf16[4,128,128]{2,1,0:T(8,128)(2,1)S(1)}, u32[]{:S(2)}, u32[]{:S(2)}) %collective-permute-start.4) | collective-permute-done | bytes 131104 | tf_op jit(solution)/shard_map/ppermute | solution.py:174
  28.4 2.1 %collective-permute-done.7.rest_1_ = bf16[4,128,128]{2,1,0:T(8,128)(2,1)S(1)} collective-permute-done((bf16[4,128,128]{2,1,0:T(8,128)(2,1)S(1)}, bf16[4,128,128]{2,1,0:T(8,128)(2,1)S(1)}, u32[]{:S(2)}, u32[]{:S(2)}) %collective-permute-start.7) | collective-permute-done | bytes 131104 | tf_op jit(solution)/shard_map/ppermute | solution.py:174
  33.2 2.1 %norm.4 = (bf16[4,256,128]{2,1,0:T(8,128)(2,1)S(1)}, bf16[4,256,128]{2,1,0:T(8,128)(2,1)S(1)}, bf16[4,128,128]{2,1,0:T(8,128)(2,1)S(1)}, bf16[4,128,128]{2,1,0:T(8,128)(2,1)S(1)}) custom-call(bf16[16,256,128]{2,1,0:T(8,128)(2,1)S(1)} %get-tuple-element.50.fq_ref, bf16[16,256,128]{2,1,0:T(8,128)(2,1)S(1)} %get-tuple-element.51.gh_ref, ...), custom_call_target="tpu_custom_call" | custom-call | flops 67108864 | bytes 4587520 | tf_op jit(solution)/shard_map/norm/pallas_call | solution.py:159
  35.9 2.1 %norm.5 = (bf16[4,256,128]{2,1,0:T(8,128)(2,1)S(1)}, bf16[4,256,128]{2,1,0:T(8,128)(2,1)S(1)}, bf16[4,128,128]{2,1,0:T(8,128)(2,1)S(1)}, bf16[4,128,128]{2,1,0:T(8,128)(2,1)S(1)}) custom-call(bf16[16,256,128]{2,1,0:T(8,128)(2,1)S(1)} %get-tuple-element.50.fq_ref, bf16[16,256,128]{2,1,0:T(8,128)(2,1)S(1)} %get-tuple-element.51.gh_ref, ...), custom_call_target="tpu_custom_call" | custom-call | flops 67108864 | bytes 4587520 | tf_op jit(solution)/shard_map/norm/pallas_call | solution.py:159
  38.7 2.1 %norm.6 = (bf16[4,256,128]{2,1,0:T(8,128)(2,1)S(1)}, bf16[4,256,128]{2,1,0:T(8,128)(2,1)S(1)}, bf16[4,128,128]{2,1,0:T(8,128)(2,1)S(1)}, bf16[4,128,128]{2,1,0:T(8,128)(2,1)S(1)}) custom-call(bf16[16,256,128]{2,1,0:T(8,128)(2,1)S(1)} %get-tuple-element.50.fq_ref, bf16[16,256,128]{2,1,0:T(8,128)(2,1)S(1)} %get-tuple-element.51.gh_ref, ...), custom_call_target="tpu_custom_call" | custom-call | flops 67108864 | bytes 4587520 | tf_op jit(solution)/shard_map/norm/pallas_call | solution.py:159
  41.4 2.1 %norm.7 = (bf16[4,256,128]{2,1,0:T(8,128)(2,1)S(1)}, bf16[4,256,128]{2,1,0:T(8,128)(2,1)S(1)}, bf16[4,128,128]{2,1,0:T(8,128)(2,1)S(1)}, bf16[4,128,128]{2,1,0:T(8,128)(2,1)S(1)}) custom-call(bf16[16,256,128]{2,1,0:T(8,128)(2,1)S(1)} %get-tuple-element.50.fq_ref, bf16[16,256,128]{2,1,0:T(8,128)(2,1)S(1)} %get-tuple-element.51.gh_ref, ...), custom_call_target="tpu_custom_call" | custom-call | flops 67108864 | bytes 4587520 | tf_op jit(solution)/shard_map/norm/pallas_call | solution.py:159
  44.2 1.3 %collective-permute-start.13 = (bf16[4,128,128]{2,1,0:T(8,128)(2,1)S(1)}, bf16[4,128,128]{2,1,0:T(8,128)(2,1)S(1)}, u32[]{:S(2)}, u32[]{:S(2)}) collective-permute-start(bf16[4,128,128]{2,1,0:T(8,128)(2,1)S(1)} %fusion.8), channel_id=1, source_target_pairs={{8,4},{9,5},{10,6},{11,7},{24,20},{25,21},{26,22},{27,23}} | collective-permute-start | bytes 393224 | tf_op jit(solution)/shard_map/ppermute | solution.py:174
  45.6 1.3 %collective-permute-start.16 = (bf16[4,128,128]{2,1,0:T(8,128)(2,1)S(1)}, bf16[4,128,128]{2,1,0:T(8,128)(2,1)S(1)}, u32[]{:S(2)}, u32[]{:S(2)}) collective-permute-start(bf16[4,128,128]{2,1,0:T(8,128)(2,1)S(1)} %fusion.10), channel_id=1, source_target_pairs={{8,4},{9,5},{10,6},{11,7},{24,20},{25,21},{26,22},{27,23}} | collective-permute-start | bytes 393224 | tf_op jit(solution)/shard_map/ppermute | solution.py:174
  48.3 1.3 %collective-permute-start.22 = (bf16[4,128,128]{2,1,0:T(8,128)(2,1)S(1)}, bf16[4,128,128]{2,1,0:T(8,128)(2,1)S(1)}, u32[]{:S(2)}, u32[]{:S(2)}) collective-permute-start(bf16[4,128,128]{2,1,0:T(8,128)(2,1)S(1)} %fusion.14), channel_id=1, source_target_pairs={{8,4},{9,5},{10,6},{11,7},{24,20},{25,21},{26,22},{27,23}} | collective-permute-start | bytes 393224 | tf_op jit(solution)/shard_map/ppermute | solution.py:174
  49.6 5.9 %collective-permute-done.13.refs_9_ = bf16[4,128,128]{2,1,0:T(8,128)(2,1)S(1)} collective-permute-done((bf16[4,128,128]{2,1,0:T(8,128)(2,1)S(1)}, bf16[4,128,128]{2,1,0:T(8,128)(2,1)S(1)}, u32[]{:S(2)}, u32[]{:S(2)}) %collective-permute-start.13) | collective-permute-done | bytes 131104 | tf_op jit(solution)/shard_map/ppermute | solution.py:174
  55.6 1.3 %collective-permute-start.14 = (bf16[4,128,128]{2,1,0:T(8,128)(2,1)S(1)}, bf16[4,128,128]{2,1,0:T(8,128)(2,1)S(1)}, u32[]{:S(2)}, u32[]{:S(2)}) collective-permute-start(bf16[4,128,128]{2,1,0:T(8,128)(2,1)S(1)} %fusion.9), channel_id=1, source_target_pairs={{4,0},{5,1},{6,2},{7,3},{20,16},{21,17},{22,18},{23,19}} | collective-permute-start | bytes 393224 | tf_op jit(solution)/shard_map/ppermute | solution.py:174
  56.9 1.5 %collective-permute-done.16.refs_12_ = bf16[4,128,128]{2,1,0:T(8,128)(2,1)S(1)} collective-permute-done((bf16[4,128,128]{2,1,0:T(8,128)(2,1)S(1)}, bf16[4,128,128]{2,1,0:T(8,128)(2,1)S(1)}, u32[]{:S(2)}, u32[]{:S(2)}) %collective-permute-start.16) | collective-permute-done | bytes 131104 | tf_op jit(solution)/shard_map/ppermute | solution.py:174
  58.4 1.3 %collective-permute-start.17 = (bf16[4,128,128]{2,1,0:T(8,128)(2,1)S(1)}, bf16[4,128,128]{2,1,0:T(8,128)(2,1)S(1)}, u32[]{:S(2)}, u32[]{:S(2)}) collective-permute-start(bf16[4,128,128]{2,1,0:T(8,128)(2,1)S(1)} %fusion.11), channel_id=1, source_target_pairs={{4,0},{5,1},{6,2},{7,3},{20,16},{21,17},{22,18},{23,19}} | collective-permute-start | bytes 393224 | tf_op jit(solution)/shard_map/ppermute | solution.py:174
  59.7 1.4 %collective-permute-done.19.refs_15_ = bf16[4,128,128]{2,1,0:T(8,128)(2,1)S(1)} collective-permute-done((bf16[4,128,128]{2,1,0:T(8,128)(2,1)S(1)}, bf16[4,128,128]{2,1,0:T(8,128)(2,1)S(1)}, u32[]{:S(2)}, u32[]{:S(2)}) %collective-permute-start.19) | collective-permute-done | bytes 131104 | tf_op jit(solution)/shard_map/ppermute | solution.py:174
  61.1 1.3 %collective-permute-start.20 = (bf16[4,128,128]{2,1,0:T(8,128)(2,1)S(1)}, bf16[4,128,128]{2,1,0:T(8,128)(2,1)S(1)}, u32[]{:S(2)}, u32[]{:S(2)}) collective-permute-start(bf16[4,128,128]{2,1,0:T(8,128)(2,1)S(1)} %fusion.13), channel_id=1, source_target_pairs={{4,0},{5,1},{6,2},{7,3},{20,16},{21,17},{22,18},{23,19}} | collective-permute-start | bytes 393224 | tf_op jit(solution)/shard_map/ppermute | solution.py:174
  62.5 1.3 %collective-permute-start.23 = (bf16[4,128,128]{2,1,0:T(8,128)(2,1)S(1)}, bf16[4,128,128]{2,1,0:T(8,128)(2,1)S(1)}, u32[]{:S(2)}, u32[]{:S(2)}) collective-permute-start(bf16[4,128,128]{2,1,0:T(8,128)(2,1)S(1)} %fusion.15), channel_id=1, source_target_pairs={{4,0},{5,1},{6,2},{7,3},{20,16},{21,17},{22,18},{23,19}} | collective-permute-start | bytes 393224 | tf_op jit(solution)/shard_map/ppermute | solution.py:174
  63.8 1.9 %back.4 = (bf16[4,256,128]{2,1,0:T(8,128)(2,1)S(1)}, f32[4,256,128]{2,1,0:T(8,128)S(1)}, f32[4,256,128]{2,1,0:T(8,128)S(1)}) custom-call(bf16[16,256,128]{2,1,0:T(8,128)(2,1)S(1)} %get-tuple-element.50.fq_ref, bf16[16,256,128]{2,1,0:T(8,128)(2,1)S(1)} %get-tuple-element.48.fk_ref, bf16[16,256,128]{2,1,0:T(8,128)(2,1)S(1)} %get-tuple-element.49.vh_ref, ...), custom_call_target="tpu_custom_call" | custom-call | flops 301989888 | bytes 7733248 | tf_op jit(solution)/shard_map/back/pallas_call | solution.py:159
  65.7 1.9 %back.5 = (bf16[4,256,128]{2,1,0:T(8,128)(2,1)S(1)}, f32[4,256,128]{2,1,0:T(8,128)S(1)}, f32[4,256,128]{2,1,0:T(8,128)S(1)}) custom-call(bf16[16,256,128]{2,1,0:T(8,128)(2,1)S(1)} %get-tuple-element.50.fq_ref, bf16[16,256,128]{2,1,0:T(8,128)(2,1)S(1)} %get-tuple-element.48.fk_ref, bf16[16,256,128]{2,1,0:T(8,128)(2,1)S(1)} %get-tuple-element.49.vh_ref, ...), custom_call_target="tpu_custom_call" | custom-call | flops 301989888 | bytes 7733248 | tf_op jit(solution)/shard_map/back/pallas_call | solution.py:159
  67.6 1.9 %back.6 = (bf16[4,256,128]{2,1,0:T(8,128)(2,1)S(1)}, f32[4,256,128]{2,1,0:T(8,128)S(1)}, f32[4,256,128]{2,1,0:T(8,128)S(1)}) custom-call(bf16[16,256,128]{2,1,0:T(8,128)(2,1)S(1)} %get-tuple-element.50.fq_ref, bf16[16,256,128]{2,1,0:T(8,128)(2,1)S(1)} %get-tuple-element.48.fk_ref, bf16[16,256,128]{2,1,0:T(8,128)(2,1)S(1)} %get-tuple-element.49.vh_ref, ...), custom_call_target="tpu_custom_call" | custom-call | flops 301989888 | bytes 7733248 | tf_op jit(solution)/shard_map/back/pallas_call | solution.py:159
  69.5 1.9 %back.7 = (bf16[4,256,128]{2,1,0:T(8,128)(2,1)S(1)}, f32[4,256,128]{2,1,0:T(8,128)S(1)}, f32[4,256,128]{2,1,0:T(8,128)S(1)}) custom-call(bf16[16,256,128]{2,1,0:T(8,128)(2,1)S(1)} %get-tuple-element.50.fq_ref, bf16[16,256,128]{2,1,0:T(8,128)(2,1)S(1)} %get-tuple-element.48.fk_ref, bf16[16,256,128]{2,1,0:T(8,128)(2,1)S(1)} %get-tuple-element.49.vh_ref, ...), custom_call_target="tpu_custom_call" | custom-call | flops 301989888 | bytes 7733248 | tf_op jit(solution)/shard_map/back/pallas_call | solution.py:159
  71.3 3.6 %gather.1 = (bf16[4096,128]{1,0:T(8,128)(2,1)}, bf16[4096,128]{1,0:T(8,128)(2,1)}) custom-call(bf16[4,256,128]{2,1,0:T(8,128)(2,1)S(1)} %get-tuple-element.54.refs_0_, bf16[4,256,128]{2,1,0:T(8,128)(2,1)S(1)} %get-tuple-element.56.refs_1_, bf16[4,256,128]{2,1,0:T(8,128)(2,1)S(1)} %get-tuple-element.58.refs_2_, ...), custom_call_target="tpu_custom_call" | custom-call | flops 134217728 | bytes 2097152 | tf_op jit(solution)/shard_map/gather/pallas_call | solution.py:159
  75.0 5.9 %last.1 = (bf16[4096,128]{1,0:T(8,128)(2,1)}, bf16[4096,128]{1,0:T(8,128)(2,1)}) custom-call(bf16[16,256,128]{2,1,0:T(8,128)(2,1)S(1)} %get-tuple-element.48.fk_ref, bf16[16,256,128]{2,1,0:T(8,128)(2,1)S(1)} %get-tuple-element.49.vh_ref, f32[16,256,128]{2,1,0:T(8,128)S(1)} %get-tuple-element.77.slope_ref, f32[4,256,128]{2,1,0:T(8,128)S(1)} %get-tuple-element.78.refs_0_, ...), custom_call_target="tpu_custom_call" | custom-call | flops 268435456 | bytes 9961472 | tf_op jit(solution)/shard_map/last/pallas_call | solution.py:159
  (52 shorter events, 11.1 us)
Async XLA Ops:
  0.6 1.2 %copy-start = (bf16[1,256,16,128]{3,2,1,0:T(8,128)(2,1)S(1)}, bf16[1,256,16,128]{3,2,1,0:T(8,128)(2,1)}, u32[]{:S(2)}) copy-start(bf16[1,256,16,128]{3,2,1,0:T(8,128)(2,1)} %param.5) | copy-start | bytes 3145732
  1.9 1.2 %copy-start.1 = (bf16[1,256,16,128]{3,2,1,0:T(8,128)(2,1)S(1)}, bf16[1,256,16,128]{3,2,1,0:T(8,128)(2,1)}, u32[]{:S(2)}) copy-start(bf16[1,256,16,128]{3,2,1,0:T(8,128)(2,1)} %param.6) | copy-start | bytes 3145732
  3.1 9.8 %copy-start.2 = (bf16[1,256,16,128]{3,2,1,0:T(8,128)(2,1)S(1)}, bf16[1,256,16,128]{3,2,1,0:T(8,128)(2,1)}, u32[]{:S(2)}) copy-start(bf16[1,256,16,128]{3,2,1,0:T(8,128)(2,1)} %param.4) | copy-start | bytes 3145732
  3.1 9.8 %copy-start.3 = (bf16[1,256,16,128]{3,2,1,0:T(8,128)(2,1)S(1)}, bf16[1,256,16,128]{3,2,1,0:T(8,128)(2,1)}, u32[]{:S(2)}) copy-start(bf16[1,256,16,128]{3,2,1,0:T(8,128)(2,1)} %param.7) | copy-start | bytes 3145732
  7.7 12.0 %collective-permute-start = (bf16[4,128,128]{2,1,0:T(8,128)(2,1)S(1)}, bf16[4,128,128]{2,1,0:T(8,128)(2,1)S(1)}, u32[]{:S(2)}, u32[]{:S(2)}) collective-permute-start(bf16[4,128,128]{2,1,0:T(8,128)(2,1)S(1)} %get-tuple-element.53), channel_id=1, source_target_pairs={{0,4},{1,5},{2,6},{3,7},{16,20},{17,21},{18,22},{19,23}} | collective-permute-start | bytes 393224 | tf_op jit(solution)/shard_map/ppermute | solution.py:174
  9.0 12.0 %collective-permute-start.3 = (bf16[4,128,128]{2,1,0:T(8,128)(2,1)S(1)}, bf16[4,128,128]{2,1,0:T(8,128)(2,1)S(1)}, u32[]{:S(2)}, u32[]{:S(2)}) collective-permute-start(bf16[4,128,128]{2,1,0:T(8,128)(2,1)S(1)} %get-tuple-element.55), channel_id=1, source_target_pairs={{0,4},{1,5},{2,6},{3,7},{16,20},{17,21},{18,22},{19,23}} | collective-permute-start | bytes 393224 | tf_op jit(solution)/shard_map/ppermute | solution.py:174
  10.3 12.1 %collective-permute-start.6 = (bf16[4,128,128]{2,1,0:T(8,128)(2,1)S(1)}, bf16[4,128,128]{2,1,0:T(8,128)(2,1)S(1)}, u32[]{:S(2)}, u32[]{:S(2)}) collective-permute-start(bf16[4,128,128]{2,1,0:T(8,128)(2,1)S(1)} %get-tuple-element.57), channel_id=1, source_target_pairs={{0,4},{1,5},{2,6},{3,7},{16,20},{17,21},{18,22},{19,23}} | collective-permute-start | bytes 393224 | tf_op jit(solution)/shard_map/ppermute | solution.py:174
  11.6 12.2 %collective-permute-start.9 = (bf16[4,128,128]{2,1,0:T(8,128)(2,1)S(1)}, bf16[4,128,128]{2,1,0:T(8,128)(2,1)S(1)}, u32[]{:S(2)}, u32[]{:S(2)}) collective-permute-start(bf16[4,128,128]{2,1,0:T(8,128)(2,1)S(1)} %get-tuple-element.59), channel_id=1, source_target_pairs={{0,4},{1,5},{2,6},{3,7},{16,20},{17,21},{18,22},{19,23}} | collective-permute-start | bytes 393224 | tf_op jit(solution)/shard_map/ppermute | solution.py:174
  19.7 5.4 %collective-permute-start.1 = (bf16[4,128,128]{2,1,0:T(8,128)(2,1)S(1)}, bf16[4,128,128]{2,1,0:T(8,128)(2,1)S(1)}, u32[]{:S(2)}, u32[]{:S(2)}) collective-permute-start(bf16[4,128,128]{2,1,0:T(8,128)(2,1)S(1)} %fusion), channel_id=1, source_target_pairs={{4,8},{5,9},{6,10},{7,11},{20,24},{21,25},{22,26},{23,27}} | collective-permute-start | bytes 393224 | tf_op jit(solution)/shard_map/ppermute | solution.py:174
  21.1 6.6 %collective-permute-start.4 = (bf16[4,128,128]{2,1,0:T(8,128)(2,1)S(1)}, bf16[4,128,128]{2,1,0:T(8,128)(2,1)S(1)}, u32[]{:S(2)}, u32[]{:S(2)}) collective-permute-start(bf16[4,128,128]{2,1,0:T(8,128)(2,1)S(1)} %fusion.2), channel_id=1, source_target_pairs={{4,8},{5,9},{6,10},{7,11},{20,24},{21,25},{22,26},{23,27}} | collective-permute-start | bytes 393224 | tf_op jit(solution)/shard_map/ppermute | solution.py:174
  22.4 8.0 %collective-permute-start.7 = (bf16[4,128,128]{2,1,0:T(8,128)(2,1)S(1)}, bf16[4,128,128]{2,1,0:T(8,128)(2,1)S(1)}, u32[]{:S(2)}, u32[]{:S(2)}) collective-permute-start(bf16[4,128,128]{2,1,0:T(8,128)(2,1)S(1)} %fusion.4), channel_id=1, source_target_pairs={{4,8},{5,9},{6,10},{7,11},{20,24},{21,25},{22,26},{23,27}} | collective-permute-start | bytes 393224 | tf_op jit(solution)/shard_map/ppermute | solution.py:174
  23.8 8.7 %collective-permute-start.10 = (bf16[4,128,128]{2,1,0:T(8,128)(2,1)S(1)}, bf16[4,128,128]{2,1,0:T(8,128)(2,1)S(1)}, u32[]{:S(2)}, u32[]{:S(2)}) collective-permute-start(bf16[4,128,128]{2,1,0:T(8,128)(2,1)S(1)} %fusion.6), channel_id=1, source_target_pairs={{4,8},{5,9},{6,10},{7,11},{20,24},{21,25},{22,26},{23,27}} | collective-permute-start | bytes 393224 | tf_op jit(solution)/shard_map/ppermute | solution.py:174
  25.2 8.0 %collective-permute-start.2 = (bf16[4,128,128]{2,1,0:T(8,128)(2,1)S(1)}, bf16[4,128,128]{2,1,0:T(8,128)(2,1)S(1)}, u32[]{:S(2)}, u32[]{:S(2)}) collective-permute-start(bf16[4,128,128]{2,1,0:T(8,128)(2,1)S(1)} %fusion.1), channel_id=1, source_target_pairs={{8,12},{9,13},{10,14},{11,15},{24,28},{25,29},{26,30},{27,31}} | collective-permute-start | bytes 393224 | tf_op jit(solution)/shard_map/ppermute | solution.py:174
  27.7 8.2 %collective-permute-start.5 = (bf16[4,128,128]{2,1,0:T(8,128)(2,1)S(1)}, bf16[4,128,128]{2,1,0:T(8,128)(2,1)S(1)}, u32[]{:S(2)}, u32[]{:S(2)}) collective-permute-start(bf16[4,128,128]{2,1,0:T(8,128)(2,1)S(1)} %fusion.3), channel_id=1, source_target_pairs={{8,12},{9,13},{10,14},{11,15},{24,28},{25,29},{26,30},{27,31}} | collective-permute-start | bytes 393224 | tf_op jit(solution)/shard_map/ppermute | solution.py:174
  30.5 8.2 %collective-permute-start.8 = (bf16[4,128,128]{2,1,0:T(8,128)(2,1)S(1)}, bf16[4,128,128]{2,1,0:T(8,128)(2,1)S(1)}, u32[]{:S(2)}, u32[]{:S(2)}) collective-permute-start(bf16[4,128,128]{2,1,0:T(8,128)(2,1)S(1)} %fusion.5), channel_id=1, source_target_pairs={{8,12},{9,13},{10,14},{11,15},{24,28},{25,29},{26,30},{27,31}} | collective-permute-start | bytes 393224 | tf_op jit(solution)/shard_map/ppermute | solution.py:174
  32.5 8.9 %collective-permute-start.11 = (bf16[4,128,128]{2,1,0:T(8,128)(2,1)S(1)}, bf16[4,128,128]{2,1,0:T(8,128)(2,1)S(1)}, u32[]{:S(2)}, u32[]{:S(2)}) collective-permute-start(bf16[4,128,128]{2,1,0:T(8,128)(2,1)S(1)} %fusion.7), channel_id=1, source_target_pairs={{8,12},{9,13},{10,14},{11,15},{24,28},{25,29},{26,30},{27,31}} | collective-permute-start | bytes 393224 | tf_op jit(solution)/shard_map/ppermute | solution.py:174
  35.3 8.9 %collective-permute-start.12 = (bf16[4,128,128]{2,1,0:T(8,128)(2,1)S(1)}, bf16[4,128,128]{2,1,0:T(8,128)(2,1)S(1)}, u32[]{:S(2)}, u32[]{:S(2)}) collective-permute-start(bf16[4,128,128]{2,1,0:T(8,128)(2,1)S(1)} %get-tuple-element.86), channel_id=1, source_target_pairs={{12,8},{13,9},{14,10},{15,11},{28,24},{29,25},{30,26},{31,27}} | collective-permute-start | bytes 393224 | tf_op jit(solution)/shard_map/ppermute | solution.py:174
  38.0 7.5 %collective-permute-start.15 = (bf16[4,128,128]{2,1,0:T(8,128)(2,1)S(1)}, bf16[4,128,128]{2,1,0:T(8,128)(2,1)S(1)}, u32[]{:S(2)}, u32[]{:S(2)}) collective-permute-start(bf16[4,128,128]{2,1,0:T(8,128)(2,1)S(1)} %get-tuple-element.87), channel_id=1, source_target_pairs={{12,8},{13,9},{14,10},{15,11},{28,24},{29,25},{30,26},{31,27}} | collective-permute-start | bytes 393224 | tf_op jit(solution)/shard_map/ppermute | solution.py:174
  40.8 6.1 %collective-permute-start.18 = (bf16[4,128,128]{2,1,0:T(8,128)(2,1)S(1)}, bf16[4,128,128]{2,1,0:T(8,128)(2,1)S(1)}, u32[]{:S(2)}, u32[]{:S(2)}) collective-permute-start(bf16[4,128,128]{2,1,0:T(8,128)(2,1)S(1)} %get-tuple-element.88), channel_id=1, source_target_pairs={{12,8},{13,9},{14,10},{15,11},{28,24},{29,25},{30,26},{31,27}} | collective-permute-start | bytes 393224 | tf_op jit(solution)/shard_map/ppermute | solution.py:174
  43.5 4.8 %collective-permute-start.21 = (bf16[4,128,128]{2,1,0:T(8,128)(2,1)S(1)}, bf16[4,128,128]{2,1,0:T(8,128)(2,1)S(1)}, u32[]{:S(2)}, u32[]{:S(2)}) collective-permute-start(bf16[4,128,128]{2,1,0:T(8,128)(2,1)S(1)} %get-tuple-element.89), channel_id=1, source_target_pairs={{12,8},{13,9},{14,10},{15,11},{28,24},{29,25},{30,26},{31,27}} | collective-permute-start | bytes 393224 | tf_op jit(solution)/shard_map/ppermute | solution.py:174
  44.2 11.3 %collective-permute-start.13 = (bf16[4,128,128]{2,1,0:T(8,128)(2,1)S(1)}, bf16[4,128,128]{2,1,0:T(8,128)(2,1)S(1)}, u32[]{:S(2)}, u32[]{:S(2)}) collective-permute-start(bf16[4,128,128]{2,1,0:T(8,128)(2,1)S(1)} %fusion.8), channel_id=1, source_target_pairs={{8,4},{9,5},{10,6},{11,7},{24,20},{25,21},{26,22},{27,23}} | collective-permute-start | bytes 393224 | tf_op jit(solution)/shard_map/ppermute | solution.py:174
  45.6 12.7 %collective-permute-start.16 = (bf16[4,128,128]{2,1,0:T(8,128)(2,1)S(1)}, bf16[4,128,128]{2,1,0:T(8,128)(2,1)S(1)}, u32[]{:S(2)}, u32[]{:S(2)}) collective-permute-start(bf16[4,128,128]{2,1,0:T(8,128)(2,1)S(1)} %fusion.10), channel_id=1, source_target_pairs={{8,4},{9,5},{10,6},{11,7},{24,20},{25,21},{26,22},{27,23}} | collective-permute-start | bytes 393224 | tf_op jit(solution)/shard_map/ppermute | solution.py:174
  46.9 14.1 %collective-permute-start.19 = (bf16[4,128,128]{2,1,0:T(8,128)(2,1)S(1)}, bf16[4,128,128]{2,1,0:T(8,128)(2,1)S(1)}, u32[]{:S(2)}, u32[]{:S(2)}) collective-permute-start(bf16[4,128,128]{2,1,0:T(8,128)(2,1)S(1)} %fusion.12), channel_id=1, source_target_pairs={{8,4},{9,5},{10,6},{11,7},{24,20},{25,21},{26,22},{27,23}} | collective-permute-start | bytes 393224 | tf_op jit(solution)/shard_map/ppermute | solution.py:174
  48.3 14.2 %collective-permute-start.22 = (bf16[4,128,128]{2,1,0:T(8,128)(2,1)S(1)}, bf16[4,128,128]{2,1,0:T(8,128)(2,1)S(1)}, u32[]{:S(2)}, u32[]{:S(2)}) collective-permute-start(bf16[4,128,128]{2,1,0:T(8,128)(2,1)S(1)} %fusion.14), channel_id=1, source_target_pairs={{8,4},{9,5},{10,6},{11,7},{24,20},{25,21},{26,22},{27,23}} | collective-permute-start | bytes 393224 | tf_op jit(solution)/shard_map/ppermute | solution.py:174
  55.6 19.4 %collective-permute-start.14 = (bf16[4,128,128]{2,1,0:T(8,128)(2,1)S(1)}, bf16[4,128,128]{2,1,0:T(8,128)(2,1)S(1)}, u32[]{:S(2)}, u32[]{:S(2)}) collective-permute-start(bf16[4,128,128]{2,1,0:T(8,128)(2,1)S(1)} %fusion.9), channel_id=1, source_target_pairs={{4,0},{5,1},{6,2},{7,3},{20,16},{21,17},{22,18},{23,19}} | collective-permute-start | bytes 393224 | tf_op jit(solution)/shard_map/ppermute | solution.py:174
  58.4 16.6 %collective-permute-start.17 = (bf16[4,128,128]{2,1,0:T(8,128)(2,1)S(1)}, bf16[4,128,128]{2,1,0:T(8,128)(2,1)S(1)}, u32[]{:S(2)}, u32[]{:S(2)}) collective-permute-start(bf16[4,128,128]{2,1,0:T(8,128)(2,1)S(1)} %fusion.11), channel_id=1, source_target_pairs={{4,0},{5,1},{6,2},{7,3},{20,16},{21,17},{22,18},{23,19}} | collective-permute-start | bytes 393224 | tf_op jit(solution)/shard_map/ppermute | solution.py:174
  61.1 13.9 %collective-permute-start.20 = (bf16[4,128,128]{2,1,0:T(8,128)(2,1)S(1)}, bf16[4,128,128]{2,1,0:T(8,128)(2,1)S(1)}, u32[]{:S(2)}, u32[]{:S(2)}) collective-permute-start(bf16[4,128,128]{2,1,0:T(8,128)(2,1)S(1)} %fusion.13), channel_id=1, source_target_pairs={{4,0},{5,1},{6,2},{7,3},{20,16},{21,17},{22,18},{23,19}} | collective-permute-start | bytes 393224 | tf_op jit(solution)/shard_map/ppermute | solution.py:174
  62.5 12.5 %collective-permute-start.23 = (bf16[4,128,128]{2,1,0:T(8,128)(2,1)S(1)}, bf16[4,128,128]{2,1,0:T(8,128)(2,1)S(1)}, u32[]{:S(2)}, u32[]{:S(2)}) collective-permute-start(bf16[4,128,128]{2,1,0:T(8,128)(2,1)S(1)} %fusion.15), channel_id=1, source_target_pairs={{4,0},{5,1},{6,2},{7,3},{20,16},{21,17},{22,18},{23,19}} | collective-permute-start | bytes 393224 | tf_op jit(solution)/shard_map/ppermute | solution.py:174

commit v2 on v1

--- a/solution.py
+++ b/solution.py
@@ -10,6 +10,7 @@
 BF, F32 = jnp.bfloat16, jnp.float32
 MIB = 1 << 20
 CHUNKS = 4
+UNROLL = 4
 
 
 def dot(a, b, ca, cb):
@@ -50,7 +51,7 @@
             state_ref[i] = dot(feat, vh, 0, 0).astype(BF)
             return carry
 
-        lax.fori_loop(0, size, one, 0)
+        lax.fori_loop(0, size, one, 0, unroll=UNROLL)
         base += size
 
 
@@ -70,7 +71,7 @@
         raw_ref[h] = dot(scores, vh_ref[h], 1, 0)
         return carry
 
-    lax.fori_loop(0, heads, one, 0)
+    lax.fori_loop(0, heads, one, 0, unroll=UNROLL)
 
 
 def norm_kernel(base, size, parts, fq_ref, gh_ref, raw_ref, *rest):
@@ -78,10 +79,7 @@
 
     def one(i, carry):
         h = base + i
-        earlier = got[0][i].astype(F32)
-        for part in got[1:]:
-            earlier = earlier + part[i].astype(F32)
-        earlier = earlier.astype(BF)
+        earlier = pick(lax.axis_index("ctx"), got, i)
         earlier_ref[i] = earlier
         fq = fq_ref[h]
         raw = raw_ref[h] + dot(fq, earlier, 1, 0)
@@ -95,7 +93,7 @@
         grad_ref[i] = dot(fq, grad, 0, 0).astype(BF)
         return carry
 
-    lax.fori_loop(0, size, one, 0)
+    lax.fori_loop(0, size, one, 0, unroll=UNROLL)
 
 
 def back_kernel(base, size, t, fq_ref, fk_ref, vh_ref, slope_ref, score_ref, grad_raw_ref, earlier_ref, gq_ref, gk_ref, gv_ref):
@@ -110,7 +108,7 @@
         gv_ref[i] = dot(score_ref[h], grad, 0, 0)
         return carry
 
-    lax.fori_loop(0, size, one, 0)
+    lax.fori_loop(0, size, one, 0, unroll=UNROLL)
 
 
 def gather_kernel(heads, t, sizes, count, *refs):
@@ -124,7 +122,7 @@
                 scratch[pl.ds(base + i, t, stride=heads), :] = piece[i].astype(F32)
                 return carry
 
-            lax.fori_loop(0, size, one, 0)
+            lax.fori_loop(0, size, one, 0, unroll=UNROLL)
             base += size
         outs[a][...] = scratch[...].astype(BF)
 
@@ -139,16 +137,13 @@
 
         def one(i, carry, base=base, mine=mine, gk=gks[c], gv=gvs[c]):
             h = base + i
-            later = mine[0][i].astype(F32)
-            for part in mine[1:]:
-                later = later + part[i].astype(F32)
-            later = later.astype(BF)
+            later = pick(parts - lax.axis_index("ctx"), mine, i)
             gfk = gk[i] + dot(vh_ref[h], later, 1, 1)
             k32[pl.ds(h, t, stride=heads), :] = gfk * slope_ref[h]
             v32[pl.ds(h, t, stride=heads), :] = gv[i] + dot(fk_ref[h], later, 1, 0)
             return carry
 
-        lax.fori_loop(0, size, one, 0)
+        lax.fori_loop(0, size, one, 0, unroll=UNROLL)
         base += size
     gk_ref[...] = k32[...].astype(BF)
     gv_ref[...] = v32[...].astype(BF)
@@ -166,18 +161,33 @@
     )(*args)
 
 
-def chain(part, n, reverse):
+def swap(x, low, n, cores):
+    pairs = []
+    for c in range(n):
+        for r in range(cores):
+            to = (2 * low + 1 - c, r) if c in (low, low + 1) else (c, r ^ 1 if cores % 2 == 0 else r)
+            pairs.append((c * cores + r, to[0] * cores + to[1]))
+    return lax.ppermute(x, ("ctx", "rep"), pairs)
+
+
+def chain(part, n, cores, reverse):
     got = []
     running = part
     for hop in range(n - 1):
-        pair = (n - 1 - hop, n - 2 - hop) if reverse else (hop, hop + 1)
-        received = lax.ppermute(running, "ctx", [pair])
+        received = swap(running, n - 2 - hop if reverse else hop, n, cores)
         got.append(received)
         running = (part.astype(F32) + received.astype(F32)).astype(BF)
     return got
 
 
-def shards(n, query_in, key_in, value_in, grad_out):
+def pick(place, got, i):
+    total = jnp.zeros(got[0].shape[1:], got[0].dtype)
+    for hop, part in enumerate(got):
+        total = jnp.where(place == hop + 1, part[i], total)
+    return total
+
+
+def shards(n, cores, query_in, key_in, value_in, grad_out):
     _, t, heads, d = query_in.shape
     m = min(CHUNKS, heads)
     sizes = [heads // m + (1 if c < heads % m else 0) for c in range(m)]
@@ -194,7 +204,7 @@
         [whole(BF), whole(BF), whole(F32)] + [S((s, d, d), BF) for s in sizes],
         [wide, wide], (k, v), heads * mm, "key",
     )
-    ups = [chain(s, n, False) for s in states]
+    ups = [chain(s, n, cores, False) for s in states]
     fq, gh, slope_q, scores, raw = call(
         functools.partial(query_kernel, heads, t),
         [whole(BF), whole(BF), whole(F32), S((heads, t, t), BF), whole(F32)],
@@ -210,7 +220,7 @@
             [], (fq, gh, raw, *ups[c]), s * mm * 2, "norm",
         )
         normed.append(nb)
-        downs.append(chain(grad, n, True))
+        downs.append(chain(grad, n, cores, True))
         gq, gk, gv = call(
             functools.partial(back_kernel, bases[c], s, t),
             [piece(BF), piece(F32), piece(F32)],
@@ -234,7 +244,7 @@
 def solution(mesh):
     placed = P(("groups", "rep"), "ctx", "head", None)
     return jax.shard_map(
-        functools.partial(shards, mesh.shape["ctx"]),
+        functools.partial(shards, mesh.shape["ctx"], mesh.shape["rep"]),
         mesh=mesh,
         in_specs=(placed,) * 4,
         out_specs=(placed,) * 4,

time: 81.4 us -> 65.1 us (0.80)
  the two profiles are of different devices: /device:TPU:8 before, /device:TPU:0 now
where the time goes in v2:
time: 65.1 us; the launch traced here: 64.9 us
  starting transfers between devices  33.7 us (52%)
  Pallas kernels  21.6 us (33%)
  waiting for transfers between devices  5.63 us (9%)
  local copies, waits for them, and re-layouts  2.45 us (4%)
  between operations  0.87 us (1%)
    ppermute x24, starting transfers between devices, swap(): return lax.ppermute(x, ('ctx', 'rep'), pairs)  33.7 us
    pallas_call x12, Pallas kernels, call(): pl.pallas_call(body, out_shape=outs, scratch_shapes=scratch, compiler_par...  21.6 us
    ppermute x24, waiting for transfers between devices, swap(): return lax.ppermute(x, ('ctx', 'rep'), pairs)  5.63 us
    unnamed x8, local copies, waits for them, and re-layouts  2.45 us
  transfers between devices with their start and end apart: 24, of which 3 were waited for; matrix products, arithmetic and copies ran while one was open for 1% of the time, Pallas kernels for 24%

profile of v2, /device:TPU:0, one launch (start us, length us, event | category | flops | bytes accessed | tf_op | source)
XLA Modules:
  0.0 64.9 jit_solution(5878250144316241758)
XLA Ops:
  0.6 1.2 %copy-done = bf16[1,256,16,128]{3,2,1,0:T(8,128)(2,1)S(1)} copy-done((bf16[1,256,16,128]{3,2,1,0:T(8,128)(2,1)S(1)}, bf16[1,256,16,128]{3,2,1,0:T(8,128)(2,1)}, u32[]{:S(2)}) %copy-start) | copy-done | bytes 1048600
  1.9 1.2 %copy-done.1 = bf16[1,256,16,128]{3,2,1,0:T(8,128)(2,1)S(1)} copy-done((bf16[1,256,16,128]{3,2,1,0:T(8,128)(2,1)S(1)}, bf16[1,256,16,128]{3,2,1,0:T(8,128)(2,1)}, u32[]{:S(2)}) %copy-start.1) | copy-done | bytes 1048600
  3.1 2.1 %key.1 = (bf16[16,256,128]{2,1,0:T(8,128)(2,1)S(1)}, bf16[16,256,128]{2,1,0:T(8,128)(2,1)S(1)}, f32[16,256,128]{2,1,0:T(8,128)S(1)}, bf16[4,128,128]{2,1,0:T(8,1...) custom-call(bf16[4096,128]{1,0:T(8,128)(2,1)S(1)} %bitcast.8, ...), custom_call_target="tpu_custom_call" | custom-call | flops 134217728 | bytes 2097152 | tf_op jit(solution)/shard_map/key/pallas_call | solution.py:154
  5.2 3.1 %collective-permute-start = (bf16[4,128,128]{2,1,0:T(8,128)(2,1)S(1)}, bf16[4,128,128]{2,1,0:T(8,128)(2,1)S(1)}, u32[]{:S(2)}, u32[]{:S(2)}) collective-permute-start(bf16[4,128,128]{2,1,0:T(8,128)(2,1)S(1)} %get-tuple-element.53), channel_id=1, source_target_pairs={{0,4},{1,5},{4,0},{5,1},{8,9},{9,8},{12,13},{13,12},{2,6},{3,7},{6... | collective-permute-start | bytes 393224 | tf_op jit(solution)/shard_map/ppermute | solution.py:170
  8.4 1.9 %collective-permute-start.6 = (bf16[4,128,128]{2,1,0:T(8,128)(2,1)S(1)}, bf16[4,128,128]{2,1,0:T(8,128)(2,1)S(1)}, u32[]{:S(2)}, u32[]{:S(2)}) collective-permute-start(bf16[4,128,128]{2,1,0:T(8,128)(2,1)S(1)} %get-tuple-element.57), channel_id=1, source_target_pairs={{0,4},{1,5},{4,0},{5,1},{8,9},{9,8},{12,13},{13,12},{2,6},{3,7},{6... | collective-permute-start | bytes 393224 | tf_op jit(solution)/shard_map/ppermute | solution.py:170
  10.4 3.9 %query.1 = (bf16[16,256,128]{2,1,0:T(8,128)(2,1)S(1)}, bf16[16,256,128]{2,1,0:T(8,128)(2,1)S(1)}, f32[16,256,128]{2,1,0:T(8,128)S(1)}, bf16[16,256,256]{2,1,0:T(8,128)(2,1)S(1)}, f32[16,256,128]{2,1,0:T(8,128)S(1)}) custom-call(bf16[4096,128]{1,0:T(8,128)(2,1)S(1)} %bitcast.10, bf16[4096,128]{1,0:T(8,128)(2,1)S(1)} %bitcast.11, ...), custom_call_target="tpu_custom_call" | custom-call | flops 536870912 | bytes 4194304 | tf_op jit(solution)/shard_map/query/pallas_call | solution.py:154
  14.4 1.0 %collective-permute-done.3.rest_0_ = bf16[4,128,128]{2,1,0:T(8,128)(2,1)S(1)} collective-permute-done((bf16[4,128,128]{2,1,0:T(8,128)(2,1)S(1)}, bf16[4,128,128]{2,1,0:T(8,128)(2,1)S(1)}, u32[]{:S(2)}, u32[]{:S(2)}) %collective-permute-start.3) | collective-permute-done | bytes 131104 | tf_op jit(solution)/shard_map/ppermute | solution.py:170
  15.6 2.7 %collective-permute-done.6.rest_0_ = bf16[4,128,128]{2,1,0:T(8,128)(2,1)S(1)} collective-permute-done((bf16[4,128,128]{2,1,0:T(8,128)(2,1)S(1)}, bf16[4,128,128]{2,1,0:T(8,128)(2,1)S(1)}, u32[]{:S(2)}, u32[]{:S(2)}) %collective-permute-start.6) | collective-permute-done | bytes 131104 | tf_op jit(solution)/shard_map/ppermute | solution.py:170
  18.4 1.9 %collective-permute-done.9.rest_0_ = bf16[4,128,128]{2,1,0:T(8,128)(2,1)S(1)} collective-permute-done((bf16[4,128,128]{2,1,0:T(8,128)(2,1)S(1)}, bf16[4,128,128]{2,1,0:T(8,128)(2,1)S(1)}, u32[]{:S(2)}, u32[]{:S(2)}) %collective-permute-start.9) | collective-permute-done | bytes 131104 | tf_op jit(solution)/shard_map/ppermute | solution.py:170
  20.4 0.6 collective-permute-start.2
  21.1 0.6 collective-permute-start.8
  21.7 0.2 collective-permute-start.11
  22.0 0.7 %norm.4 = (bf16[4,256,128]{2,1,0:T(8,128)(2,1)S(1)}, bf16[4,256,128]{2,1,0:T(8,128)(2,1)S(1)}, bf16[4,128,128]{2,1,0:T(8,128)(2,1)S(1)}, bf16[4,128,128]{2,1,0:T(8,128)(2,1)S(1)}) custom-call(bf16[16,256,128]{2,1,0:T(8,128)(2,1)S(1)} %get-tuple-element.50.fq_ref, bf16[16,256,128]{2,1,0:T(8,128)(2,1)S(1)} %get-tuple-element.51.gh_ref, ...), custom_call_target="tpu_custom_call" | custom-call | flops 67108864 | bytes 4587520 | tf_op jit(solution)/shard_map/norm/pallas_call | solution.py:154
  22.7 0.4 collective-permute-start.12
  23.1 0.7 %norm.5 = (bf16[4,256,128]{2,1,0:T(8,128)(2,1)S(1)}, bf16[4,256,128]{2,1,0:T(8,128)(2,1)S(1)}, bf16[4,128,128]{2,1,0:T(8,128)(2,1)S(1)}, bf16[4,128,128]{2,1,0:T(8,128)(2,1)S(1)}) custom-call(bf16[16,256,128]{2,1,0:T(8,128)(2,1)S(1)} %get-tuple-element.50.fq_ref, bf16[16,256,128]{2,1,0:T(8,128)(2,1)S(1)} %get-tuple-element.51.gh_ref, ...), custom_call_target="tpu_custom_call" | custom-call | flops 67108864 | bytes 4587520 | tf_op jit(solution)/shard_map/norm/pallas_call | solution.py:154
  23.9 0.2 collective-permute-start.15
  24.1 0.7 %norm.6 = (bf16[4,256,128]{2,1,0:T(8,128)(2,1)S(1)}, bf16[4,256,128]{2,1,0:T(8,128)(2,1)S(1)}, bf16[4,128,128]{2,1,0:T(8,128)(2,1)S(1)}, bf16[4,128,128]{2,1,0:T(8,128)(2,1)S(1)}) custom-call(bf16[16,256,128]{2,1,0:T(8,128)(2,1)S(1)} %get-tuple-element.50.fq_ref, bf16[16,256,128]{2,1,0:T(8,128)(2,1)S(1)} %get-tuple-element.51.gh_ref, ...), custom_call_target="tpu_custom_call" | custom-call | flops 67108864 | bytes 4587520 | tf_op jit(solution)/shard_map/norm/pallas_call | solution.py:154
  24.8 0.4 collective-permute-start.18
  25.2 0.7 %norm.7 = (bf16[4,256,128]{2,1,0:T(8,128)(2,1)S(1)}, bf16[4,256,128]{2,1,0:T(8,128)(2,1)S(1)}, bf16[4,128,128]{2,1,0:T(8,128)(2,1)S(1)}, bf16[4,128,128]{2,1,0:T(8,128)(2,1)S(1)}) custom-call(bf16[16,256,128]{2,1,0:T(8,128)(2,1)S(1)} %get-tuple-element.50.fq_ref, bf16[16,256,128]{2,1,0:T(8,128)(2,1)S(1)} %get-tuple-element.51.gh_ref, ...), custom_call_target="tpu_custom_call" | custom-call | flops 67108864 | bytes 4587520 | tf_op jit(solution)/shard_map/norm/pallas_call | solution.py:154
  26.2 0.4 collective-permute-start.13
  26.9 0.4 collective-permute-start.19
  27.4 0.2 collective-permute-start.22
  27.7 20.5 %collective-permute-start.14 = (bf16[4,128,128]{2,1,0:T(8,128)(2,1)S(1)}, bf16[4,128,128]{2,1,0:T(8,128)(2,1)S(1)}, u32[]{:S(2)}, u32[]{:S(2)}) collective-permute-start(bf16[4,128,128]{2,1,0:T(8,128)(2,1)S(1)} %fusion.9), channel_id=1, source_target_pairs={{0,4},{1,5},{4,0},{5,1},{8,9},{9,8},{12,13},{13,12},{2,6},{3,7},{6... | collective-permute-start | bytes 393224 | tf_op jit(solution)/shard_map/ppermute | solution.py:170
  48.2 0.7 %collective-permute-start.17 = (bf16[4,128,128]{2,1,0:T(8,128)(2,1)S(1)}, bf16[4,128,128]{2,1,0:T(8,128)(2,1)S(1)}, u32[]{:S(2)}, u32[]{:S(2)}) collective-permute-start(bf16[4,128,128]{2,1,0:T(8,128)(2,1)S(1)} %fusion.11), channel_id=1, source_target_pairs={{0,4},{1,5},{4,0},{5,1},{8,9},{9,8},{12,13},{13,12},{2,6},{3,7},{6... | collective-permute-start | bytes 393224 | tf_op jit(solution)/shard_map/ppermute | solution.py:170
  49.0 1.7 %collective-permute-start.20 = (bf16[4,128,128]{2,1,0:T(8,128)(2,1)S(1)}, bf16[4,128,128]{2,1,0:T(8,128)(2,1)S(1)}, u32[]{:S(2)}, u32[]{:S(2)}) collective-permute-start(bf16[4,128,128]{2,1,0:T(8,128)(2,1)S(1)} %fusion.13), channel_id=1, source_target_pairs={{0,4},{1,5},{4,0},{5,1},{8,9},{9,8},{12,13},{13,12},{2,6},{3,7},{6... | collective-permute-start | bytes 393224 | tf_op jit(solution)/shard_map/ppermute | solution.py:170
  50.7 1.4 %collective-permute-start.23 = (bf16[4,128,128]{2,1,0:T(8,128)(2,1)S(1)}, bf16[4,128,128]{2,1,0:T(8,128)(2,1)S(1)}, u32[]{:S(2)}, u32[]{:S(2)}) collective-permute-start(bf16[4,128,128]{2,1,0:T(8,128)(2,1)S(1)} %fusion.15), channel_id=1, source_target_pairs={{0,4},{1,5},{4,0},{5,1},{8,9},{9,8},{12,13},{13,12},{2,6},{3,7},{6... | collective-permute-start | bytes 393224 | tf_op jit(solution)/shard_map/ppermute | solution.py:170
  52.1 1.3 %back.4 = (bf16[4,256,128]{2,1,0:T(8,128)(2,1)S(1)}, f32[4,256,128]{2,1,0:T(8,128)S(1)}, f32[4,256,128]{2,1,0:T(8,128)S(1)}) custom-call(bf16[16,256,128]{2,1,0:T(8,128)(2,1)S(1)} %get-tuple-element.50.fq_ref, bf16[16,256,128]{2,1,0:T(8,128)(2,1)S(1)} %get-tuple-element.48.fk_ref, bf16[16,256,128]{2,1,0:T(8,128)(2,1)S(1)} %get-tuple-element.49.vh_ref, ...), custom_call_target="tpu_custom_call" | custom-call | flops 301989888 | bytes 7733248 | tf_op jit(solution)/shard_map/back/pallas_call | solution.py:154
  53.4 1.3 %back.5 = (bf16[4,256,128]{2,1,0:T(8,128)(2,1)S(1)}, f32[4,256,128]{2,1,0:T(8,128)S(1)}, f32[4,256,128]{2,1,0:T(8,128)S(1)}) custom-call(bf16[16,256,128]{2,1,0:T(8,128)(2,1)S(1)} %get-tuple-element.50.fq_ref, bf16[16,256,128]{2,1,0:T(8,128)(2,1)S(1)} %get-tuple-element.48.fk_ref, bf16[16,256,128]{2,1,0:T(8,128)(2,1)S(1)} %get-tuple-element.49.vh_ref, ...), custom_call_target="tpu_custom_call" | custom-call | flops 301989888 | bytes 7733248 | tf_op jit(solution)/shard_map/back/pallas_call | solution.py:154
  54.8 1.3 %back.6 = (bf16[4,256,128]{2,1,0:T(8,128)(2,1)S(1)}, f32[4,256,128]{2,1,0:T(8,128)S(1)}, f32[4,256,128]{2,1,0:T(8,128)S(1)}) custom-call(bf16[16,256,128]{2,1,0:T(8,128)(2,1)S(1)} %get-tuple-element.50.fq_ref, bf16[16,256,128]{2,1,0:T(8,128)(2,1)S(1)} %get-tuple-element.48.fk_ref, bf16[16,256,128]{2,1,0:T(8,128)(2,1)S(1)} %get-tuple-element.49.vh_ref, ...), custom_call_target="tpu_custom_call" | custom-call | flops 301989888 | bytes 7733248 | tf_op jit(solution)/shard_map/back/pallas_call | solution.py:154
  56.1 1.3 %back.7 = (bf16[4,256,128]{2,1,0:T(8,128)(2,1)S(1)}, f32[4,256,128]{2,1,0:T(8,128)S(1)}, f32[4,256,128]{2,1,0:T(8,128)S(1)}) custom-call(bf16[16,256,128]{2,1,0:T(8,128)(2,1)S(1)} %get-tuple-element.50.fq_ref, bf16[16,256,128]{2,1,0:T(8,128)(2,1)S(1)} %get-tuple-element.48.fk_ref, bf16[16,256,128]{2,1,0:T(8,128)(2,1)S(1)} %get-tuple-element.49.vh_ref, ...), custom_call_target="tpu_custom_call" | custom-call | flops 301989888 | bytes 7733248 | tf_op jit(solution)/shard_map/back/pallas_call | solution.py:154
  57.4 3.6 %gather.1 = (bf16[4096,128]{1,0:T(8,128)(2,1)}, bf16[4096,128]{1,0:T(8,128)(2,1)}) custom-call(bf16[4,256,128]{2,1,0:T(8,128)(2,1)S(1)} %get-tuple-element.54.refs_0_, bf16[4,256,128]{2,1,0:T(8,128)(2,1)S(1)} %get-tuple-element.56.refs_1_, bf16[4,256,128]{2,1,0:T(8,128)(2,1)S(1)} %get-tuple-element.58.refs_2_, ...), custom_call_target="tpu_custom_call" | custom-call | flops 134217728 | bytes 2097152 | tf_op jit(solution)/shard_map/gather/pallas_call | solution.py:154
  61.1 3.8 %last.1 = (bf16[4096,128]{1,0:T(8,128)(2,1)}, bf16[4096,128]{1,0:T(8,128)(2,1)}) custom-call(bf16[16,256,128]{2,1,0:T(8,128)(2,1)S(1)} %get-tuple-element.48.fk_ref, bf16[16,256,128]{2,1,0:T(8,128)(2,1)S(1)} %get-tuple-element.49.vh_ref, f32[16,256,128]{2,1,0:T(8,128)S(1)} %get-tuple-element.77.slope_ref, f32[4,256,128]{2,1,0:T(8,128)S(1)} %get-tuple-element.78.refs_0_, ...), custom_call_target="tpu_custom_call" | custom-call | flops 268435456 | bytes 9961472 | tf_op jit(solution)/shard_map/last/pallas_call | solution.py:154
  (52 shorter events, 1.6 us)
Async XLA Ops:
  0.6 1.2 %copy-start = (bf16[1,256,16,128]{3,2,1,0:T(8,128)(2,1)S(1)}, bf16[1,256,16,128]{3,2,1,0:T(8,128)(2,1)}, u32[]{:S(2)}) copy-start(bf16[1,256,16,128]{3,2,1,0:T(8,128)(2,1)} %param.5) | copy-start | bytes 3145732
  1.9 1.2 %copy-start.1 = (bf16[1,256,16,128]{3,2,1,0:T(8,128)(2,1)S(1)}, bf16[1,256,16,128]{3,2,1,0:T(8,128)(2,1)}, u32[]{:S(2)}) copy-start(bf16[1,256,16,128]{3,2,1,0:T(8,128)(2,1)} %param.6) | copy-start | bytes 3145732
  3.1 7.3 %copy-start.2 = (bf16[1,256,16,128]{3,2,1,0:T(8,128)(2,1)S(1)}, bf16[1,256,16,128]{3,2,1,0:T(8,128)(2,1)}, u32[]{:S(2)}) copy-start(bf16[1,256,16,128]{3,2,1,0:T(8,128)(2,1)} %param.4) | copy-start | bytes 3145732
  3.1 7.3 %copy-start.3 = (bf16[1,256,16,128]{3,2,1,0:T(8,128)(2,1)S(1)}, bf16[1,256,16,128]{3,2,1,0:T(8,128)(2,1)}, u32[]{:S(2)}) copy-start(bf16[1,256,16,128]{3,2,1,0:T(8,128)(2,1)} %param.7) | copy-start | bytes 3145732
  5.2 9.1 %collective-permute-start = (bf16[4,128,128]{2,1,0:T(8,128)(2,1)S(1)}, bf16[4,128,128]{2,1,0:T(8,128)(2,1)S(1)}, u32[]{:S(2)}, u32[]{:S(2)}) collective-permute-start(bf16[4,128,128]{2,1,0:T(8,128)(2,1)S(1)} %get-tuple-element.53), channel_id=1, source_target_pairs={{0,4},{1,5},{4,0},{5,1},{8,9},{9,8},{12,13},{13,12},{2,6},{3,7},{6... | collective-permute-start | bytes 393224 | tf_op jit(solution)/shard_map/ppermute | solution.py:170
  8.3 7.1 %collective-permute-start.3 = (bf16[4,128,128]{2,1,0:T(8,128)(2,1)S(1)}, bf16[4,128,128]{2,1,0:T(8,128)(2,1)S(1)}, u32[]{:S(2)}, u32[]{:S(2)}) collective-permute-start(bf16[4,128,128]{2,1,0:T(8,128)(2,1)S(1)} %get-tuple-element.55), channel_id=1, source_target_pairs={{0,4},{1,5},{4,0},{5,1},{8,9},{9,8},{12,13},{13,12},{2,6},{3,7},{6... | collective-permute-start | bytes 393224 | tf_op jit(solution)/shard_map/ppermute | solution.py:170
  8.4 9.9 %collective-permute-start.6 = (bf16[4,128,128]{2,1,0:T(8,128)(2,1)S(1)}, bf16[4,128,128]{2,1,0:T(8,128)(2,1)S(1)}, u32[]{:S(2)}, u32[]{:S(2)}) collective-permute-start(bf16[4,128,128]{2,1,0:T(8,128)(2,1)S(1)} %get-tuple-element.57), channel_id=1, source_target_pairs={{0,4},{1,5},{4,0},{5,1},{8,9},{9,8},{12,13},{13,12},{2,6},{3,7},{6... | collective-permute-start | bytes 393224 | tf_op jit(solution)/shard_map/ppermute | solution.py:170
  10.3 9.9 %collective-permute-start.9 = (bf16[4,128,128]{2,1,0:T(8,128)(2,1)S(1)}, bf16[4,128,128]{2,1,0:T(8,128)(2,1)S(1)}, u32[]{:S(2)}, u32[]{:S(2)}) collective-permute-start(bf16[4,128,128]{2,1,0:T(8,128)(2,1)S(1)} %get-tuple-element.59), channel_id=1, source_target_pairs={{0,4},{1,5},{4,0},{5,1},{8,9},{9,8},{12,13},{13,12},{2,6},{3,7},{6... | collective-permute-start | bytes 393224 | tf_op jit(solution)/shard_map/ppermute | solution.py:170
  14.3 6.0 %collective-permute-start.1 = (bf16[4,128,128]{2,1,0:T(8,128)(2,1)S(1)}, bf16[4,128,128]{2,1,0:T(8,128)(2,1)S(1)}, u32[]{:S(2)}, u32[]{:S(2)}) collective-permute-start(bf16[4,128,128]{2,1,0:T(8,128)(2,1)S(1)} %fusion), channel_id=1, source_target_pairs={{0,1},{1,0},{4,8},{5,9},{8,4},{9,5},{12,13},{13,12},{2,3},{3,2},{6... | collective-permute-start | bytes 393224 | tf_op jit(solution)/shard_map/ppermute | solution.py:170
  15.5 5.5 %collective-permute-start.4 = (bf16[4,128,128]{2,1,0:T(8,128)(2,1)S(1)}, bf16[4,128,128]{2,1,0:T(8,128)(2,1)S(1)}, u32[]{:S(2)}, u32[]{:S(2)}) collective-permute-start(bf16[4,128,128]{2,1,0:T(8,128)(2,1)S(1)} %fusion.2), channel_id=1, source_target_pairs={{0,1},{1,0},{4,8},{5,9},{8,4},{9,5},{12,13},{13,12},{2,3},{3,2},{6... | collective-permute-start | bytes 393224 | tf_op jit(solution)/shard_map/ppermute | solution.py:170
  18.3 2.8 %collective-permute-start.7 = (bf16[4,128,128]{2,1,0:T(8,128)(2,1)S(1)}, bf16[4,128,128]{2,1,0:T(8,128)(2,1)S(1)}, u32[]{:S(2)}, u32[]{:S(2)}) collective-permute-start(bf16[4,128,128]{2,1,0:T(8,128)(2,1)S(1)} %fusion.4), channel_id=1, source_target_pairs={{0,1},{1,0},{4,8},{5,9},{8,4},{9,5},{12,13},{13,12},{2,3},{3,2},{6... | collective-permute-start | bytes 393224 | tf_op jit(solution)/shard_map/ppermute | solution.py:170
  20.3 1.4 %collective-permute-start.10 = (bf16[4,128,128]{2,1,0:T(8,128)(2,1)S(1)}, bf16[4,128,128]{2,1,0:T(8,128)(2,1)S(1)}, u32[]{:S(2)}, u32[]{:S(2)}) collective-permute-start(bf16[4,128,128]{2,1,0:T(8,128)(2,1)S(1)} %fusion.6), channel_id=1, source_target_pairs={{0,1},{1,0},{4,8},{5,9},{8,4},{9,5},{12,13},{13,12},{2,3},{3,2},{6... | collective-permute-start | bytes 393224 | tf_op jit(solution)/shard_map/ppermute | solution.py:170
  20.4 1.5 %collective-permute-start.2 = (bf16[4,128,128]{2,1,0:T(8,128)(2,1)S(1)}, bf16[4,128,128]{2,1,0:T(8,128)(2,1)S(1)}, u32[]{:S(2)}, u32[]{:S(2)}) collective-permute-start(bf16[4,128,128]{2,1,0:T(8,128)(2,1)S(1)} %fusion.1), channel_id=1, source_target_pairs={{0,1},{1,0},{4,5},{5,4},{8,12},{9,13},{12,8},{13,9},{2,3},{3,2},{6... | collective-permute-start | bytes 393224 | tf_op jit(solution)/shard_map/ppermute | solution.py:170
  21.0 2.1 %collective-permute-start.5 = (bf16[4,128,128]{2,1,0:T(8,128)(2,1)S(1)}, bf16[4,128,128]{2,1,0:T(8,128)(2,1)S(1)}, u32[]{:S(2)}, u32[]{:S(2)}) collective-permute-start(bf16[4,128,128]{2,1,0:T(8,128)(2,1)S(1)} %fusion.3), channel_id=1, source_target_pairs={{0,1},{1,0},{4,5},{5,4},{8,12},{9,13},{12,8},{13,9},{2,3},{3,2},{6... | collective-permute-start | bytes 393224 | tf_op jit(solution)/shard_map/ppermute | solution.py:170
  21.1 2.9 %collective-permute-start.8 = (bf16[4,128,128]{2,1,0:T(8,128)(2,1)S(1)}, bf16[4,128,128]{2,1,0:T(8,128)(2,1)S(1)}, u32[]{:S(2)}, u32[]{:S(2)}) collective-permute-start(bf16[4,128,128]{2,1,0:T(8,128)(2,1)S(1)} %fusion.5), channel_id=1, source_target_pairs={{0,1},{1,0},{4,5},{5,4},{8,12},{9,13},{12,8},{13,9},{2,3},{3,2},{6... | collective-permute-start | bytes 393224 | tf_op jit(solution)/shard_map/ppermute | solution.py:170
  21.7 3.5 %collective-permute-start.11 = (bf16[4,128,128]{2,1,0:T(8,128)(2,1)S(1)}, bf16[4,128,128]{2,1,0:T(8,128)(2,1)S(1)}, u32[]{:S(2)}, u32[]{:S(2)}) collective-permute-start(bf16[4,128,128]{2,1,0:T(8,128)(2,1)S(1)} %fusion.7), channel_id=1, source_target_pairs={{0,1},{1,0},{4,5},{5,4},{8,12},{9,13},{12,8},{13,9},{2,3},{3,2},{6... | collective-permute-start | bytes 393224 | tf_op jit(solution)/shard_map/ppermute | solution.py:170
  22.7 3.5 %collective-permute-start.12 = (bf16[4,128,128]{2,1,0:T(8,128)(2,1)S(1)}, bf16[4,128,128]{2,1,0:T(8,128)(2,1)S(1)}, u32[]{:S(2)}, u32[]{:S(2)}) collective-permute-start(bf16[4,128,128]{2,1,0:T(8,128)(2,1)S(1)} %get-tuple-element.86), channel_id=1, source_target_pairs={{0,1},{1,0},{4,5},{5,4},{8,12},{9,13},{12,8},{13,9},{2,3},{3,2},{6... | collective-permute-start | bytes 393224 | tf_op jit(solution)/shard_map/ppermute | solution.py:170
  23.9 2.8 %collective-permute-start.15 = (bf16[4,128,128]{2,1,0:T(8,128)(2,1)S(1)}, bf16[4,128,128]{2,1,0:T(8,128)(2,1)S(1)}, u32[]{:S(2)}, u32[]{:S(2)}) collective-permute-start(bf16[4,128,128]{2,1,0:T(8,128)(2,1)S(1)} %get-tuple-element.87), channel_id=1, source_target_pairs={{0,1},{1,0},{4,5},{5,4},{8,12},{9,13},{12,8},{13,9},{2,3},{3,2},{6... | collective-permute-start | bytes 393224 | tf_op jit(solution)/shard_map/ppermute | solution.py:170
  24.8 2.1 %collective-permute-start.18 = (bf16[4,128,128]{2,1,0:T(8,128)(2,1)S(1)}, bf16[4,128,128]{2,1,0:T(8,128)(2,1)S(1)}, u32[]{:S(2)}, u32[]{:S(2)}) collective-permute-start(bf16[4,128,128]{2,1,0:T(8,128)(2,1)S(1)} %get-tuple-element.88), channel_id=1, source_target_pairs={{0,1},{1,0},{4,5},{5,4},{8,12},{9,13},{12,8},{13,9},{2,3},{3,2},{6... | collective-permute-start | bytes 393224 | tf_op jit(solution)/shard_map/ppermute | solution.py:170
  26.0 1.4 %collective-permute-start.21 = (bf16[4,128,128]{2,1,0:T(8,128)(2,1)S(1)}, bf16[4,128,128]{2,1,0:T(8,128)(2,1)S(1)}, u32[]{:S(2)}, u32[]{:S(2)}) collective-permute-start(bf16[4,128,128]{2,1,0:T(8,128)(2,1)S(1)} %get-tuple-element.89), channel_id=1, source_target_pairs={{0,1},{1,0},{4,5},{5,4},{8,12},{9,13},{12,8},{13,9},{2,3},{3,2},{6... | collective-permute-start | bytes 393224 | tf_op jit(solution)/shard_map/ppermute | solution.py:170
  26.2 1.4 %collective-permute-start.13 = (bf16[4,128,128]{2,1,0:T(8,128)(2,1)S(1)}, bf16[4,128,128]{2,1,0:T(8,128)(2,1)S(1)}, u32[]{:S(2)}, u32[]{:S(2)}) collective-permute-start(bf16[4,128,128]{2,1,0:T(8,128)(2,1)S(1)} %fusion.8), channel_id=1, source_target_pairs={{0,1},{1,0},{4,8},{5,9},{8,4},{9,5},{12,13},{13,12},{2,3},{3,2},{6... | collective-permute-start | bytes 393224 | tf_op jit(solution)/shard_map/ppermute | solution.py:170
  26.7 21.5 %collective-permute-start.16 = (bf16[4,128,128]{2,1,0:T(8,128)(2,1)S(1)}, bf16[4,128,128]{2,1,0:T(8,128)(2,1)S(1)}, u32[]{:S(2)}, u32[]{:S(2)}) collective-permute-start(bf16[4,128,128]{2,1,0:T(8,128)(2,1)S(1)} %fusion.10), channel_id=1, source_target_pairs={{0,1},{1,0},{4,8},{5,9},{8,4},{9,5},{12,13},{13,12},{2,3},{3,2},{6... | collective-permute-start | bytes 393224 | tf_op jit(solution)/shard_map/ppermute | solution.py:170
  26.9 22.0 %collective-permute-start.19 = (bf16[4,128,128]{2,1,0:T(8,128)(2,1)S(1)}, bf16[4,128,128]{2,1,0:T(8,128)(2,1)S(1)}, u32[]{:S(2)}, u32[]{:S(2)}) collective-permute-start(bf16[4,128,128]{2,1,0:T(8,128)(2,1)S(1)} %fusion.12), channel_id=1, source_target_pairs={{0,1},{1,0},{4,8},{5,9},{8,4},{9,5},{12,13},{13,12},{2,3},{3,2},{6... | collective-permute-start | bytes 393224 | tf_op jit(solution)/shard_map/ppermute | solution.py:170
  27.4 23.2 %collective-permute-start.22 = (bf16[4,128,128]{2,1,0:T(8,128)(2,1)S(1)}, bf16[4,128,128]{2,1,0:T(8,128)(2,1)S(1)}, u32[]{:S(2)}, u32[]{:S(2)}) collective-permute-start(bf16[4,128,128]{2,1,0:T(8,128)(2,1)S(1)} %fusion.14), channel_id=1, source_target_pairs={{0,1},{1,0},{4,8},{5,9},{8,4},{9,5},{12,13},{13,12},{2,3},{3,2},{6... | collective-permute-start | bytes 393224 | tf_op jit(solution)/shard_map/ppermute | solution.py:170
  27.7 33.4 %collective-permute-start.14 = (bf16[4,128,128]{2,1,0:T(8,128)(2,1)S(1)}, bf16[4,128,128]{2,1,0:T(8,128)(2,1)S(1)}, u32[]{:S(2)}, u32[]{:S(2)}) collective-permute-start(bf16[4,128,128]{2,1,0:T(8,128)(2,1)S(1)} %fusion.9), channel_id=1, source_target_pairs={{0,4},{1,5},{4,0},{5,1},{8,9},{9,8},{12,13},{13,12},{2,6},{3,7},{6... | collective-permute-start | bytes 393224 | tf_op jit(solution)/shard_map/ppermute | solution.py:170
  48.2 12.8 %collective-permute-start.17 = (bf16[4,128,128]{2,1,0:T(8,128)(2,1)S(1)}, bf16[4,128,128]{2,1,0:T(8,128)(2,1)S(1)}, u32[]{:S(2)}, u32[]{:S(2)}) collective-permute-start(bf16[4,128,128]{2,1,0:T(8,128)(2,1)S(1)} %fusion.11), channel_id=1, source_target_pairs={{0,4},{1,5},{4,0},{5,1},{8,9},{9,8},{12,13},{13,12},{2,6},{3,7},{6... | collective-permute-start | bytes 393224 | tf_op jit(solution)/shard_map/ppermute | solution.py:170
  49.0 12.1 %collective-permute-start.20 = (bf16[4,128,128]{2,1,0:T(8,128)(2,1)S(1)}, bf16[4,128,128]{2,1,0:T(8,128)(2,1)S(1)}, u32[]{:S(2)}, u32[]{:S(2)}) collective-permute-start(bf16[4,128,128]{2,1,0:T(8,128)(2,1)S(1)} %fusion.13), channel_id=1, source_target_pairs={{0,4},{1,5},{4,0},{5,1},{8,9},{9,8},{12,13},{13,12},{2,6},{3,7},{6... | collective-permute-start | bytes 393224 | tf_op jit(solution)/shard_map/ppermute | solution.py:170
  50.7 10.3 %collective-permute-start.23 = (bf16[4,128,128]{2,1,0:T(8,128)(2,1)S(1)}, bf16[4,128,128]{2,1,0:T(8,128)(2,1)S(1)}, u32[]{:S(2)}, u32[]{:S(2)}) collective-permute-start(bf16[4,128,128]{2,1,0:T(8,128)(2,1)S(1)} %fusion.15), channel_id=1, source_target_pairs={{0,4},{1,5},{4,0},{5,1},{8,9},{9,8},{12,13},{13,12},{2,6},{3,7},{6... | collective-permute-start | bytes 393224 | tf_op jit(solution)/shard_map/ppermute | solution.py:170

commit v3 on v2

v3 whole, which is shorter than its diff:
```python
import functools

import jax
import jax.numpy as jnp
from jax import lax
from jax.experimental import pallas as pl
from jax.experimental.pallas import tpu as pltpu
from jax.sharding import PartitionSpec as P

BF, F32 = jnp.bfloat16, jnp.float32
MIB = 1 << 20
SIZES = [4, 4, 4, 4]
UNROLL = 4
BLOCKS = 4


def dot(a, b, ca, cb):
    return lax.dot_general(a, b, (((ca,), (cb,)), ((), ())), preferred_element_type=F32)


def silu_parts(x):
    sigma = 1.0 / (1.0 + jnp.exp(-x))
    return x * sigma, sigma * (1.0 + x * (1.0 - sigma))


def low_mask(t):
    rows = lax.broadcasted_iota(jnp.int32, (t, t), 0)
    cols = lax.broadcasted_iota(jnp.int32, (t, t), 1)
    return rows >= cols


def widen(src, dst):
    dst[...] = src[...].astype(F32)


def blocks_of(rows):
    size = rows // BLOCKS if rows % (16 * BLOCKS) == 0 else rows
    return [pl.ds(at, size) for at in range(0, rows, size)]


def fetch(sources, landings, wides, sems):
    copies = []
    for src, dst, wide in zip(sources, landings, wides):
        for rows in blocks_of(src.shape[0]):
            copy = pltpu.make_async_copy(src.at[rows], dst.at[rows], sems.at[len(copies)])
            copy.start()
            copies.append((copy, dst, wide, rows))
    for copy, dst, wide, rows in copies:
        copy.wait()
        wide[rows, :] = dst[rows, :].astype(F32)


def flush(wides, stages, results, sems):
    copies = []
    for wide, stage, dst in zip(wides, stages, results):
        for rows in blocks_of(wide.shape[0]):
            stage[rows, :] = wide[rows, :].astype(BF)
            copies.append(pltpu.make_async_copy(stage.at[rows], dst.at[rows], sems.at[len(copies)]))
            copies[-1].start()
    for copy in copies:
        copy.wait()


def key_kernel(base, size, heads, t, first, *refs):
    if first:
        k_ref, v_ref, state_ref, fk_ref, vh_ref, slope_ref, k32, v32, k16, v16, sems = refs
        fetch((k_ref, v_ref), (k16, v16), (k32, v32), sems)
    else:
        k32, v32, state_ref, fk_ref, vh_ref, slope_ref = refs

    def one(i, carry):
        feat, slope = silu_parts(k32[pl.ds(base + i, t, stride=heads), :])
        feat = feat.astype(BF)
        vh = v32[pl.ds(base + i, t, stride=heads), :].astype(BF)
        fk_ref[i] = feat
        vh_ref[i] = vh
        slope_ref[i] = slope
        state_ref[i] = dot(feat, vh, 0, 0).astype(BF)
        return carry

    lax.fori_loop(0, size, one, 0, unroll=UNROLL)


def query_kernel(base, size, heads, t, first, *refs):
    if first:
        q_ref, g_ref, fk_ref, vh_ref, raw_ref, fq_ref, gh_ref, slope_ref, score_ref, q32, g32 = refs
        widen(q_ref, q32)
        widen(g_ref, g32)
    else:
        q32, g32, fk_ref, vh_ref, raw_ref, fq_ref, gh_ref, slope_ref, score_ref = refs

    def one(i, carry):
        feat, slope = silu_parts(q32[pl.ds(base + i, t, stride=heads), :])
        feat = feat.astype(BF)
        fq_ref[i] = feat
        slope_ref[i] = slope
        gh_ref[i] = g32[pl.ds(base + i, t, stride=heads), :].astype(BF)
        scores = jnp.where(low_mask(t), dot(feat, fk_ref[i], 1, 1), 0.0).astype(BF)
        score_ref[i] = scores
        raw_ref[i] = dot(scores, vh_ref[i], 1, 0)
        return carry

    lax.fori_loop(0, size, one, 0, unroll=UNROLL)


def norm_kernel(base, size, heads, t, parts, fq_ref, gh_ref, raw_ref, *rest):
    got, (grad_ref, grad_raw_ref, earlier_ref, wide_ref) = rest[:parts], rest[-4:]

    def one(i, carry):
        earlier = pick(lax.axis_index("ctx"), got, i)
        earlier_ref[i] = earlier
        fq = fq_ref[i]
        raw = raw_ref[i] + dot(fq, earlier, 1, 0)
        inverse = lax.rsqrt(jnp.mean(raw * raw, axis=-1, keepdims=True) + 1.0)
        normed = raw * inverse
        up = gh_ref[i].astype(F32)
        grad = inverse * (up - normed * jnp.mean(up * normed, axis=-1, keepdims=True))
        grad = grad.astype(BF)
        wide_ref[pl.ds(base + i, t, stride=heads), :] = normed
        grad_raw_ref[i] = grad
        grad_ref[i] = dot(fq, grad, 0, 0).astype(BF)
        return carry

    lax.fori_loop(0, size, one, 0, unroll=UNROLL)


def back_kernel(base, size, heads, t, fq_ref, fk_ref, vh_ref, slope_ref, score_ref, grad_raw_ref, earlier_ref, *rest):
    gk_ref, gv_ref, wide_ref = rest[-3:]

    def one(i, carry):
        grad = grad_raw_ref[i]
        fq = fq_ref[i]
        grad_scores = jnp.where(low_mask(t), dot(grad, vh_ref[i], 1, 1), 0.0).astype(BF)
        gfq = dot(grad_scores, fk_ref[i], 1, 0) + dot(grad, earlier_ref[i], 1, 1)
        wide_ref[pl.ds(base + i, t, stride=heads), :] = gfq * slope_ref[i]
        gk_ref[i] = dot(grad_scores, fq, 0, 0)
        gv_ref[i] = dot(score_ref[i], grad, 0, 0)
        return carry

    lax.fori_loop(0, size, one, 0, unroll=UNROLL)


def gather_kernel(count, *refs):
    flush(refs[:count], refs[2 * count : 3 * count], refs[count : 2 * count], refs[-1])


def later_step(base, size, heads, t, parts, refs, wide_k, wide_v):
    fk_ref, vh_ref, slope_ref, gk, gv = refs[:5]
    got = refs[5 : 5 + parts]

    def one(i, carry):
        later = pick(parts - lax.axis_index("ctx"), got, i)
        gfk = gk[i] + dot(vh_ref[i], later, 1, 1)
        wide_k[pl.ds(base + i, t, stride=heads), :] = gfk * slope_ref[i]
        wide_v[pl.ds(base + i, t, stride=heads), :] = gv[i] + dot(fk_ref[i], later, 1, 0)
        return carry

    lax.fori_loop(0, size, one, 0, unroll=UNROLL)


def later_kernel(base, size, heads, t, parts, *refs):
    later_step(base, size, heads, t, parts, refs, *refs[-2:])


def last_kernel(base, size, heads, t, parts, *refs):
    if base:
        wide_k, wide_v, k_out, v_out, k16, v16, sems = refs[5 + parts :]
    else:
        k_out, v_out, k16, v16, sems, wide_k, wide_v = refs[5 + parts :]
    later_step(base, size, heads, t, parts, refs, wide_k, wide_v)
    flush((wide_k, wide_v), (k16, v16), (k_out, v_out), sems)


def call(body, outs, scratch, args, flops, name, specs, out_specs, aliases):
    moved = sum(a.size * a.dtype.itemsize for a in args)
    return pl.pallas_call(
        body,
        out_shape=outs,
        in_specs=specs,
        out_specs=out_specs,
        scratch_shapes=scratch,
        input_output_aliases=aliases,
        compiler_params=pltpu.CompilerParams(vmem_limit_bytes=28 * MIB),
        cost_estimate=pl.CostEstimate(flops=flops, bytes_accessed=moved, transcendentals=0),
        name=name,
    )(*args)


def swap(x, low, n, cores):
    pairs = []
    for c in range(n):
        for r in range(cores):
            to = (2 * low + 1 - c, r) if c in (low, low + 1) else (c, r ^ 1 if cores % 2 == 0 else r)
            pairs.append((c * cores + r, to[0] * cores + to[1]))
    return lax.ppermute(x, ("ctx", "rep"), pairs)


class Order:
    def __init__(self):
        self.before = []

    def tie(self, x):
        return lax.optimization_barrier((x, *self.before))[0] if self.before else x

    def compute(self, body, outs, scratch, args, tied, flops, name, far_in=(), far_out=(), aliases={}):
        args = list(args)
        args[tied] = self.tie(args[tied])
        for i in far_in:
            args[i] = pltpu.with_memory_space_constraint(args[i], pltpu.HBM)
        near, far = pl.BlockSpec(memory_space=pltpu.VMEM), pl.BlockSpec(memory_space=pltpu.HBM)
        made = call(
            body, outs, scratch, args, flops, name,
            [far if i in far_in else near for i in range(len(args))],
            [far if i in far_out else near for i in range(len(outs))], aliases,
        )
        self.before = [made[0]]
        return made


class Chain:
    def __init__(self, order, part, n, cores, reverse):
        self.order, self.part, self.n, self.cores, self.reverse = order, part, n, cores, reverse
        self.got = []

    def hop(self):
        h = len(self.got)
        if h:
            running = (self.part.astype(F32) + self.order.tie(self.got[-1]).astype(F32)).astype(BF)
        else:
            running = self.order.tie(self.part)
        self.order.before.append(running)
        self.got.append(swap(running, self.n - 2 - h if self.reverse else h, self.n, self.cores))


def pick(place, got, i):
    total = jnp.zeros(got[0].shape[1:], got[0].dtype)
    for hop, part in enumerate(got):
        total = jnp.where(place == hop + 1, part[i], total)
    return total


ORDER = [
    "k0", "u0", "k1", "u1", "q0", "k2", "u2", "k3", "u0", "u3", "q1", "u1", "u0", "u2",
    "q2", "u1", "u3", "u2", "n0", "d0", "n1", "d1", "q3", "b0", "u3", "n2", "d0", "b2",
    "d2", "d1", "n3", "d3", "d0", "b3", "d2", "d1", "g0", "d3", "d2", "b1", "d3", "g1",
    "l0", "l1", "l2", "l3",
]


def plan(hops):
    left = {step: ORDER.count(step) for step in ORDER}
    for step in ORDER:
        left[step] -= 1
        if step[0] not in "ud":
            yield step
            continue
        listed = ORDER.count(step)
        done = listed - left[step]
        if done <= hops:
            yield from [step] * (hops - listed + 1 if left[step] == 0 and hops > listed else 1)


def shards(n, cores, query_in, key_in, value_in, grad_out):
    _, t, heads, d = query_in.shape
    sizes = SIZES if sum(SIZES) == heads else [heads // len(SIZES)] * len(SIZES)
    assert sum(sizes) == heads
    m = len(sizes)
    bases = [sum(sizes[:c]) for c in range(m)]
    q, k, v, g = (a.reshape(t * heads, d) for a in (query_in, key_in, value_in, grad_out))
    S = jax.ShapeDtypeStruct
    flat = S((t * heads, d), BF)
    wide = pltpu.VMEM((t * heads, d), F32)
    mm = 2 * t * d * d

    order = Order()
    flat16 = pltpu.VMEM((t * heads, d), BF)
    sems = pltpu.SemaphoreType.DMA((2 * BLOCKS,))
    broad = S((t * heads, d), F32)
    up, down, parts, held = {}, {}, {}, {}

    def of(c, dt):
        return S((sizes[c], t, d), dt)

    def key(c):
        outs = [S((sizes[c], d, d), BF), of(c, BF), of(c, BF), of(c, F32)]
        body = functools.partial(key_kernel, bases[c], sizes[c], heads, t, c == 0)
        if c == 0:
            state, *held["key", c], held["k32"], held["v32"] = order.compute(
                body, outs + [broad] * 2, [flat16, flat16, sems], (k, v), 0, sizes[c] * mm, "key", far_in=(0, 1)
            )
        else:
            state, *held["key", c] = order.compute(
                body, outs, [], (held["k32"], held["v32"]), 0, sizes[c] * mm, "key"
            )
        up[c] = Chain(order, state, n, cores, False)

    def query(c):
        outs = [of(c, F32), of(c, BF), of(c, BF), of(c, F32), S((sizes[c], t, t), BF)]
        fk, vh, _ = held["key", c]
        body = functools.partial(query_kernel, bases[c], sizes[c], heads, t, c == 0)
        if c == 0:
            *held["query", c], held["q32"], held["g32"] = order.compute(
                body, outs + [broad] * 2, [], (q, g, fk, vh), 2, sizes[c] * mm * 4, "query"
            )
        else:
            held["query", c] = order.compute(
                body, outs, [], (held["q32"], held["g32"], fk, vh), 2, sizes[c] * mm * 4, "query"
            )

    def onto(args, outs, names):
        have = [held[name] for name in names if name in held]
        aliases = {len(args) + i: len(outs) + i for i in range(len(have))}
        return (*args, *have), outs + [broad] * len(names), aliases

    def norm(c):
        raw, fq, gh, _, _ = held["query", c]
        s = sizes[c]
        state = S((s, d, d), BF)
        args, outs, aliases = onto((fq, gh, raw, *up[c].got), [state, S((s, t, d), BF), state], ["normed"])
        grad, grad_raw, earlier, held["normed"] = order.compute(
            functools.partial(norm_kernel, bases[c], s, heads, t, n - 1),
            outs, [], args, 3, s * mm * 2, "norm", aliases=aliases,
        )
        held[c] = grad_raw, earlier
        down[c] = Chain(order, grad, n, cores, True)

    def back(c):
        _, fq, _, slope_q, scores = held["query", c]
        fk, vh, _ = held["key", c]
        s = sizes[c]
        piece = S((s, t, d), F32)
        args, outs, aliases = onto((fq, fk, vh, slope_q, scores, *held[c]), [piece, piece], ["gq"])
        *parts[c], held["gq"] = order.compute(
            functools.partial(back_kernel, bases[c], s, heads, t),
            outs, [], args, 6, s * mm * 9, "back", aliases=aliases,
        )

    def gather(which):
        name = ("normed", "gq")[which]
        held["out", which], = order.compute(
            functools.partial(gather_kernel, 1), [flat], [flat16, sems], [held[name]], 0, heads * mm, "gather",
            far_out=(0,),
        )

    def later(c):
        s = sizes[c]
        args = (*held["key", c], *parts[c], *down[c].got)
        if c < m - 1:
            args, outs, aliases = onto(args, [], ["gk", "gv"])
            held["gk"], held["gv"] = order.compute(
                functools.partial(later_kernel, bases[c], s, heads, t, n - 1),
                outs, [], args, 5, s * mm * 2, "later", aliases=aliases,
            )
        else:
            wides = [held["gk"], held["gv"]] if m > 1 else []
            held["last"] = order.compute(
                functools.partial(last_kernel, bases[c], s, heads, t, n - 1),
                [flat, flat], [flat16, flat16, sems] + ([] if wides else [wide, wide]),
                (*args, *wides), 5, s * mm * 2, "last", far_out=(0, 1),
            )

    steps = dict(
        u=lambda c: up[c].hop(), d=lambda c: down[c].hop(), k=key, q=query, n=norm, b=back, g=gather, l=later
    )
    for step in plan(n - 1):
        steps[step[0]](*map(int, step[1:].split(".") if step[1:] else ()))
    output, grad_query = held["out", 0], held["out", 1]
    grad_key, grad_value = held["last"]
    return tuple(a.reshape(1, t, heads, d) for a in (output, grad_query, grad_key, grad_value))


def solution(mesh):
    placed = P(("groups", "rep"), "ctx", "head", None)
    return jax.shard_map(
        functools.partial(shards, mesh.shape["ctx"], mesh.shape["rep"]),
        mesh=mesh,
        in_specs=(placed,) * 4,
        out_specs=(placed,) * 4,
        check_vma=False,
    )
```

time: 65.1 us -> 55.2 us (0.85)
  starting transfers between devices: 33.7 us -> 26.7 us
  waiting for transfers between devices: 5.63 us -> 2.77 us
  local copies, waits for them, and re-layouts: 2.45 us -> 0.85 us
  Pallas kernels: 21.6 us -> 22.8 us
    ppermute x24, starting transfers between devices: 33.7 us -> 26.7 us  [swap(): return lax.ppermute(x, ('ctx', 'rep'), pairs)]
    ppermute x24, waiting for transfers between devices: 5.63 us -> 2.77 us  [swap(): return lax.ppermute(x, ('ctx', 'rep'), pairs)]
    unnamed x8 -> x4, local copies, waits for them, and re-layouts: 2.45 us -> 0.85 us
    pallas_call x12 -> x22, Pallas kernels: 21.6 us -> 22.8 us  [call(): pl.pallas_call(body, out_shape=outs, in_specs=specs, out_specs=out_specs,...]
  transfers between devices with their start and end apart: 24 -> 24, of which waited for: 3 -> 3; matrix products, arithmetic and copies ran while one was open for 1% -> 1% of each run, Pallas kernels for 24% -> 34%
where the time goes in v3:
time: 55.2 us; the launch traced here: 55 us
  starting transfers between devices  26.7 us (48%)
  Pallas kernels  22.8 us (41%)
  waiting for transfers between devices  2.77 us (5%)
  between operations  1.22 us (2%)
  local copies, waits for them, and re-layouts  0.85 us (2%)
  other arithmetic  0.62 us (1%)
    ppermute x24, starting transfers between devices, swap(): return lax.ppermute(x, ('ctx', 'rep'), pairs)  26.7 us
    pallas_call x22, Pallas kernels, call(): pl.pallas_call(body, out_shape=outs, in_specs=specs, out_specs=out_specs,...  22.8 us
    ppermute x24, waiting for transfers between devices, swap(): return lax.ppermute(x, ('ctx', 'rep'), pairs)  2.77 us
  transfers between devices with their start and end apart: 24, of which 3 were waited for; matrix products, arithmetic and copies ran while one was open for 1% of the time, Pallas kernels for 34%

profile of v3, /device:TPU:0, one launch (start us, length us, event | category | flops | bytes accessed | tf_op | source)
XLA Modules:
  0.0 55.0 jit_solution(3189063150007649302)
XLA Ops:
  0.6 2.2 %key.4 = (bf16[4,128,128]{2,1,0:T(8,128)(2,1)S(1)}, bf16[4,256,128]{2,1,0:T(8,128)(2,1)S(1)}, bf16[4,256,128]{2,1,0:T(8,128)(2,1)S(1)}, f32[4,256,128]{2,1,0:T(8...) custom-call(bf16[4096,128]{1,0:T(8,128)(2,1)} %bitcast.12, bf16[4096,128]{1,0:T(8,128)(2,1)} %bitcast.13), custom_call_target="tpu_custom_call" | custom-call | flops 33554432 | bytes 2097152 | tf_op jit(solution)/shard_map/key/pallas_call | solution.py:176
  2.8 3.1 %collective-permute-start = (bf16[4,128,128]{2,1,0:T(8,128)(2,1)S(1)}, bf16[4,128,128]{2,1,0:T(8,128)(2,1)S(1)}, u32[]{:S(2)}, u32[]{:S(2)}) collective-permute-start(bf16[4,128,128]{2,1,0:T(8,128)(2,1)S(1)} %get-tuple-element.128), channel_id=1, source_target_pairs={{0,4},{1,5},{4,0},{5,1},{8,9},{9,8},{12,13},{13,12},{2,6},{3,7},{6... | collective-permute-start | bytes 393224 | tf_op jit(solution)/shard_map/ppermute | solution.py:195
  5.9 0.6 %key.5 = (bf16[4,128,128]{2,1,0:T(8,128)(2,1)S(1)}, bf16[4,256,128]{2,1,0:T(8,128)(2,1)S(1)}, bf16[4,256,128]{2,1,0:T(8,128)(2,1)S(1)}, f32[4,256,128]{2,1,0:T(8,128)S(1)}) custom-call(f32[4096,128]{1,0:T(8,128)S(1)} %get-tuple-element.141.refs_0_, f32[4096,128]{1,0:T(8,128)S(1)} %get-tuple-element.130.refs_1_), custom_call_target="tpu_custom_call" | custom-call | flops 33554432 | bytes 4194304 | tf_op jit(solution)/shard_map/key/pallas_call | solution.py:176
  7.4 1.1 %query.4 = (f32[4,256,128]{2,1,0:T(8,128)S(1)}, bf16[4,256,128]{2,1,0:T(8,128)(2,1)S(1)}, bf16[4,256,128]{2,1,0:T(8,128)(2,1)S(1)}, f32[4,256,128]{2,1,0:T(8,128...) custom-call(bf16[4096,128]{1,0:T(8,128)(2,1)S(1)} %bitcast.8, ...), custom_call_target="tpu_custom_call" | custom-call | flops 134217728 | bytes 2621440 | tf_op jit(solution)/shard_map/query/pallas_call | solution.py:176
  8.5 0.6 %key.6 = (bf16[4,128,128]{2,1,0:T(8,128)(2,1)S(1)}, bf16[4,256,128]{2,1,0:T(8,128)(2,1)S(1)}, bf16[4,256,128]{2,1,0:T(8,128)(2,1)S(1)}, f32[4,256,128]{2,1,0:T(8,128)S(1)}) custom-call(f32[4096,128]{1,0:T(8,128)S(1)} %get-tuple-element.141.refs_0_, f32[4096,128]{1,0:T(8,128)S(1)} %get-tuple-element.130.refs_1_), custom_call_target="tpu_custom_call" | custom-call | flops 33554432 | bytes 4194304 | tf_op jit(solution)/shard_map/key/pallas_call | solution.py:176
  9.1 1.2 %collective-permute-start.3 = (bf16[4,128,128]{2,1,0:T(8,128)(2,1)S(1)}, bf16[4,128,128]{2,1,0:T(8,128)(2,1)S(1)}, u32[]{:S(2)}, u32[]{:S(2)}) collective-permute-start(bf16[4,128,128]{2,1,0:T(8,128)(2,1)S(1)} %get-tuple-element.140), channel_id=1, source_target_pairs={{0,4},{1,5},{4,0},{5,1},{8,9},{9,8},{12,13},{13,12},{2,6},{3,7},{6... | collective-permute-start | bytes 393224 | tf_op jit(solution)/shard_map/ppermute | solution.py:195
  10.3 0.6 %key.7 = (bf16[4,128,128]{2,1,0:T(8,128)(2,1)S(1)}, bf16[4,256,128]{2,1,0:T(8,128)(2,1)S(1)}, bf16[4,256,128]{2,1,0:T(8,128)(2,1)S(1)}, f32[4,256,128]{2,1,0:T(8,128)S(1)}) custom-call(f32[4096,128]{1,0:T(8,128)S(1)} %get-tuple-element.141.refs_0_, f32[4096,128]{1,0:T(8,128)S(1)} %get-tuple-element.130.refs_1_), custom_call_target="tpu_custom_call" | custom-call | flops 33554432 | bytes 4194304 | tf_op jit(solution)/shard_map/key/pallas_call | solution.py:176
  11.1 1.4 %collective-permute-start.5 = (bf16[4,128,128]{2,1,0:T(8,128)(2,1)S(1)}, bf16[4,128,128]{2,1,0:T(8,128)(2,1)S(1)}, u32[]{:S(2)}, u32[]{:S(2)}) collective-permute-start(bf16[4,128,128]{2,1,0:T(8,128)(2,1)S(1)} %get-tuple-element.146), channel_id=1, source_target_pairs={{0,4},{1,5},{4,0},{5,1},{8,9},{9,8},{12,13},{13,12},{2,6},{3,7},{6... | collective-permute-start | bytes 393224 | tf_op jit(solution)/shard_map/ppermute | solution.py:195
  12.5 0.8 %query.5 = (f32[4,256,128]{2,1,0:T(8,128)S(1)}, bf16[4,256,128]{2,1,0:T(8,128)(2,1)S(1)}, bf16[4,256,128]{2,1,0:T(8,128)(2,1)S(1)}, f32[4,256,128]{2,1,0:T(8,128)S(1)}, bf16[4,256,256]{2,1,0:T(8,128)(2,1)S(1)}) custom-call(f32[4096,128]{1,0:T(8,128)S(1)} %get-tuple-element.135.refs_0_, f32[4096,128]{1,0:T(8,128)S(1)} %get-tuple-element.136.refs_1_, ...), custom_call_target="tpu_custom_call" | custom-call | flops 134217728 | bytes 4718592 | tf_op jit(solution)/shard_map/query/pallas_call | solution.py:176
  13.5 0.6 %collective-permute-start.7 = (bf16[4,128,128]{2,1,0:T(8,128)(2,1)S(1)}, bf16[4,128,128]{2,1,0:T(8,128)(2,1)S(1)}, u32[]{:S(2)}, u32[]{:S(2)}) collective-permute-start(bf16[4,128,128]{2,1,0:T(8,128)(2,1)S(1)} %fusion.1), channel_id=1, source_target_pairs={{0,1},{1,0},{4,5},{5,4},{8,12},{9,13},{12,8},{13,9},{2,3},{3,2},{6... | collective-permute-start | bytes 393224 | tf_op jit(solution)/shard_map/ppermute | solution.py:195
  14.1 1.7 %collective-permute-done.3.rest_0_ = bf16[4,128,128]{2,1,0:T(8,128)(2,1)S(1)} collective-permute-done((bf16[4,128,128]{2,1,0:T(8,128)(2,1)S(1)}, bf16[4,128,128]{2,1,0:T(8,128)(2,1)S(1)}, u32[]{:S(2)}, u32[]{:S(2)}) %collective-permute-start.3) | collective-permute-done | bytes 131104 | tf_op jit(solution)/shard_map/ppermute | solution.py:195
  15.9 0.8 %query.6 = (f32[4,256,128]{2,1,0:T(8,128)S(1)}, bf16[4,256,128]{2,1,0:T(8,128)(2,1)S(1)}, bf16[4,256,128]{2,1,0:T(8,128)(2,1)S(1)}, f32[4,256,128]{2,1,0:T(8,128)S(1)}, bf16[4,256,256]{2,1,0:T(8,128)(2,1)S(1)}) custom-call(f32[4096,128]{1,0:T(8,128)S(1)} %get-tuple-element.135.refs_0_, f32[4096,128]{1,0:T(8,128)S(1)} %get-tuple-element.136.refs_1_, ...), custom_call_target="tpu_custom_call" | custom-call | flops 134217728 | bytes 4718592 | tf_op jit(solution)/shard_map/query/pallas_call | solution.py:176
  16.8 0.6 %collective-permute-start.8 = (bf16[4,128,128]{2,1,0:T(8,128)(2,1)S(1)}, bf16[4,128,128]{2,1,0:T(8,128)(2,1)S(1)}, u32[]{:S(2)}, u32[]{:S(2)}) collective-permute-start(bf16[4,128,128]{2,1,0:T(8,128)(2,1)S(1)} %fusion.3), channel_id=1, source_target_pairs={{0,1},{1,0},{4,5},{5,4},{8,12},{9,13},{12,8},{13,9},{2,3},{3,2},{6... | collective-permute-start | bytes 393224 | tf_op jit(solution)/shard_map/ppermute | solution.py:195
  18.6 0.9 %norm.4 = (bf16[4,128,128]{2,1,0:T(8,128)(2,1)S(1)}, bf16[4,256,128]{2,1,0:T(8,128)(2,1)S(1)}, bf16[4,128,128]{2,1,0:T(8,128)(2,1)S(1)}, f32[4096,128]{1,0:T(8,128)S(1)}) custom-call(bf16[4,256,128]{2,1,0:T(8,128)(2,1)S(1)} %get-tuple-element.152.fq_ref, bf16[4,256,128]{2,1,0:T(8,128)(2,1)S(1)} %get-tuple-element.153.gh_ref, ...), custom_call_target="tpu_custom_call" | custom-call | flops 67108864 | bytes 1441792 | tf_op jit(solution)/shard_map/norm/pallas_call | solution.py:176
  19.6 0.9 %norm.5 = (bf16[4,128,128]{2,1,0:T(8,128)(2,1)S(1)}, bf16[4,256,128]{2,1,0:T(8,128)(2,1)S(1)}, bf16[4,128,128]{2,1,0:T(8,128)(2,1)S(1)}, f32[4096,128]{1,0:T(8,128)S(1)}) custom-call(bf16[4,256,128]{2,1,0:T(8,128)(2,1)S(1)} %get-tuple-element.149.fq_ref, bf16[4,256,128]{2,1,0:T(8,128)(2,1)S(1)} %get-tuple-element.150.gh_ref, ...), custom_call_target="tpu_custom_call", output_to_operand_aliasing={{3}: (6, {})} | custom-call | flops 67108864 | bytes 3538944 | tf_op jit(solution)/shard_map/norm/pallas_call | solution.py:176
  21.0 0.8 %query.7 = (f32[4,256,128]{2,1,0:T(8,128)S(1)}, bf16[4,256,128]{2,1,0:T(8,128)(2,1)S(1)}, bf16[4,256,128]{2,1,0:T(8,128)(2,1)S(1)}, f32[4,256,128]{2,1,0:T(8,128)S(1)}, bf16[4,256,256]{2,1,0:T(8,128)(2,1)S(1)}) custom-call(f32[4096,128]{1,0:T(8,128)S(1)} %get-tuple-element.135.refs_0_, f32[4096,128]{1,0:T(8,128)S(1)} %get-tuple-element.136.refs_1_, ...), custom_call_target="tpu_custom_call" | custom-call | flops 134217728 | bytes 4718592 | tf_op jit(solution)/shard_map/query/pallas_call | solution.py:176
  21.8 1.4 %back.4 = (f32[4,256,128]{2,1,0:T(8,128)S(1)}, f32[4,256,128]{2,1,0:T(8,128)S(1)}, f32[4096,128]{1,0:T(8,128)S(1)}) custom-call(bf16[4,256,128]{2,1,0:T(8,128)(2,1)S(1)} %get-tuple-element.152.fq_ref, bf16[4,256,128]{2,1,0:T(8,128)(2,1)S(1)} %get-tuple-element.133.refs_2_.fk_ref.refs_0_, bf16[4,256,128]{2,1,0:T(8,128)(2,1)S(1)} %get-tuple-element.134.refs_3_.vh_ref.refs_1_, ...), custom_call_target="tpu_custom_call" | custom-call | flops 301989888 | bytes 2228224 | tf_op jit(solution)/shard_map/back/pallas_call | solution.py:176
  23.3 0.9 %norm.6 = (bf16[4,128,128]{2,1,0:T(8,128)(2,1)S(1)}, bf16[4,256,128]{2,1,0:T(8,128)(2,1)S(1)}, bf16[4,128,128]{2,1,0:T(8,128)(2,1)S(1)}, f32[4096,128]{1,0:T(8,128)S(1)}) custom-call(bf16[4,256,128]{2,1,0:T(8,128)(2,1)S(1)} %get-tuple-element.176.fq_ref, bf16[4,256,128]{2,1,0:T(8,128)(2,1)S(1)} %get-tuple-element.179.gh_ref, ...), custom_call_target="tpu_custom_call", output_to_operand_aliasing={{3}: (6, {})} | custom-call | flops 67108864 | bytes 3538944 | tf_op jit(solution)/shard_map/norm/pallas_call | solution.py:176
  24.9 1.4 %back.5 = (f32[4,256,128]{2,1,0:T(8,128)S(1)}, f32[4,256,128]{2,1,0:T(8,128)S(1)}, f32[4096,128]{1,0:T(8,128)S(1)}) custom-call(bf16[4,256,128]{2,1,0:T(8,128)(2,1)S(1)} %get-tuple-element.176.fq_ref, bf16[4,256,128]{2,1,0:T(8,128)(2,1)S(1)} %get-tuple-element.158.refs_2_.fk_ref.refs_0_, ...), custom_call_target="tpu_custom_call", output_to_operand_aliasing={{2}: (7, {})} | custom-call | flops 301989888 | bytes 4325376 | tf_op jit(solution)/shard_map/back/pallas_call | solution.py:176
  26.9 1.1 %norm.7 = (bf16[4,128,128]{2,1,0:T(8,128)(2,1)S(1)}, bf16[4,256,128]{2,1,0:T(8,128)(2,1)S(1)}, bf16[4,128,128]{2,1,0:T(8,128)(2,1)S(1)}, f32[4096,128]{1,0:T(8,128)S(1)}) custom-call(bf16[4,256,128]{2,1,0:T(8,128)(2,1)S(1)} %get-tuple-element.173.fq_ref, bf16[4,256,128]{2,1,0:T(8,128)(2,1)S(1)} %get-tuple-element.174.gh_ref, ...), custom_call_target="tpu_custom_call", output_to_operand_aliasing={{3}: (6, {})} | custom-call | flops 67108864 | bytes 3538944 | tf_op jit(solution)/shard_map/norm/pallas_call | solution.py:176
  28.1 9.9 %collective-permute-start.20 = (bf16[4,128,128]{2,1,0:T(8,128)(2,1)S(1)}, bf16[4,128,128]{2,1,0:T(8,128)(2,1)S(1)}, u32[]{:S(2)}, u32[]{:S(2)}) collective-permute-start(bf16[4,128,128]{2,1,0:T(8,128)(2,1)S(1)} %fusion.9), channel_id=1, source_target_pairs={{0,4},{1,5},{4,0},{5,1},{8,9},{9,8},{12,13},{13,12},{2,6},{3,7},{6... | collective-permute-start | bytes 393224 | tf_op jit(solution)/shard_map/ppermute | solution.py:195
  38.0 1.4 %back.6 = (f32[4,256,128]{2,1,0:T(8,128)S(1)}, f32[4,256,128]{2,1,0:T(8,128)S(1)}, f32[4096,128]{1,0:T(8,128)S(1)}) custom-call(bf16[4,256,128]{2,1,0:T(8,128)(2,1)S(1)} %get-tuple-element.173.fq_ref, bf16[4,256,128]{2,1,0:T(8,128)(2,1)S(1)} %get-tuple-element.171.refs_2_.fk_ref.refs_0_, ...), custom_call_target="tpu_custom_call", output_to_operand_aliasing={{2}: (7, {})} | custom-call | flops 301989888 | bytes 4325376 | tf_op jit(solution)/shard_map/back/pallas_call | solution.py:176
  39.7 2.4 %collective-permute-start.21 = (bf16[4,128,128]{2,1,0:T(8,128)(2,1)S(1)}, bf16[4,128,128]{2,1,0:T(8,128)(2,1)S(1)}, u32[]{:S(2)}, u32[]{:S(2)}) collective-permute-start(bf16[4,128,128]{2,1,0:T(8,128)(2,1)S(1)} %fusion.11), channel_id=1, source_target_pairs={{0,4},{1,5},{4,0},{5,1},{8,9},{9,8},{12,13},{13,12},{2,6},{3,7},{6... | collective-permute-start | bytes 393224 | tf_op jit(solution)/shard_map/ppermute | solution.py:195
  42.2 1.1 %gather.2 = bf16[4096,128]{1,0:T(8,128)(2,1)} custom-call(f32[4096,128]{1,0:T(8,128)S(1)} %get-tuple-element.213.refs_0_), custom_call_target="tpu_custom_call" | custom-call | flops 134217728 | bytes 2097152 | tf_op jit(solution)/shard_map/gather/pallas_call | solution.py:176
  43.4 2.9 %collective-permute-start.22 = (bf16[4,128,128]{2,1,0:T(8,128)(2,1)S(1)}, bf16[4,128,128]{2,1,0:T(8,128)(2,1)S(1)}, u32[]{:S(2)}, u32[]{:S(2)}) collective-permute-start(bf16[4,128,128]{2,1,0:T(8,128)(2,1)S(1)} %fusion.13), channel_id=1, source_target_pairs={{0,4},{1,5},{4,0},{5,1},{8,9},{9,8},{12,13},{13,12},{2,6},{3,7},{6... | collective-permute-start | bytes 393224 | tf_op jit(solution)/shard_map/ppermute | solution.py:195
  46.3 1.4 %back.7 = (f32[4,256,128]{2,1,0:T(8,128)S(1)}, f32[4,256,128]{2,1,0:T(8,128)S(1)}, f32[4096,128]{1,0:T(8,128)S(1)}) custom-call(bf16[4,256,128]{2,1,0:T(8,128)(2,1)S(1)} %get-tuple-element.149.fq_ref, bf16[4,256,128]{2,1,0:T(8,128)(2,1)S(1)} %get-tuple-element.147.refs_2_.fk_ref.refs_0_, ...), custom_call_target="tpu_custom_call", output_to_operand_aliasing={{2}: (7, {})} | custom-call | flops 301989888 | bytes 4325376 | tf_op jit(solution)/shard_map/back/pallas_call | solution.py:176
  47.7 1.4 %collective-permute-start.23 = (bf16[4,128,128]{2,1,0:T(8,128)(2,1)S(1)}, bf16[4,128,128]{2,1,0:T(8,128)(2,1)S(1)}, u32[]{:S(2)}, u32[]{:S(2)}) collective-permute-start(bf16[4,128,128]{2,1,0:T(8,128)(2,1)S(1)} %fusion.15), channel_id=1, source_target_pairs={{0,4},{1,5},{4,0},{5,1},{8,9},{9,8},{12,13},{13,12},{2,6},{3,7},{6... | collective-permute-start | bytes 393224 | tf_op jit(solution)/shard_map/ppermute | solution.py:195
  49.1 1.1 %gather.3 = bf16[4096,128]{1,0:T(8,128)(2,1)} custom-call(f32[4096,128]{1,0:T(8,128)S(1)} %get-tuple-element.225.refs_0_), custom_call_target="tpu_custom_call" | custom-call | flops 134217728 | bytes 2097152 | tf_op jit(solution)/shard_map/gather/pallas_call | solution.py:176
  50.2 0.7 %later.3 = (f32[4096,128]{1,0:T(8,128)S(1)}, f32[4096,128]{1,0:T(8,128)S(1)}) custom-call(bf16[4,256,128]{2,1,0:T(8,128)(2,1)S(1)} %get-tuple-element.133.refs_2_.fk_ref.refs_0_, bf16[4,256,128]{2,1,0:T(8,128)(2,1)S(1)} %get-tuple-element.134.refs_3_.vh_ref.refs_1_, f32[4,256,128]{2,1,0:T(8,128)S(1)} %get-tuple-element.232.refs_2_, ...), custom_call_target="tpu_custom_call" | custom-call | flops 67108864 | bytes 2490368 | tf_op jit(solution)/shard_map/later/pallas_call | solution.py:176
  50.9 0.7 %later.4 = (f32[4096,128]{1,0:T(8,128)S(1)}, f32[4096,128]{1,0:T(8,128)S(1)}) custom-call(bf16[4,256,128]{2,1,0:T(8,128)(2,1)S(1)} %get-tuple-element.147.refs_2_.fk_ref.refs_0_, bf16[4,256,128]{2,1,0:T(8,128)(2,1)S(1)} %get-tuple-element.148.refs_3_.vh_ref.refs_1_, ...), custom_call_target="tpu_custom_call", output_to_operand_aliasing={{0}: (8, {}), {1}: (9, {})} | custom-call | flops 67108864 | bytes 6684672 | tf_op jit(solution)/shard_map/later/pallas_call | solution.py:176
  51.6 0.7 %later.5 = (f32[4096,128]{1,0:T(8,128)S(1)}, f32[4096,128]{1,0:T(8,128)S(1)}) custom-call(bf16[4,256,128]{2,1,0:T(8,128)(2,1)S(1)} %get-tuple-element.158.refs_2_.fk_ref.refs_0_, bf16[4,256,128]{2,1,0:T(8,128)(2,1)S(1)} %get-tuple-element.159.refs_3_.vh_ref.refs_1_, ...), custom_call_target="tpu_custom_call", output_to_operand_aliasing={{0}: (8, {}), {1}: (9, {})} | custom-call | flops 67108864 | bytes 6684672 | tf_op jit(solution)/shard_map/later/pallas_call | solution.py:176
  52.8 2.0 %last.1 = (bf16[4096,128]{1,0:T(8,128)(2,1)}, bf16[4096,128]{1,0:T(8,128)(2,1)}) custom-call(bf16[4,256,128]{2,1,0:T(8,128)(2,1)S(1)} %get-tuple-element.171.refs_2_.fk_ref.refs_0_, bf16[4,256,128]{2,1,0:T(8,128)(2,1)S(1)} %get-tuple-element.172.refs_3_.vh_ref.refs_1_, f32[4,256,128]{2,1,0:T(8,128)S(1)} %get-tuple-element.226.refs_2_, ...), custom_call_target="tpu_custom_call" | custom-call | flops 67108864 | bytes 6684672 | tf_op jit(solution)/shard_map/last/pallas_call | solution.py:176
  (58 shorter events, 5.8 us)
Async XLA Ops:
  2.8 8.1 %collective-permute-start = (bf16[4,128,128]{2,1,0:T(8,128)(2,1)S(1)}, bf16[4,128,128]{2,1,0:T(8,128)(2,1)S(1)}, u32[]{:S(2)}, u32[]{:S(2)}) collective-permute-start(bf16[4,128,128]{2,1,0:T(8,128)(2,1)S(1)} %get-tuple-element.128), channel_id=1, source_target_pairs={{0,4},{1,5},{4,0},{5,1},{8,9},{9,8},{12,13},{13,12},{2,6},{3,7},{6... | collective-permute-start | bytes 393224 | tf_op jit(solution)/shard_map/ppermute | solution.py:195
  5.9 1.2 %copy-start = (bf16[1,256,16,128]{3,2,1,0:T(8,128)(2,1)S(1)}, bf16[1,256,16,128]{3,2,1,0:T(8,128)(2,1)}, u32[]{:S(2)}) copy-start(bf16[1,256,16,128]{3,2,1,0:T(8,128)(2,1)} %param.4) | copy-start | bytes 3145732
  5.9 1.5 %copy-start.1 = (bf16[1,256,16,128]{3,2,1,0:T(8,128)(2,1)S(1)}, bf16[1,256,16,128]{3,2,1,0:T(8,128)(2,1)}, u32[]{:S(2)}) copy-start(bf16[1,256,16,128]{3,2,1,0:T(8,128)(2,1)} %param.7) | copy-start | bytes 3145732
  6.5 6.8 %collective-permute-start.1 = (bf16[4,128,128]{2,1,0:T(8,128)(2,1)S(1)}, bf16[4,128,128]{2,1,0:T(8,128)(2,1)S(1)}, u32[]{:S(2)}, u32[]{:S(2)}) collective-permute-start(bf16[4,128,128]{2,1,0:T(8,128)(2,1)S(1)} %get-tuple-element.132), channel_id=1, source_target_pairs={{0,4},{1,5},{4,0},{5,1},{8,9},{9,8},{12,13},{13,12},{2,6},{3,7},{6... | collective-permute-start | bytes 393224 | tf_op jit(solution)/shard_map/ppermute | solution.py:195
  9.1 6.7 %collective-permute-start.3 = (bf16[4,128,128]{2,1,0:T(8,128)(2,1)S(1)}, bf16[4,128,128]{2,1,0:T(8,128)(2,1)S(1)}, u32[]{:S(2)}, u32[]{:S(2)}) collective-permute-start(bf16[4,128,128]{2,1,0:T(8,128)(2,1)S(1)} %get-tuple-element.140), channel_id=1, source_target_pairs={{0,4},{1,5},{4,0},{5,1},{8,9},{9,8},{12,13},{13,12},{2,6},{3,7},{6... | collective-permute-start | bytes 393224 | tf_op jit(solution)/shard_map/ppermute | solution.py:195
  11.0 2.5 %collective-permute-start.2 = (bf16[4,128,128]{2,1,0:T(8,128)(2,1)S(1)}, bf16[4,128,128]{2,1,0:T(8,128)(2,1)S(1)}, u32[]{:S(2)}, u32[]{:S(2)}) collective-permute-start(bf16[4,128,128]{2,1,0:T(8,128)(2,1)S(1)} %fusion), channel_id=1, source_target_pairs={{0,1},{1,0},{4,8},{5,9},{8,4},{9,5},{12,13},{13,12},{2,3},{3,2},{6... | collective-permute-start | bytes 393224 | tf_op jit(solution)/shard_map/ppermute | solution.py:195
  11.1 6.8 %collective-permute-start.5 = (bf16[4,128,128]{2,1,0:T(8,128)(2,1)S(1)}, bf16[4,128,128]{2,1,0:T(8,128)(2,1)S(1)}, u32[]{:S(2)}, u32[]{:S(2)}) collective-permute-start(bf16[4,128,128]{2,1,0:T(8,128)(2,1)S(1)} %get-tuple-element.146), channel_id=1, source_target_pairs={{0,4},{1,5},{4,0},{5,1},{8,9},{9,8},{12,13},{13,12},{2,6},{3,7},{6... | collective-permute-start | bytes 393224 | tf_op jit(solution)/shard_map/ppermute | solution.py:195
  13.4 3.4 %collective-permute-start.4 = (bf16[4,128,128]{2,1,0:T(8,128)(2,1)S(1)}, bf16[4,128,128]{2,1,0:T(8,128)(2,1)S(1)}, u32[]{:S(2)}, u32[]{:S(2)}) collective-permute-start(bf16[4,128,128]{2,1,0:T(8,128)(2,1)S(1)} %fusion.2), channel_id=1, source_target_pairs={{0,1},{1,0},{4,8},{5,9},{8,4},{9,5},{12,13},{13,12},{2,3},{3,2},{6... | collective-permute-start | bytes 393224 | tf_op jit(solution)/shard_map/ppermute | solution.py:195
  13.5 5.1 %collective-permute-start.7 = (bf16[4,128,128]{2,1,0:T(8,128)(2,1)S(1)}, bf16[4,128,128]{2,1,0:T(8,128)(2,1)S(1)}, u32[]{:S(2)}, u32[]{:S(2)}) collective-permute-start(bf16[4,128,128]{2,1,0:T(8,128)(2,1)S(1)} %fusion.1), channel_id=1, source_target_pairs={{0,1},{1,0},{4,5},{5,4},{8,12},{9,13},{12,8},{13,9},{2,3},{3,2},{6... | collective-permute-start | bytes 393224 | tf_op jit(solution)/shard_map/ppermute | solution.py:195
  15.8 2.1 %collective-permute-start.6 = (bf16[4,128,128]{2,1,0:T(8,128)(2,1)S(1)}, bf16[4,128,128]{2,1,0:T(8,128)(2,1)S(1)}, u32[]{:S(2)}, u32[]{:S(2)}) collective-permute-start(bf16[4,128,128]{2,1,0:T(8,128)(2,1)S(1)} %fusion.4), channel_id=1, source_target_pairs={{0,1},{1,0},{4,8},{5,9},{8,4},{9,5},{12,13},{13,12},{2,3},{3,2},{6... | collective-permute-start | bytes 393224 | tf_op jit(solution)/shard_map/ppermute | solution.py:195
  16.8 2.7 %collective-permute-start.8 = (bf16[4,128,128]{2,1,0:T(8,128)(2,1)S(1)}, bf16[4,128,128]{2,1,0:T(8,128)(2,1)S(1)}, u32[]{:S(2)}, u32[]{:S(2)}) collective-permute-start(bf16[4,128,128]{2,1,0:T(8,128)(2,1)S(1)} %fusion.3), channel_id=1, source_target_pairs={{0,1},{1,0},{4,5},{5,4},{8,12},{9,13},{12,8},{13,9},{2,3},{3,2},{6... | collective-permute-start | bytes 393224 | tf_op jit(solution)/shard_map/ppermute | solution.py:195
  17.9 5.3 %collective-permute-start.9 = (bf16[4,128,128]{2,1,0:T(8,128)(2,1)S(1)}, bf16[4,128,128]{2,1,0:T(8,128)(2,1)S(1)}, u32[]{:S(2)}, u32[]{:S(2)}) collective-permute-start(bf16[4,128,128]{2,1,0:T(8,128)(2,1)S(1)} %fusion.6), channel_id=1, source_target_pairs={{0,1},{1,0},{4,8},{5,9},{8,4},{9,5},{12,13},{13,12},{2,3},{3,2},{6... | collective-permute-start | bytes 393224 | tf_op jit(solution)/shard_map/ppermute | solution.py:195
  18.0 5.3 %collective-permute-start.10 = (bf16[4,128,128]{2,1,0:T(8,128)(2,1)S(1)}, bf16[4,128,128]{2,1,0:T(8,128)(2,1)S(1)}, u32[]{:S(2)}, u32[]{:S(2)}) collective-permute-start(bf16[4,128,128]{2,1,0:T(8,128)(2,1)S(1)} %fusion.5), channel_id=1, source_target_pairs={{0,1},{1,0},{4,5},{5,4},{8,12},{9,13},{12,8},{13,9},{2,3},{3,2},{6... | collective-permute-start | bytes 393224 | tf_op jit(solution)/shard_map/ppermute | solution.py:195
  19.5 4.8 %collective-permute-start.11 = (bf16[4,128,128]{2,1,0:T(8,128)(2,1)S(1)}, bf16[4,128,128]{2,1,0:T(8,128)(2,1)S(1)}, u32[]{:S(2)}, u32[]{:S(2)}) collective-permute-start(bf16[4,128,128]{2,1,0:T(8,128)(2,1)S(1)} %get-tuple-element.166), channel_id=1, source_target_pairs={{0,1},{1,0},{4,5},{5,4},{8,12},{9,13},{12,8},{13,9},{2,3},{3,2},{6... | collective-permute-start | bytes 393224 | tf_op jit(solution)/shard_map/ppermute | solution.py:195
  20.4 5.9 %collective-permute-start.12 = (bf16[4,128,128]{2,1,0:T(8,128)(2,1)S(1)}, bf16[4,128,128]{2,1,0:T(8,128)(2,1)S(1)}, u32[]{:S(2)}, u32[]{:S(2)}) collective-permute-start(bf16[4,128,128]{2,1,0:T(8,128)(2,1)S(1)} %get-tuple-element.170), channel_id=1, source_target_pairs={{0,1},{1,0},{4,5},{5,4},{8,12},{9,13},{12,8},{13,9},{2,3},{3,2},{6... | collective-permute-start | bytes 393224 | tf_op jit(solution)/shard_map/ppermute | solution.py:195
  23.3 3.6 %collective-permute-start.13 = (bf16[4,128,128]{2,1,0:T(8,128)(2,1)S(1)}, bf16[4,128,128]{2,1,0:T(8,128)(2,1)S(1)}, u32[]{:S(2)}, u32[]{:S(2)}) collective-permute-start(bf16[4,128,128]{2,1,0:T(8,128)(2,1)S(1)} %fusion.7), channel_id=1, source_target_pairs={{0,1},{1,0},{4,5},{5,4},{8,12},{9,13},{12,8},{13,9},{2,3},{3,2},{6... | collective-permute-start | bytes 393224 | tf_op jit(solution)/shard_map/ppermute | solution.py:195
  24.3 3.8 %collective-permute-start.14 = (bf16[4,128,128]{2,1,0:T(8,128)(2,1)S(1)}, bf16[4,128,128]{2,1,0:T(8,128)(2,1)S(1)}, u32[]{:S(2)}, u32[]{:S(2)}) collective-permute-start(bf16[4,128,128]{2,1,0:T(8,128)(2,1)S(1)} %fusion.8), channel_id=1, source_target_pairs={{0,1},{1,0},{4,8},{5,9},{8,4},{9,5},{12,13},{13,12},{2,3},{3,2},{6... | collective-permute-start | bytes 393224 | tf_op jit(solution)/shard_map/ppermute | solution.py:195
  26.2 13.2 %collective-permute-start.15 = (bf16[4,128,128]{2,1,0:T(8,128)(2,1)S(1)}, bf16[4,128,128]{2,1,0:T(8,128)(2,1)S(1)}, u32[]{:S(2)}, u32[]{:S(2)}) collective-permute-start(bf16[4,128,128]{2,1,0:T(8,128)(2,1)S(1)} %get-tuple-element.196), channel_id=1, source_target_pairs={{0,1},{1,0},{4,5},{5,4},{8,12},{9,13},{12,8},{13,9},{2,3},{3,2},{6... | collective-permute-start | bytes 393224 | tf_op jit(solution)/shard_map/ppermute | solution.py:195
  26.3 13.4 %collective-permute-start.16 = (bf16[4,128,128]{2,1,0:T(8,128)(2,1)S(1)}, bf16[4,128,128]{2,1,0:T(8,128)(2,1)S(1)}, u32[]{:S(2)}, u32[]{:S(2)}) collective-permute-start(bf16[4,128,128]{2,1,0:T(8,128)(2,1)S(1)} %fusion.10), channel_id=1, source_target_pairs={{0,1},{1,0},{4,8},{5,9},{8,4},{9,5},{12,13},{13,12},{2,3},{3,2},{6... | collective-permute-start | bytes 393224 | tf_op jit(solution)/shard_map/ppermute | solution.py:195
  28.0 15.3 %collective-permute-start.17 = (bf16[4,128,128]{2,1,0:T(8,128)(2,1)S(1)}, bf16[4,128,128]{2,1,0:T(8,128)(2,1)S(1)}, u32[]{:S(2)}, u32[]{:S(2)}) collective-permute-start(bf16[4,128,128]{2,1,0:T(8,128)(2,1)S(1)} %get-tuple-element.206), channel_id=1, source_target_pairs={{0,1},{1,0},{4,5},{5,4},{8,12},{9,13},{12,8},{13,9},{2,3},{3,2},{6... | collective-permute-start | bytes 393224 | tf_op jit(solution)/shard_map/ppermute | solution.py:195
  28.1 22.1 %collective-permute-start.20 = (bf16[4,128,128]{2,1,0:T(8,128)(2,1)S(1)}, bf16[4,128,128]{2,1,0:T(8,128)(2,1)S(1)}, u32[]{:S(2)}, u32[]{:S(2)}) collective-permute-start(bf16[4,128,128]{2,1,0:T(8,128)(2,1)S(1)} %fusion.9), channel_id=1, source_target_pairs={{0,4},{1,5},{4,0},{5,1},{8,9},{9,8},{12,13},{13,12},{2,6},{3,7},{6... | collective-permute-start | bytes 393224 | tf_op jit(solution)/shard_map/ppermute | solution.py:195
  39.4 3.9 %collective-permute-start.18 = (bf16[4,128,128]{2,1,0:T(8,128)(2,1)S(1)}, bf16[4,128,128]{2,1,0:T(8,128)(2,1)S(1)}, u32[]{:S(2)}, u32[]{:S(2)}) collective-permute-start(bf16[4,128,128]{2,1,0:T(8,128)(2,1)S(1)} %fusion.12), channel_id=1, source_target_pairs={{0,1},{1,0},{4,8},{5,9},{8,4},{9,5},{12,13},{13,12},{2,3},{3,2},{6... | collective-permute-start | bytes 393224 | tf_op jit(solution)/shard_map/ppermute | solution.py:195
  39.7 11.2 %collective-permute-start.21 = (bf16[4,128,128]{2,1,0:T(8,128)(2,1)S(1)}, bf16[4,128,128]{2,1,0:T(8,128)(2,1)S(1)}, u32[]{:S(2)}, u32[]{:S(2)}) collective-permute-start(bf16[4,128,128]{2,1,0:T(8,128)(2,1)S(1)} %fusion.11), channel_id=1, source_target_pairs={{0,4},{1,5},{4,0},{5,1},{8,9},{9,8},{12,13},{13,12},{2,6},{3,7},{6... | collective-permute-start | bytes 393224 | tf_op jit(solution)/shard_map/ppermute | solution.py:195
  43.3 4.4 %collective-permute-start.19 = (bf16[4,128,128]{2,1,0:T(8,128)(2,1)S(1)}, bf16[4,128,128]{2,1,0:T(8,128)(2,1)S(1)}, u32[]{:S(2)}, u32[]{:S(2)}) collective-permute-start(bf16[4,128,128]{2,1,0:T(8,128)(2,1)S(1)} %fusion.14), channel_id=1, source_target_pairs={{0,1},{1,0},{4,8},{5,9},{8,4},{9,5},{12,13},{13,12},{2,3},{3,2},{6... | collective-permute-start | bytes 393224 | tf_op jit(solution)/shard_map/ppermute | solution.py:195
  43.4 8.2 %collective-permute-start.22 = (bf16[4,128,128]{2,1,0:T(8,128)(2,1)S(1)}, bf16[4,128,128]{2,1,0:T(8,128)(2,1)S(1)}, u32[]{:S(2)}, u32[]{:S(2)}) collective-permute-start(bf16[4,128,128]{2,1,0:T(8,128)(2,1)S(1)} %fusion.13), channel_id=1, source_target_pairs={{0,4},{1,5},{4,0},{5,1},{8,9},{9,8},{12,13},{13,12},{2,6},{3,7},{6... | collective-permute-start | bytes 393224 | tf_op jit(solution)/shard_map/ppermute | solution.py:195
  47.7 5.1 %collective-permute-start.23 = (bf16[4,128,128]{2,1,0:T(8,128)(2,1)S(1)}, bf16[4,128,128]{2,1,0:T(8,128)(2,1)S(1)}, u32[]{:S(2)}, u32[]{:S(2)}) collective-permute-start(bf16[4,128,128]{2,1,0:T(8,128)(2,1)S(1)} %fusion.15), channel_id=1, source_target_pairs={{0,4},{1,5},{4,0},{5,1},{8,9},{9,8},{12,13},{13,12},{2,6},{3,7},{6... | collective-permute-start | bytes 393224 | tf_op jit(solution)/shard_map/ppermute | solution.py:195

commit v4 on v3

--- a/solution.py
+++ b/solution.py
@@ -9,9 +9,16 @@
 
 BF, F32 = jnp.bfloat16, jnp.float32
 MIB = 1 << 20
+SCOPED = 12 * MIB
 SIZES = [4, 4, 4, 4]
 UNROLL = 4
 BLOCKS = 4
+ORDER = [
+    "k0", "u0", "k1", "k3", "u1", "q0", "k2", "u2", "u0", "u3", "u1", "q3", "u0", "u2",
+    "q1", "u1", "u3", "n0", "x20", "b0", "n1", "x31", "q2", "d0", "n2", "d2", "d1", "n3",
+    "d3", "d0", "d2", "d1", "g0", "d3", "d2", "b3", "b1", "d3", "b2", "g1", "l1", "l0",
+    "l2", "l3",
+]
 
 
 def dot(a, b, ca, cb):
@@ -38,16 +45,18 @@
     return [pl.ds(at, size) for at in range(0, rows, size)]
 
 
-def fetch(sources, landings, wides, sems):
+def fetch(src, landing, sems):
     copies = []
-    for src, dst, wide in zip(sources, landings, wides):
-        for rows in blocks_of(src.shape[0]):
-            copy = pltpu.make_async_copy(src.at[rows], dst.at[rows], sems.at[len(copies)])
-            copy.start()
-            copies.append((copy, dst, wide, rows))
-    for copy, dst, wide, rows in copies:
+    for rows in blocks_of(src.shape[0]):
+        copies.append((pltpu.make_async_copy(src.at[rows], landing.at[rows], sems.at[len(copies)]), rows))
+        copies[-1][0].start()
+    return copies
+
+
+def land(copies, landing, wide):
+    for copy, rows in copies:
         copy.wait()
-        wide[rows, :] = dst[rows, :].astype(F32)
+        wide[rows, :] = landing[rows, :].astype(F32)
 
 
 def flush(wides, stages, results, sems):
@@ -63,8 +72,10 @@
 
 def key_kernel(base, size, heads, t, first, *refs):
     if first:
-        k_ref, v_ref, state_ref, fk_ref, vh_ref, slope_ref, k32, v32, k16, v16, sems = refs
-        fetch((k_ref, v_ref), (k16, v16), (k32, v32), sems)
+        k_ref, v_ref, state_ref, fk_ref, vh_ref, slope_ref, k32, v32, k16, v16, k_sems, v_sems = refs
+        k_copies, v_copies = fetch(k_ref, k16, k_sems), fetch(v_ref, v16, v_sems)
+        land(k_copies, k16, k32)
+        land(v_copies, v16, v32)
     else:
         k32, v32, state_ref, fk_ref, vh_ref, slope_ref = refs
 
@@ -103,8 +114,8 @@
     lax.fori_loop(0, size, one, 0, unroll=UNROLL)
 
 
-def norm_kernel(base, size, heads, t, parts, fq_ref, gh_ref, raw_ref, *rest):
-    got, (grad_ref, grad_raw_ref, earlier_ref, wide_ref) = rest[:parts], rest[-4:]
+def norm_kernel(base, size, heads, t, chain, fq_ref, gh_ref, raw_ref, *rest):
+    got, (grad_ref, grad_raw_ref, earlier_ref, wide_ref) = rest[: chain.hops], rest[-4:]
 
     def one(i, carry):
         earlier = pick(lax.axis_index("ctx"), got, i)
@@ -144,12 +155,11 @@
     flush(refs[:count], refs[2 * count : 3 * count], refs[count : 2 * count], refs[-1])
 
 
-def later_step(base, size, heads, t, parts, refs, wide_k, wide_v):
-    fk_ref, vh_ref, slope_ref, gk, gv = refs[:5]
-    got = refs[5 : 5 + parts]
+def later_kernel(base, size, heads, t, chain, fk_ref, vh_ref, slope_ref, gk, gv, *rest):
+    got, (wide_k, wide_v) = rest[: chain.hops], rest[-2:]
 
     def one(i, carry):
-        later = pick(parts - lax.axis_index("ctx"), got, i)
+        later = pick(chain.n - 1 - lax.axis_index("ctx"), got, i)
         gfk = gk[i] + dot(vh_ref[i], later, 1, 1)
         wide_k[pl.ds(base + i, t, stride=heads), :] = gfk * slope_ref[i]
         wide_v[pl.ds(base + i, t, stride=heads), :] = gv[i] + dot(fk_ref[i], later, 1, 0)
@@ -158,17 +168,32 @@
     lax.fori_loop(0, size, one, 0, unroll=UNROLL)
 
 
-def later_kernel(base, size, heads, t, parts, *refs):
-    later_step(base, size, heads, t, parts, refs, *refs[-2:])
-
-
-def last_kernel(base, size, heads, t, parts, *refs):
+def last_kernel(base, size, heads, t, chain, *refs):
+    fk_ref, vh_ref, slope_ref, gk, gv = refs[:5]
+    got = refs[5 : 5 + chain.hops]
     if base:
-        wide_k, wide_v, k_out, v_out, k16, v16, sems = refs[5 + parts :]
+        wide_k, wide_v, k_out, v_out, k16, v16, sems, later_ref = refs[5 + chain.hops :]
     else:
-        k_out, v_out, k16, v16, sems, wide_k, wide_v = refs[5 + parts :]
-    later_step(base, size, heads, t, parts, refs, wide_k, wide_v)
-    flush((wide_k, wide_v), (k16, v16), (k_out, v_out), sems)
+        k_out, v_out, k16, v16, sems, later_ref, wide_k, wide_v = refs[5 + chain.hops :]
+    for i in range(size):
+        later_ref[i] = pick(chain.n - 1 - lax.axis_index("ctx"), got, i)
+    copies = []
+    count = t // BLOCKS
+    for at in range(0, t, count):
+        here = pl.ds(at, count)
+        rows = pl.ds(at * heads, count * heads)
+        for wide, stage, dst in ((wide_v, v16, v_out), (wide_k, k16, k_out)):
+            for i in range(size):
+                if wide is wide_v:
+                    value = gv[i, here] + dot(fk_ref[i, here], later_ref[i], 1, 0)
+                else:
+                    value = (gk[i, here] + dot(vh_ref[i, here], later_ref[i], 1, 1)) * slope_ref[i, here]
+                wide[pl.ds(at * heads + base + i, count, stride=heads), :] = value
+            stage[rows, :] = wide[rows, :].astype(BF)
+            copies.append(pltpu.make_async_copy(stage.at[rows], dst.at[rows], sems.at[len(copies)]))
+            copies[-1].start()
+    for copy in copies:
+        copy.wait()
 
 
 def call(body, outs, scratch, args, flops, name, specs, out_specs, aliases):
@@ -180,7 +205,7 @@
         out_specs=out_specs,
         scratch_shapes=scratch,
         input_output_aliases=aliases,
-        compiler_params=pltpu.CompilerParams(vmem_limit_bytes=28 * MIB),
+        compiler_params=pltpu.CompilerParams(vmem_limit_bytes=SCOPED),
         cost_estimate=pl.CostEstimate(flops=flops, bytes_accessed=moved, transcendentals=0),
         name=name,
     )(*args)
@@ -221,43 +246,59 @@
     def __init__(self, order, part, n, cores, reverse):
         self.order, self.part, self.n, self.cores, self.reverse = order, part, n, cores, reverse
         self.got = []
+        self.hops = n - 1
+
+    def carried(self):
+        if not self.got:
+            return self.order.tie(self.part)
+        return (self.part.astype(F32) + self.order.tie(self.got[-1]).astype(F32)).astype(BF)
 
     def hop(self):
+        running = self.carried()
+        self.order.before.append(running)
         h = len(self.got)
-        if h:
-            running = (self.part.astype(F32) + self.order.tie(self.got[-1]).astype(F32)).astype(BF)
-        else:
-            running = self.order.tie(self.part)
-        self.order.before.append(running)
         self.got.append(swap(running, self.n - 2 - h if self.reverse else h, self.n, self.cores))
 
 
+def merge_kernel(n, part_ref, got_ref, other_ref, out_ref):
+    total = (part_ref[...].astype(F32) + got_ref[...].astype(F32)).astype(BF)
+    out_ref[...] = jnp.where(lax.axis_index("ctx") == n - 1, other_ref[...], total)
+
+
+def join(up, down):
+    if up.part.shape != down.part.shape or not up.got:
+        up.hop()
+        down.hop()
+        return
+    running, = up.order.compute(
+        functools.partial(merge_kernel, up.n), [jax.ShapeDtypeStruct(up.part.shape, BF)], [],
+        (up.part, up.got[-1], down.part), 1, 3 * up.part.size, "merge",
+    )
+    received = swap(running, up.n - 2, up.n, up.cores)
+    up.got.append(received)
+    down.got.append(received)
+
+
 def pick(place, got, i):
-    total = jnp.zeros(got[0].shape[1:], got[0].dtype)
+    total = jnp.zeros(got[0].shape[1:], BF)
     for hop, part in enumerate(got):
         total = jnp.where(place == hop + 1, part[i], total)
     return total
 
 
-ORDER = [
-    "k0", "u0", "k1", "u1", "q0", "k2", "u2", "k3", "u0", "u3", "q1", "u1", "u0", "u2",
-    "q2", "u1", "u3", "u2", "n0", "d0", "n1", "d1", "q3", "b0", "u3", "n2", "d0", "b2",
-    "d2", "d1", "n3", "d3", "d0", "b3", "d2", "d1", "g0", "d3", "d2", "b1", "d3", "g1",
-    "l0", "l1", "l2", "l3",
-]
-
-
 def plan(hops):
-    left = {step: ORDER.count(step) for step in ORDER}
+    joined = {name for step in ORDER if step[0] == "x" for name in ("u" + step[1], "d" + step[2])}
+    done = dict.fromkeys(ORDER, 0)
     for step in ORDER:
-        left[step] -= 1
+        done[step] += 1
         if step[0] not in "ud":
             yield step
             continue
-        listed = ORDER.count(step)
-        done = listed - left[step]
-        if done <= hops:
-            yield from [step] * (hops - listed + 1 if left[step] == 0 and hops > listed else 1)
+        wanted = hops - (step in joined)
+        if done[step] == ORDER.count(step):
+            yield from [step] * (wanted - done[step] + 1)
+        elif done[step] <= wanted:
+            yield step
 
 
 def shards(n, cores, query_in, key_in, value_in, grad_out):
@@ -286,7 +327,7 @@
         body = functools.partial(key_kernel, bases[c], sizes[c], heads, t, c == 0)
         if c == 0:
             state, *held["key", c], held["k32"], held["v32"] = order.compute(
-                body, outs + [broad] * 2, [flat16, flat16, sems], (k, v), 0, sizes[c] * mm, "key", far_in=(0, 1)
+                body, outs + [broad] * 2, [flat16, flat16, sems, sems], (k, v), 0, sizes[c] * mm, "key", far_in=(0, 1)
             )
         else:
             state, *held["key", c] = order.compute(
@@ -318,7 +359,7 @@
         state = S((s, d, d), BF)
         args, outs, aliases = onto((fq, gh, raw, *up[c].got), [state, S((s, t, d), BF), state], ["normed"])
         grad, grad_raw, earlier, held["normed"] = order.compute(
-            functools.partial(norm_kernel, bases[c], s, heads, t, n - 1),
+            functools.partial(norm_kernel, bases[c], s, heads, t, up[c]),
             outs, [], args, 3, s * mm * 2, "norm", aliases=aliases,
         )
         held[c] = grad_raw, earlier
@@ -348,22 +389,23 @@
         if c < m - 1:
             args, outs, aliases = onto(args, [], ["gk", "gv"])
             held["gk"], held["gv"] = order.compute(
-                functools.partial(later_kernel, bases[c], s, heads, t, n - 1),
+                functools.partial(later_kernel, bases[c], s, heads, t, down[c]),
                 outs, [], args, 5, s * mm * 2, "later", aliases=aliases,
             )
         else:
             wides = [held["gk"], held["gv"]] if m > 1 else []
             held["last"] = order.compute(
-                functools.partial(last_kernel, bases[c], s, heads, t, n - 1),
-                [flat, flat], [flat16, flat16, sems] + ([] if wides else [wide, wide]),
+                functools.partial(last_kernel, bases[c], s, heads, t, down[c]),
+                [flat, flat], [flat16, flat16, sems, pltpu.VMEM((s, d, d), BF)] + ([] if wides else [wide, wide]),
                 (*args, *wides), 5, s * mm * 2, "last", far_out=(0, 1),
             )
 
     steps = dict(
-        u=lambda c: up[c].hop(), d=lambda c: down[c].hop(), k=key, q=query, n=norm, b=back, g=gather, l=later
+        u=lambda c: up[c].hop(), d=lambda c: down[c].hop(), x=lambda c, e: join(up[c], down[e]),
+        k=key, q=query, n=norm, b=back, g=gather, l=later,
     )
     for step in plan(n - 1):
-        steps[step[0]](*map(int, step[1:].split(".") if step[1:] else ()))
+        steps[step[0]](*map(int, step[1:]))
     output, grad_query = held["out", 0], held["out", 1]
     grad_key, grad_value = held["last"]
     return tuple(a.reshape(1, t, heads, d) for a in (output, grad_query, grad_key, grad_value))

time: 55.2 us -> 51.3 us (0.929)
  starting transfers between devices: 26.7 us -> 23.6 us
    ppermute x24 -> x22, starting transfers between devices: 26.7 us -> 23.6 us  [swap(): return lax.ppermute(x, ('ctx', 'rep'), pairs)]
    ppermute x24 -> x22, waiting for transfers between devices: 2.77 us -> 2.25 us  [swap(): return lax.ppermute(x, ('ctx', 'rep'), pairs)]
    pallas_call x22 -> x24, Pallas kernels: 22.8 us -> 22.7 us  [call(): pl.pallas_call(body, out_shape=outs, in_specs=specs, out_specs=out_specs,...]
  transfers between devices with their start and end apart: 24 -> 22, of which waited for: 3 -> 2; matrix products, arithmetic and copies ran while one was open for 1% -> 1% of each run, Pallas kernels for 34% -> 36%
where the time goes in v4:
time: 51.3 us; the launch traced here: 51.1 us
  starting transfers between devices  23.6 us (46%)
  Pallas kernels  22.7 us (44%)
  waiting for transfers between devices  2.25 us (4%)
  between operations  1.22 us (2%)
  local copies, waits for them, and re-layouts  0.85 us (2%)
  other arithmetic  0.54 us (1%)
    ppermute x22, starting transfers between devices, swap(): return lax.ppermute(x, ('ctx', 'rep'), pairs)  23.6 us
    pallas_call x24, Pallas kernels, call(): pl.pallas_call(body, out_shape=outs, in_specs=specs, out_specs=out_specs,...  22.7 us
    ppermute x22, waiting for transfers between devices, swap(): return lax.ppermute(x, ('ctx', 'rep'), pairs)  2.25 us
  transfers between devices with their start and end apart: 22, of which 2 were waited for; matrix products, arithmetic and copies ran while one was open for 1% of the time, Pallas kernels for 36%

profile of v4, /device:TPU:0, one launch (start us, length us, event | category | flops | bytes accessed | tf_op | source)
XLA Modules:
  0.0 51.1 jit_solution(10811087309601699401)
XLA Ops:
  0.6 2.3 %key.4 = (bf16[4,128,128]{2,1,0:T(8,128)(2,1)S(1)}, bf16[4,256,128]{2,1,0:T(8,128)(2,1)S(1)}, bf16[4,256,128]{2,1,0:T(8,128)(2,1)S(1)}, f32[4,256,128]{2,1,0:T(8...) custom-call(bf16[4096,128]{1,0:T(8,128)(2,1)} %bitcast.12, bf16[4096,128]{1,0:T(8,128)(2,1)} %bitcast.13), custom_call_target="tpu_custom_call" | custom-call | flops 33554432 | bytes 2097152 | tf_op jit(solution)/shard_map/key/pallas_call | solution.py:201
  3.0 3.1 %collective-permute-start = (bf16[4,128,128]{2,1,0:T(8,128)(2,1)S(1)}, bf16[4,128,128]{2,1,0:T(8,128)(2,1)S(1)}, u32[]{:S(2)}, u32[]{:S(2)}) collective-permute-start(bf16[4,128,128]{2,1,0:T(8,128)(2,1)S(1)} %get-tuple-element.126), channel_id=1, source_target_pairs={{0,4},{1,5},{4,0},{5,1},{8,9},{9,8},{12,13},{13,12},{2,6},{3,7},{6... | collective-permute-start | bytes 393224 | tf_op jit(solution)/shard_map/ppermute | solution.py:220
  6.0 0.6 %key.5 = (bf16[4,128,128]{2,1,0:T(8,128)(2,1)S(1)}, bf16[4,256,128]{2,1,0:T(8,128)(2,1)S(1)}, bf16[4,256,128]{2,1,0:T(8,128)(2,1)S(1)}, f32[4,256,128]{2,1,0:T(8,128)S(1)}) custom-call(f32[4096,128]{1,0:T(8,128)S(1)} %get-tuple-element.139.refs_0_, f32[4096,128]{1,0:T(8,128)S(1)} %get-tuple-element.128.refs_1_), custom_call_target="tpu_custom_call" | custom-call | flops 33554432 | bytes 4194304 | tf_op jit(solution)/shard_map/key/pallas_call | solution.py:201
  6.7 0.6 %key.6 = (bf16[4,128,128]{2,1,0:T(8,128)(2,1)S(1)}, bf16[4,256,128]{2,1,0:T(8,128)(2,1)S(1)}, bf16[4,256,128]{2,1,0:T(8,128)(2,1)S(1)}, f32[4,256,128]{2,1,0:T(8,128)S(1)}) custom-call(f32[4096,128]{1,0:T(8,128)S(1)} %get-tuple-element.139.refs_0_, f32[4096,128]{1,0:T(8,128)S(1)} %get-tuple-element.128.refs_1_), custom_call_target="tpu_custom_call" | custom-call | flops 33554432 | bytes 4194304 | tf_op jit(solution)/shard_map/key/pallas_call | solution.py:201
  8.2 1.1 %query.4 = (f32[4,256,128]{2,1,0:T(8,128)S(1)}, bf16[4,256,128]{2,1,0:T(8,128)(2,1)S(1)}, bf16[4,256,128]{2,1,0:T(8,128)(2,1)S(1)}, f32[4,256,128]{2,1,0:T(8,128...) custom-call(bf16[4096,128]{1,0:T(8,128)(2,1)S(1)} %bitcast.8, ...), custom_call_target="tpu_custom_call" | custom-call | flops 134217728 | bytes 2621440 | tf_op jit(solution)/shard_map/query/pallas_call | solution.py:201
  9.3 0.6 %key.7 = (bf16[4,128,128]{2,1,0:T(8,128)(2,1)S(1)}, bf16[4,256,128]{2,1,0:T(8,128)(2,1)S(1)}, bf16[4,256,128]{2,1,0:T(8,128)(2,1)S(1)}, f32[4,256,128]{2,1,0:T(8,128)S(1)}) custom-call(f32[4096,128]{1,0:T(8,128)S(1)} %get-tuple-element.139.refs_0_, f32[4096,128]{1,0:T(8,128)S(1)} %get-tuple-element.128.refs_1_), custom_call_target="tpu_custom_call" | custom-call | flops 33554432 | bytes 4194304 | tf_op jit(solution)/shard_map/key/pallas_call | solution.py:201
  9.9 1.2 %collective-permute-start.4 = (bf16[4,128,128]{2,1,0:T(8,128)(2,1)S(1)}, bf16[4,128,128]{2,1,0:T(8,128)(2,1)S(1)}, u32[]{:S(2)}, u32[]{:S(2)}) collective-permute-start(bf16[4,128,128]{2,1,0:T(8,128)(2,1)S(1)} %get-tuple-element.141.part_ref), channel_id=1, source_target_pairs={{0,4},{1,5},{4,0},{5,1},{8,9},{9,8},{12,13},{13,12},{2,6},{3,7},{6... | collective-permute-start | bytes 393224 | tf_op jit(solution)/shard_map/ppermute | solution.py:220
  11.2 1.4 %collective-permute-start.2 = (bf16[4,128,128]{2,1,0:T(8,128)(2,1)S(1)}, bf16[4,128,128]{2,1,0:T(8,128)(2,1)S(1)}, u32[]{:S(2)}, u32[]{:S(2)}) collective-permute-start(bf16[4,128,128]{2,1,0:T(8,128)(2,1)S(1)} %get-tuple-element.143.part_ref), channel_id=1, source_target_pairs={{0,4},{1,5},{4,0},{5,1},{8,9},{9,8},{12,13},{13,12},{2,6},{3,7},{6... | collective-permute-start | bytes 393224 | tf_op jit(solution)/shard_map/ppermute | solution.py:220
  12.8 0.8 %query.5 = (f32[4,256,128]{2,1,0:T(8,128)S(1)}, bf16[4,256,128]{2,1,0:T(8,128)(2,1)S(1)}, bf16[4,256,128]{2,1,0:T(8,128)(2,1)S(1)}, f32[4,256,128]{2,1,0:T(8,128)S(1)}, bf16[4,256,256]{2,1,0:T(8,128)(2,1)S(1)}) custom-call(f32[4096,128]{1,0:T(8,128)S(1)} %get-tuple-element.135.refs_0_, f32[4096,128]{1,0:T(8,128)S(1)} %get-tuple-element.136.refs_1_, ...), custom_call_target="tpu_custom_call" | custom-call | flops 134217728 | bytes 4718592 | tf_op jit(solution)/shard_map/query/pallas_call | solution.py:201
  13.7 0.6 %collective-permute-start.7 = (bf16[4,128,128]{2,1,0:T(8,128)(2,1)S(1)}, bf16[4,128,128]{2,1,0:T(8,128)(2,1)S(1)}, u32[]{:S(2)}, u32[]{:S(2)}) collective-permute-start(bf16[4,128,128]{2,1,0:T(8,128)(2,1)S(1)} %fusion.1), channel_id=1, source_target_pairs={{0,1},{1,0},{4,5},{5,4},{8,12},{9,13},{12,8},{13,9},{2,3},{3,2},{6... | collective-permute-start | bytes 393224 | tf_op jit(solution)/shard_map/ppermute | solution.py:220
  14.2 1.8 %collective-permute-done.4.rest_0_ = bf16[4,128,128]{2,1,0:T(8,128)(2,1)S(1)} collective-permute-done((bf16[4,128,128]{2,1,0:T(8,128)(2,1)S(1)}, bf16[4,128,128]{2,1,0:T(8,128)(2,1)S(1)}, u32[]{:S(2)}, u32[]{:S(2)}) %collective-permute-start.4) | collective-permute-done | bytes 131104 | tf_op jit(solution)/shard_map/ppermute | solution.py:220
  16.1 0.8 %query.6 = (f32[4,256,128]{2,1,0:T(8,128)S(1)}, bf16[4,256,128]{2,1,0:T(8,128)(2,1)S(1)}, bf16[4,256,128]{2,1,0:T(8,128)(2,1)S(1)}, f32[4,256,128]{2,1,0:T(8,128)S(1)}, bf16[4,256,256]{2,1,0:T(8,128)(2,1)S(1)}) custom-call(f32[4096,128]{1,0:T(8,128)S(1)} %get-tuple-element.135.refs_0_, f32[4096,128]{1,0:T(8,128)S(1)} %get-tuple-element.136.refs_1_, ...), custom_call_target="tpu_custom_call" | custom-call | flops 134217728 | bytes 4718592 | tf_op jit(solution)/shard_map/query/pallas_call | solution.py:201
  17.0 0.6 %collective-permute-start.9 = (bf16[4,128,128]{2,1,0:T(8,128)(2,1)S(1)}, bf16[4,128,128]{2,1,0:T(8,128)(2,1)S(1)}, u32[]{:S(2)}, u32[]{:S(2)}) collective-permute-start(bf16[4,128,128]{2,1,0:T(8,128)(2,1)S(1)} %fusion.3), channel_id=1, source_target_pairs={{0,1},{1,0},{4,5},{5,4},{8,12},{9,13},{12,8},{13,9},{2,3},{3,2},{6... | collective-permute-start | bytes 393224 | tf_op jit(solution)/shard_map/ppermute | solution.py:220
  18.1 0.9 %norm.4 = (bf16[4,128,128]{2,1,0:T(8,128)(2,1)S(1)}, bf16[4,256,128]{2,1,0:T(8,128)(2,1)S(1)}, bf16[4,128,128]{2,1,0:T(8,128)(2,1)S(1)}, f32[4096,128]{1,0:T(8,128)S(1)}) custom-call(bf16[4,256,128]{2,1,0:T(8,128)(2,1)S(1)} %get-tuple-element.161.fq_ref, bf16[4,256,128]{2,1,0:T(8,128)(2,1)S(1)} %get-tuple-element.164.gh_ref, ...), custom_call_target="tpu_custom_call" | custom-call | flops 67108864 | bytes 1441792 | tf_op jit(solution)/shard_map/norm/pallas_call | solution.py:201
  19.6 1.4 %back.4 = (f32[4,256,128]{2,1,0:T(8,128)S(1)}, f32[4,256,128]{2,1,0:T(8,128)S(1)}, f32[4096,128]{1,0:T(8,128)S(1)}) custom-call(bf16[4,256,128]{2,1,0:T(8,128)(2,1)S(1)} %get-tuple-element.161.fq_ref, bf16[4,256,128]{2,1,0:T(8,128)(2,1)S(1)} %get-tuple-element.133.refs_2_.fk_ref, bf16[4,256,128]{2,1,0:T(8,128)(2,1)S(1)} %get-tuple-element.134.refs_3_.vh_ref, ...), custom_call_target="tpu_custom_call" | custom-call | flops 301989888 | bytes 2228224 | tf_op jit(solution)/shard_map/back/pallas_call | solution.py:201
  21.0 0.9 %norm.5 = (bf16[4,128,128]{2,1,0:T(8,128)(2,1)S(1)}, bf16[4,256,128]{2,1,0:T(8,128)(2,1)S(1)}, bf16[4,128,128]{2,1,0:T(8,128)(2,1)S(1)}, f32[4096,128]{1,0:T(8,128)S(1)}) custom-call(bf16[4,256,128]{2,1,0:T(8,128)(2,1)S(1)} %get-tuple-element.159.fq_ref, bf16[4,256,128]{2,1,0:T(8,128)(2,1)S(1)} %get-tuple-element.160.gh_ref, ...), custom_call_target="tpu_custom_call", output_to_operand_aliasing={{3}: (6, {})} | custom-call | flops 67108864 | bytes 3538944 | tf_op jit(solution)/shard_map/norm/pallas_call | solution.py:201
  22.0 0.8 %query.7 = (f32[4,256,128]{2,1,0:T(8,128)S(1)}, bf16[4,256,128]{2,1,0:T(8,128)(2,1)S(1)}, bf16[4,256,128]{2,1,0:T(8,128)(2,1)S(1)}, f32[4,256,128]{2,1,0:T(8,128)S(1)}, bf16[4,256,256]{2,1,0:T(8,128)(2,1)S(1)}) custom-call(f32[4096,128]{1,0:T(8,128)S(1)} %get-tuple-element.135.refs_0_, f32[4096,128]{1,0:T(8,128)S(1)} %get-tuple-element.136.refs_1_, ...), custom_call_target="tpu_custom_call" | custom-call | flops 134217728 | bytes 4718592 | tf_op jit(solution)/shard_map/query/pallas_call | solution.py:201
  23.5 0.9 %norm.6 = (bf16[4,128,128]{2,1,0:T(8,128)(2,1)S(1)}, bf16[4,256,128]{2,1,0:T(8,128)(2,1)S(1)}, bf16[4,128,128]{2,1,0:T(8,128)(2,1)S(1)}, f32[4096,128]{1,0:T(8,128)S(1)}) custom-call(bf16[4,256,128]{2,1,0:T(8,128)(2,1)S(1)} %get-tuple-element.178.fq_ref, bf16[4,256,128]{2,1,0:T(8,128)(2,1)S(1)} %get-tuple-element.179.gh_ref, ...), custom_call_target="tpu_custom_call", output_to_operand_aliasing={{3}: (6, {})} | custom-call | flops 67108864 | bytes 3538944 | tf_op jit(solution)/shard_map/norm/pallas_call | solution.py:201
  25.1 0.9 %norm.7 = (bf16[4,128,128]{2,1,0:T(8,128)(2,1)S(1)}, bf16[4,256,128]{2,1,0:T(8,128)(2,1)S(1)}, bf16[4,128,128]{2,1,0:T(8,128)(2,1)S(1)}, f32[4096,128]{1,0:T(8,128)S(1)}) custom-call(bf16[4,256,128]{2,1,0:T(8,128)(2,1)S(1)} %get-tuple-element.147.fq_ref, bf16[4,256,128]{2,1,0:T(8,128)(2,1)S(1)} %get-tuple-element.148.gh_ref, ...), custom_call_target="tpu_custom_call", output_to_operand_aliasing={{3}: (6, {})} | custom-call | flops 67108864 | bytes 3538944 | tf_op jit(solution)/shard_map/norm/pallas_call | solution.py:201
  26.1 8.8 %collective-permute-start.19 = (bf16[4,128,128]{2,1,0:T(8,128)(2,1)S(1)}, bf16[4,128,128]{2,1,0:T(8,128)(2,1)S(1)}, u32[]{:S(2)}, u32[]{:S(2)}) collective-permute-start(bf16[4,128,128]{2,1,0:T(8,128)(2,1)S(1)} %fusion.5), channel_id=1, source_target_pairs={{0,4},{1,5},{4,0},{5,1},{8,9},{9,8},{12,13},{13,12},{2,6},{3,7},{6... | collective-permute-start | bytes 393224 | tf_op jit(solution)/shard_map/ppermute | solution.py:220
  35.2 2.8 %collective-permute-start.18 = (bf16[4,128,128]{2,1,0:T(8,128)(2,1)S(1)}, bf16[4,128,128]{2,1,0:T(8,128)(2,1)S(1)}, u32[]{:S(2)}, u32[]{:S(2)}) collective-permute-start(bf16[4,128,128]{2,1,0:T(8,128)(2,1)S(1)} %fusion.7), channel_id=1, source_target_pairs={{0,4},{1,5},{4,0},{5,1},{8,9},{9,8},{12,13},{13,12},{2,6},{3,7},{6... | collective-permute-start | bytes 393224 | tf_op jit(solution)/shard_map/ppermute | solution.py:220
  38.0 1.1 %gather.2 = bf16[4096,128]{1,0:T(8,128)(2,1)} custom-call(f32[4096,128]{1,0:T(8,128)S(1)} %get-tuple-element.195.refs_0_), custom_call_target="tpu_custom_call" | custom-call | flops 134217728 | bytes 2097152 | tf_op jit(solution)/shard_map/gather/pallas_call | solution.py:201
  39.5 1.6 %collective-permute-start.20 = (bf16[4,128,128]{2,1,0:T(8,128)(2,1)S(1)}, bf16[4,128,128]{2,1,0:T(8,128)(2,1)S(1)}, u32[]{:S(2)}, u32[]{:S(2)}) collective-permute-start(bf16[4,128,128]{2,1,0:T(8,128)(2,1)S(1)} %fusion.9), channel_id=1, source_target_pairs={{0,4},{1,5},{4,0},{5,1},{8,9},{9,8},{12,13},{13,12},{2,6},{3,7},{6... | collective-permute-start | bytes 393224 | tf_op jit(solution)/shard_map/ppermute | solution.py:220
  41.0 1.4 %back.5 = (f32[4,256,128]{2,1,0:T(8,128)S(1)}, f32[4,256,128]{2,1,0:T(8,128)S(1)}, f32[4096,128]{1,0:T(8,128)S(1)}) custom-call(bf16[4,256,128]{2,1,0:T(8,128)(2,1)S(1)} %get-tuple-element.147.fq_ref, bf16[4,256,128]{2,1,0:T(8,128)(2,1)S(1)} %get-tuple-element.145.refs_2_.fk_ref.refs_0_, ...), custom_call_target="tpu_custom_call", output_to_operand_aliasing={{2}: (7, {})} | custom-call | flops 301989888 | bytes 4325376 | tf_op jit(solution)/shard_map/back/pallas_call | solution.py:201
  42.4 1.4 %back.6 = (f32[4,256,128]{2,1,0:T(8,128)S(1)}, f32[4,256,128]{2,1,0:T(8,128)S(1)}, f32[4096,128]{1,0:T(8,128)S(1)}) custom-call(bf16[4,256,128]{2,1,0:T(8,128)(2,1)S(1)} %get-tuple-element.159.fq_ref, bf16[4,256,128]{2,1,0:T(8,128)(2,1)S(1)} %get-tuple-element.154.refs_2_.fk_ref, ...), custom_call_target="tpu_custom_call", output_to_operand_aliasing={{2}: (7, {})} | custom-call | flops 301989888 | bytes 4325376 | tf_op jit(solution)/shard_map/back/pallas_call | solution.py:201
  43.8 0.8 %collective-permute-start.21 = (bf16[4,128,128]{2,1,0:T(8,128)(2,1)S(1)}, bf16[4,128,128]{2,1,0:T(8,128)(2,1)S(1)}, u32[]{:S(2)}, u32[]{:S(2)}) collective-permute-start(bf16[4,128,128]{2,1,0:T(8,128)(2,1)S(1)} %fusion.11), channel_id=1, source_target_pairs={{0,4},{1,5},{4,0},{5,1},{8,9},{9,8},{12,13},{13,12},{2,6},{3,7},{6... | collective-permute-start | bytes 393224 | tf_op jit(solution)/shard_map/ppermute | solution.py:220
  44.6 1.4 %back.7 = (f32[4,256,128]{2,1,0:T(8,128)S(1)}, f32[4,256,128]{2,1,0:T(8,128)S(1)}, f32[4096,128]{1,0:T(8,128)S(1)}) custom-call(bf16[4,256,128]{2,1,0:T(8,128)(2,1)S(1)} %get-tuple-element.178.fq_ref, bf16[4,256,128]{2,1,0:T(8,128)(2,1)S(1)} %get-tuple-element.176.refs_2_.fk_ref, ...), custom_call_target="tpu_custom_call", output_to_operand_aliasing={{2}: (7, {})} | custom-call | flops 301989888 | bytes 4325376 | tf_op jit(solution)/shard_map/back/pallas_call | solution.py:201
  46.0 1.1 %gather.3 = bf16[4096,128]{1,0:T(8,128)(2,1)} custom-call(f32[4096,128]{1,0:T(8,128)S(1)} %get-tuple-element.221.refs_0_), custom_call_target="tpu_custom_call" | custom-call | flops 134217728 | bytes 2097152 | tf_op jit(solution)/shard_map/gather/pallas_call | solution.py:201
  47.1 0.7 %later.3 = (f32[4096,128]{1,0:T(8,128)S(1)}, f32[4096,128]{1,0:T(8,128)S(1)}) custom-call(bf16[4,256,128]{2,1,0:T(8,128)(2,1)S(1)} %get-tuple-element.154.refs_2_.fk_ref, bf16[4,256,128]{2,1,0:T(8,128)(2,1)S(1)} %get-tuple-element.155.refs_3_.vh_ref, f32[4,256,128]{2,1,0:T(8,128)S(1)} %get-tuple-element.228.slope_ref, ...), custom_call_target="tpu_custom_call" | custom-call | flops 67108864 | bytes 2490368 | tf_op jit(solution)/shard_map/later/pallas_call | solution.py:201
  47.8 0.7 %later.4 = (f32[4096,128]{1,0:T(8,128)S(1)}, f32[4096,128]{1,0:T(8,128)S(1)}) custom-call(bf16[4,256,128]{2,1,0:T(8,128)(2,1)S(1)} %get-tuple-element.133.refs_2_.fk_ref, bf16[4,256,128]{2,1,0:T(8,128)(2,1)S(1)} %get-tuple-element.134.refs_3_.vh_ref, f32[4,256,128]{2,1,0:T(8,128)S(1)} %get-tuple-element.226.slope_ref, ...), custom_call_target="tpu_custom_call", output_to_operand_aliasing={{0}: (8, {}), {1}: (9, {})} | custom-call | flops 67108864 | bytes 6684672 | tf_op jit(solution)/shard_map/later/pallas_call | solution.py:201
  48.5 0.7 %later.5 = (f32[4096,128]{1,0:T(8,128)S(1)}, f32[4096,128]{1,0:T(8,128)S(1)}) custom-call(bf16[4,256,128]{2,1,0:T(8,128)(2,1)S(1)} %get-tuple-element.176.refs_2_.fk_ref, bf16[4,256,128]{2,1,0:T(8,128)(2,1)S(1)} %get-tuple-element.177.refs_3_.vh_ref, f32[4,256,128]{2,1,0:T(8,128)S(1)} %get-tuple-element.224.slope_ref, ...), custom_call_target="tpu_custom_call", output_to_operand_aliasing={{0}: (8, {}), {1}: (9, {})} | custom-call | flops 67108864 | bytes 6684672 | tf_op jit(solution)/shard_map/later/pallas_call | solution.py:201
  49.2 1.7 %last.1 = (bf16[4096,128]{1,0:T(8,128)(2,1)}, bf16[4096,128]{1,0:T(8,128)(2,1)}) custom-call(bf16[4,256,128]{2,1,0:T(8,128)(2,1)S(1)} %get-tuple-element.145.refs_2_.fk_ref.refs_0_, bf16[4,256,128]{2,1,0:T(8,128)(2,1)S(1)} %get-tuple-element.146.refs_3_.vh_ref.refs_1_, f32[4,256,128]{2,1,0:T(8,128)S(1)} %get-tuple-element.222.refs_2_, ...), custom_call_target="tpu_custom_call" | custom-call | flops 67108864 | bytes 6684672 | tf_op jit(solution)/shard_map/last/pallas_call | solution.py:201
  (54 shorter events, 4.7 us)
Async XLA Ops:
  3.0 8.1 %collective-permute-start = (bf16[4,128,128]{2,1,0:T(8,128)(2,1)S(1)}, bf16[4,128,128]{2,1,0:T(8,128)(2,1)S(1)}, u32[]{:S(2)}, u32[]{:S(2)}) collective-permute-start(bf16[4,128,128]{2,1,0:T(8,128)(2,1)S(1)} %get-tuple-element.126), channel_id=1, source_target_pairs={{0,4},{1,5},{4,0},{5,1},{8,9},{9,8},{12,13},{13,12},{2,6},{3,7},{6... | collective-permute-start | bytes 393224 | tf_op jit(solution)/shard_map/ppermute | solution.py:220
  6.6 1.2 %copy-start = (bf16[1,256,16,128]{3,2,1,0:T(8,128)(2,1)S(1)}, bf16[1,256,16,128]{3,2,1,0:T(8,128)(2,1)}, u32[]{:S(2)}) copy-start(bf16[1,256,16,128]{3,2,1,0:T(8,128)(2,1)} %param.4) | copy-start | bytes 3145732
  6.6 1.5 %copy-start.1 = (bf16[1,256,16,128]{3,2,1,0:T(8,128)(2,1)S(1)}, bf16[1,256,16,128]{3,2,1,0:T(8,128)(2,1)}, u32[]{:S(2)}) copy-start(bf16[1,256,16,128]{3,2,1,0:T(8,128)(2,1)} %param.7) | copy-start | bytes 3145732
  7.3 5.4 %collective-permute-start.1 = (bf16[4,128,128]{2,1,0:T(8,128)(2,1)S(1)}, bf16[4,128,128]{2,1,0:T(8,128)(2,1)S(1)}, u32[]{:S(2)}, u32[]{:S(2)}) collective-permute-start(bf16[4,128,128]{2,1,0:T(8,128)(2,1)S(1)} %get-tuple-element.132), channel_id=1, source_target_pairs={{0,4},{1,5},{4,0},{5,1},{8,9},{9,8},{12,13},{13,12},{2,6},{3,7},{6... | collective-permute-start | bytes 393224 | tf_op jit(solution)/shard_map/ppermute | solution.py:220
  9.9 6.2 %collective-permute-start.4 = (bf16[4,128,128]{2,1,0:T(8,128)(2,1)S(1)}, bf16[4,128,128]{2,1,0:T(8,128)(2,1)S(1)}, u32[]{:S(2)}, u32[]{:S(2)}) collective-permute-start(bf16[4,128,128]{2,1,0:T(8,128)(2,1)S(1)} %get-tuple-element.141.part_ref), channel_id=1, source_target_pairs={{0,4},{1,5},{4,0},{5,1},{8,9},{9,8},{12,13},{13,12},{2,6},{3,7},{6... | collective-permute-start | bytes 393224 | tf_op jit(solution)/shard_map/ppermute | solution.py:220
  11.1 2.5 %collective-permute-start.3 = (bf16[4,128,128]{2,1,0:T(8,128)(2,1)S(1)}, bf16[4,128,128]{2,1,0:T(8,128)(2,1)S(1)}, u32[]{:S(2)}, u32[]{:S(2)}) collective-permute-start(bf16[4,128,128]{2,1,0:T(8,128)(2,1)S(1)} %fusion), channel_id=1, source_target_pairs={{0,1},{1,0},{4,8},{5,9},{8,4},{9,5},{12,13},{13,12},{2,3},{3,2},{6... | collective-permute-start | bytes 393224 | tf_op jit(solution)/shard_map/ppermute | solution.py:220
  11.2 6.8 %collective-permute-start.2 = (bf16[4,128,128]{2,1,0:T(8,128)(2,1)S(1)}, bf16[4,128,128]{2,1,0:T(8,128)(2,1)S(1)}, u32[]{:S(2)}, u32[]{:S(2)}) collective-permute-start(bf16[4,128,128]{2,1,0:T(8,128)(2,1)S(1)} %get-tuple-element.143.part_ref), channel_id=1, source_target_pairs={{0,4},{1,5},{4,0},{5,1},{8,9},{9,8},{12,13},{13,12},{2,6},{3,7},{6... | collective-permute-start | bytes 393224 | tf_op jit(solution)/shard_map/ppermute | solution.py:220
  12.7 4.3 %collective-permute-start.5 = (bf16[4,128,128]{2,1,0:T(8,128)(2,1)S(1)}, bf16[4,128,128]{2,1,0:T(8,128)(2,1)S(1)}, u32[]{:S(2)}, u32[]{:S(2)}) collective-permute-start(bf16[4,128,128]{2,1,0:T(8,128)(2,1)S(1)} %fusion.2), channel_id=1, source_target_pairs={{0,1},{1,0},{4,8},{5,9},{8,4},{9,5},{12,13},{13,12},{2,3},{3,2},{6... | collective-permute-start | bytes 393224 | tf_op jit(solution)/shard_map/ppermute | solution.py:220
  13.7 4.4 %collective-permute-start.7 = (bf16[4,128,128]{2,1,0:T(8,128)(2,1)S(1)}, bf16[4,128,128]{2,1,0:T(8,128)(2,1)S(1)}, u32[]{:S(2)}, u32[]{:S(2)}) collective-permute-start(bf16[4,128,128]{2,1,0:T(8,128)(2,1)S(1)} %fusion.1), channel_id=1, source_target_pairs={{0,1},{1,0},{4,5},{5,4},{8,12},{9,13},{12,8},{13,9},{2,3},{3,2},{6... | collective-permute-start | bytes 393224 | tf_op jit(solution)/shard_map/ppermute | solution.py:220
  16.1 2.9 %collective-permute-start.8 = (bf16[4,128,128]{2,1,0:T(8,128)(2,1)S(1)}, bf16[4,128,128]{2,1,0:T(8,128)(2,1)S(1)}, u32[]{:S(2)}, u32[]{:S(2)}) collective-permute-start(bf16[4,128,128]{2,1,0:T(8,128)(2,1)S(1)} %add_convert_fusion.1), channel_id=1, source_target_pairs={{0,1},{1,0},{4,8},{5,9},{8,4},{9,5},{12,13},{13,12},{2,3},{3,2},{6... | collective-permute-start | bytes 393224 | tf_op jit(solution)/shard_map/ppermute | solution.py:220
  17.0 3.9 %collective-permute-start.9 = (bf16[4,128,128]{2,1,0:T(8,128)(2,1)S(1)}, bf16[4,128,128]{2,1,0:T(8,128)(2,1)S(1)}, u32[]{:S(2)}, u32[]{:S(2)}) collective-permute-start(bf16[4,128,128]{2,1,0:T(8,128)(2,1)S(1)} %fusion.3), channel_id=1, source_target_pairs={{0,1},{1,0},{4,5},{5,4},{8,12},{9,13},{12,8},{13,9},{2,3},{3,2},{6... | collective-permute-start | bytes 393224 | tf_op jit(solution)/shard_map/ppermute | solution.py:220
  18.0 3.9 %collective-permute-start.6 = (bf16[4,128,128]{2,1,0:T(8,128)(2,1)S(1)}, bf16[4,128,128]{2,1,0:T(8,128)(2,1)S(1)}, u32[]{:S(2)}, u32[]{:S(2)}) collective-permute-start(bf16[4,128,128]{2,1,0:T(8,128)(2,1)S(1)} %add_convert_fusion), channel_id=1, source_target_pairs={{0,1},{1,0},{4,8},{5,9},{8,4},{9,5},{12,13},{13,12},{2,3},{3,2},{6... | collective-permute-start | bytes 393224 | tf_op jit(solution)/shard_map/ppermute | solution.py:220
  19.1 3.8 %collective-permute-start.10 = (bf16[4,128,128]{2,1,0:T(8,128)(2,1)S(1)}, bf16[4,128,128]{2,1,0:T(8,128)(2,1)S(1)}, u32[]{:S(2)}, u32[]{:S(2)}) collective-permute-start(bf16[4,128,128]{2,1,0:T(8,128)(2,1)S(1)} %merge.2), channel_id=1, source_target_pairs={{0,1},{1,0},{4,5},{5,4},{8,12},{9,13},{12,8},{13,9},{2,3},{3,2},{6... | collective-permute-start | bytes 393224 | tf_op jit(solution)/shard_map/ppermute | solution.py:220
  22.0 2.5 %collective-permute-start.11 = (bf16[4,128,128]{2,1,0:T(8,128)(2,1)S(1)}, bf16[4,128,128]{2,1,0:T(8,128)(2,1)S(1)}, u32[]{:S(2)}, u32[]{:S(2)}) collective-permute-start(bf16[4,128,128]{2,1,0:T(8,128)(2,1)S(1)} %merge.3), channel_id=1, source_target_pairs={{0,1},{1,0},{4,5},{5,4},{8,12},{9,13},{12,8},{13,9},{2,3},{3,2},{6... | collective-permute-start | bytes 393224 | tf_op jit(solution)/shard_map/ppermute | solution.py:220
  22.9 3.1 %collective-permute-start.12 = (bf16[4,128,128]{2,1,0:T(8,128)(2,1)S(1)}, bf16[4,128,128]{2,1,0:T(8,128)(2,1)S(1)}, u32[]{:S(2)}, u32[]{:S(2)}) collective-permute-start(bf16[4,128,128]{2,1,0:T(8,128)(2,1)S(1)} %fusion.4), channel_id=1, source_target_pairs={{0,1},{1,0},{4,8},{5,9},{8,4},{9,5},{12,13},{13,12},{2,3},{3,2},{6... | collective-permute-start | bytes 393224 | tf_op jit(solution)/shard_map/ppermute | solution.py:220
  24.4 10.5 %collective-permute-start.13 = (bf16[4,128,128]{2,1,0:T(8,128)(2,1)S(1)}, bf16[4,128,128]{2,1,0:T(8,128)(2,1)S(1)}, u32[]{:S(2)}, u32[]{:S(2)}) collective-permute-start(bf16[4,128,128]{2,1,0:T(8,128)(2,1)S(1)} %get-tuple-element.185), channel_id=1, source_target_pairs={{0,1},{1,0},{4,5},{5,4},{8,12},{9,13},{12,8},{13,9},{2,3},{3,2},{6... | collective-permute-start | bytes 393224 | tf_op jit(solution)/shard_map/ppermute | solution.py:220
  24.5 10.7 %collective-permute-start.14 = (bf16[4,128,128]{2,1,0:T(8,128)(2,1)S(1)}, bf16[4,128,128]{2,1,0:T(8,128)(2,1)S(1)}, u32[]{:S(2)}, u32[]{:S(2)}) collective-permute-start(bf16[4,128,128]{2,1,0:T(8,128)(2,1)S(1)} %fusion.6), channel_id=1, source_target_pairs={{0,1},{1,0},{4,8},{5,9},{8,4},{9,5},{12,13},{13,12},{2,3},{3,2},{6... | collective-permute-start | bytes 393224 | tf_op jit(solution)/shard_map/ppermute | solution.py:220
  26.0 13.1 %collective-permute-start.15 = (bf16[4,128,128]{2,1,0:T(8,128)(2,1)S(1)}, bf16[4,128,128]{2,1,0:T(8,128)(2,1)S(1)}, u32[]{:S(2)}, u32[]{:S(2)}) collective-permute-start(bf16[4,128,128]{2,1,0:T(8,128)(2,1)S(1)} %get-tuple-element.191), channel_id=1, source_target_pairs={{0,1},{1,0},{4,5},{5,4},{8,12},{9,13},{12,8},{13,9},{2,3},{3,2},{6... | collective-permute-start | bytes 393224 | tf_op jit(solution)/shard_map/ppermute | solution.py:220
  26.1 21.7 %collective-permute-start.19 = (bf16[4,128,128]{2,1,0:T(8,128)(2,1)S(1)}, bf16[4,128,128]{2,1,0:T(8,128)(2,1)S(1)}, u32[]{:S(2)}, u32[]{:S(2)}) collective-permute-start(bf16[4,128,128]{2,1,0:T(8,128)(2,1)S(1)} %fusion.5), channel_id=1, source_target_pairs={{0,4},{1,5},{4,0},{5,1},{8,9},{9,8},{12,13},{13,12},{2,6},{3,7},{6... | collective-permute-start | bytes 393224 | tf_op jit(solution)/shard_map/ppermute | solution.py:220
  34.9 4.5 %collective-permute-start.16 = (bf16[4,128,128]{2,1,0:T(8,128)(2,1)S(1)}, bf16[4,128,128]{2,1,0:T(8,128)(2,1)S(1)}, u32[]{:S(2)}, u32[]{:S(2)}) collective-permute-start(bf16[4,128,128]{2,1,0:T(8,128)(2,1)S(1)} %fusion.8), channel_id=1, source_target_pairs={{0,1},{1,0},{4,8},{5,9},{8,4},{9,5},{12,13},{13,12},{2,3},{3,2},{6... | collective-permute-start | bytes 393224 | tf_op jit(solution)/shard_map/ppermute | solution.py:220
  35.2 11.8 %collective-permute-start.18 = (bf16[4,128,128]{2,1,0:T(8,128)(2,1)S(1)}, bf16[4,128,128]{2,1,0:T(8,128)(2,1)S(1)}, u32[]{:S(2)}, u32[]{:S(2)}) collective-permute-start(bf16[4,128,128]{2,1,0:T(8,128)(2,1)S(1)} %fusion.7), channel_id=1, source_target_pairs={{0,4},{1,5},{4,0},{5,1},{8,9},{9,8},{12,13},{13,12},{2,6},{3,7},{6... | collective-permute-start | bytes 393224 | tf_op jit(solution)/shard_map/ppermute | solution.py:220
  39.2 4.6 %collective-permute-start.17 = (bf16[4,128,128]{2,1,0:T(8,128)(2,1)S(1)}, bf16[4,128,128]{2,1,0:T(8,128)(2,1)S(1)}, u32[]{:S(2)}, u32[]{:S(2)}) collective-permute-start(bf16[4,128,128]{2,1,0:T(8,128)(2,1)S(1)} %fusion.10), channel_id=1, source_target_pairs={{0,1},{1,0},{4,8},{5,9},{8,4},{9,5},{12,13},{13,12},{2,3},{3,2},{6... | collective-permute-start | bytes 393224 | tf_op jit(solution)/shard_map/ppermute | solution.py:220
  39.5 9.0 %collective-permute-start.20 = (bf16[4,128,128]{2,1,0:T(8,128)(2,1)S(1)}, bf16[4,128,128]{2,1,0:T(8,128)(2,1)S(1)}, u32[]{:S(2)}, u32[]{:S(2)}) collective-permute-start(bf16[4,128,128]{2,1,0:T(8,128)(2,1)S(1)} %fusion.9), channel_id=1, source_target_pairs={{0,4},{1,5},{4,0},{5,1},{8,9},{9,8},{12,13},{13,12},{2,6},{3,7},{6... | collective-permute-start | bytes 393224 | tf_op jit(solution)/shard_map/ppermute | solution.py:220
  43.8 5.4 %collective-permute-start.21 = (bf16[4,128,128]{2,1,0:T(8,128)(2,1)S(1)}, bf16[4,128,128]{2,1,0:T(8,128)(2,1)S(1)}, u32[]{:S(2)}, u32[]{:S(2)}) collective-permute-start(bf16[4,128,128]{2,1,0:T(8,128)(2,1)S(1)} %fusion.11), channel_id=1, source_target_pairs={{0,4},{1,5},{4,0},{5,1},{8,9},{9,8},{12,13},{13,12},{2,6},{3,7},{6... | collective-permute-start | bytes 393224 | tf_op jit(solution)/shard_map/ppermute | solution.py:220

commit v5 on v4

--- a/solution.py
+++ b/solution.py
@@ -14,9 +14,9 @@
 UNROLL = 4
 BLOCKS = 4
 ORDER = [
-    "k0", "u0", "k1", "k3", "u1", "q0", "k2", "u2", "u0", "u3", "u1", "q3", "u0", "u2",
-    "q1", "u1", "u3", "n0", "x20", "b0", "n1", "x31", "q2", "d0", "n2", "d2", "d1", "n3",
-    "d3", "d0", "d2", "d1", "g0", "d3", "d2", "b3", "b1", "d3", "b2", "g1", "l1", "l0",
+    "k0", "u0", "k2", "k1", "q0", "u1", "u2", "q1", "u0", "k3", "u3", "u1", "u0", "u2",
+    "q3", "u1", "u3", "n0", "x20", "q2", "n1", "x31", "b1", "d0", "n2", "d2", "d1", "n3",
+    "d3", "d0", "d2", "d1", "g0", "d3", "d2", "b3", "b0", "d3", "l1", "l0", "b2", "g1",
     "l2", "l3",
 ]
 

time: 51.3 us -> 50.8 us (level)
  starting transfers between devices: 23.6 us -> 20.7 us
  waiting for transfers between devices: 2.25 us -> 4.54 us
    ppermute x22, starting transfers between devices: 23.6 us -> 20.7 us  [swap(): return lax.ppermute(x, ('ctx', 'rep'), pairs)]
    ppermute x22, waiting for transfers between devices: 2.25 us -> 4.54 us  [swap(): return lax.ppermute(x, ('ctx', 'rep'), pairs)]
  transfers between devices with their start and end apart: 22 -> 22, of which waited for: 2 -> 3; matrix products, arithmetic and copies ran while one was open for 1% -> 1% of each run, Pallas kernels for 36% -> 37%
where the time goes in v5:
time: 50.8 us; the launch traced here: 50.6 us
  Pallas kernels  22.6 us (44%)
  starting transfers between devices  20.7 us (41%)
  waiting for transfers between devices  4.54 us (9%)
  between operations  1.24 us (2%)
  local copies, waits for them, and re-layouts  0.94 us (2%)
  other arithmetic  0.54 us (1%)
    pallas_call x24, Pallas kernels, call(): pl.pallas_call(body, out_shape=outs, in_specs=specs, out_specs=out_specs,...  22.6 us
    ppermute x22, starting transfers between devices, swap(): return lax.ppermute(x, ('ctx', 'rep'), pairs)  20.7 us
    ppermute x22, waiting for transfers between devices, swap(): return lax.ppermute(x, ('ctx', 'rep'), pairs)  4.54 us
  transfers between devices with their start and end apart: 22, of which 3 were waited for; matrix products, arithmetic and copies ran while one was open for 1% of the time, Pallas kernels for 37%

profile of v5, /device:TPU:0, one launch (start us, length us, event | category | flops | bytes accessed | tf_op | source)
XLA Modules:
  0.0 50.6 jit_solution(16114091113458162880)
XLA Ops:
  0.6 2.3 %key.4 = (bf16[4,128,128]{2,1,0:T(8,128)(2,1)S(1)}, bf16[4,256,128]{2,1,0:T(8,128)(2,1)S(1)}, bf16[4,256,128]{2,1,0:T(8,128)(2,1)S(1)}, f32[4,256,128]{2,1,0:T(8...) custom-call(bf16[4096,128]{1,0:T(8,128)(2,1)} %bitcast.12, bf16[4096,128]{1,0:T(8,128)(2,1)} %bitcast.13), custom_call_target="tpu_custom_call" | custom-call | flops 33554432 | bytes 2097152 | tf_op jit(solution)/shard_map/key/pallas_call | solution.py:201
  3.0 3.1 %collective-permute-start = (bf16[4,128,128]{2,1,0:T(8,128)(2,1)S(1)}, bf16[4,128,128]{2,1,0:T(8,128)(2,1)S(1)}, u32[]{:S(2)}, u32[]{:S(2)}) collective-permute-start(bf16[4,128,128]{2,1,0:T(8,128)(2,1)S(1)} %get-tuple-element.126), channel_id=1, source_target_pairs={{0,4},{1,5},{4,0},{5,1},{8,9},{9,8},{12,13},{13,12},{2,6},{3,7},{6... | collective-permute-start | bytes 393224 | tf_op jit(solution)/shard_map/ppermute | solution.py:220
  6.0 0.6 %key.5 = (bf16[4,128,128]{2,1,0:T(8,128)(2,1)S(1)}, bf16[4,256,128]{2,1,0:T(8,128)(2,1)S(1)}, bf16[4,256,128]{2,1,0:T(8,128)(2,1)S(1)}, f32[4,256,128]{2,1,0:T(8,128)S(1)}) custom-call(f32[4096,128]{1,0:T(8,128)S(1)} %get-tuple-element.144.refs_0_, f32[4096,128]{1,0:T(8,128)S(1)} %get-tuple-element.128.refs_1_), custom_call_target="tpu_custom_call" | custom-call | flops 33554432 | bytes 4194304 | tf_op jit(solution)/shard_map/key/pallas_call | solution.py:201
  6.7 0.6 %key.6 = (bf16[4,128,128]{2,1,0:T(8,128)(2,1)S(1)}, bf16[4,256,128]{2,1,0:T(8,128)(2,1)S(1)}, bf16[4,256,128]{2,1,0:T(8,128)(2,1)S(1)}, f32[4,256,128]{2,1,0:T(8,128)S(1)}) custom-call(f32[4096,128]{1,0:T(8,128)S(1)} %get-tuple-element.144.refs_0_, f32[4096,128]{1,0:T(8,128)S(1)} %get-tuple-element.128.refs_1_), custom_call_target="tpu_custom_call" | custom-call | flops 33554432 | bytes 4194304 | tf_op jit(solution)/shard_map/key/pallas_call | solution.py:201
  7.3 0.6 %copy-done = bf16[1,256,16,128]{3,2,1,0:T(8,128)(2,1)S(1)} copy-done((bf16[1,256,16,128]{3,2,1,0:T(8,128)(2,1)S(1)}, bf16[1,256,16,128]{3,2,1,0:T(8,128)(2,1)}, u32[]{:S(2)}) %copy-start) | copy-done | bytes 1048600
  8.2 1.1 %query.4 = (f32[4,256,128]{2,1,0:T(8,128)S(1)}, bf16[4,256,128]{2,1,0:T(8,128)(2,1)S(1)}, bf16[4,256,128]{2,1,0:T(8,128)(2,1)S(1)}, f32[4,256,128]{2,1,0:T(8,128...) custom-call(bf16[4096,128]{1,0:T(8,128)(2,1)S(1)} %bitcast.8, ...), custom_call_target="tpu_custom_call" | custom-call | flops 134217728 | bytes 2621440 | tf_op jit(solution)/shard_map/query/pallas_call | solution.py:201
  9.3 2.0 %collective-permute-start.3 = (bf16[4,128,128]{2,1,0:T(8,128)(2,1)S(1)}, bf16[4,128,128]{2,1,0:T(8,128)(2,1)S(1)}, u32[]{:S(2)}, u32[]{:S(2)}) collective-permute-start(bf16[4,128,128]{2,1,0:T(8,128)(2,1)S(1)} %get-tuple-element.139.part_ref), channel_id=1, source_target_pairs={{0,4},{1,5},{4,0},{5,1},{8,9},{9,8},{12,13},{13,12},{2,6},{3,7},{6... | collective-permute-start | bytes 393224 | tf_op jit(solution)/shard_map/ppermute | solution.py:220
  11.4 0.8 %query.5 = (f32[4,256,128]{2,1,0:T(8,128)S(1)}, bf16[4,256,128]{2,1,0:T(8,128)(2,1)S(1)}, bf16[4,256,128]{2,1,0:T(8,128)(2,1)S(1)}, f32[4,256,128]{2,1,0:T(8,128)S(1)}, bf16[4,256,256]{2,1,0:T(8,128)(2,1)S(1)}) custom-call(f32[4096,128]{1,0:T(8,128)S(1)} %get-tuple-element.134.refs_0_, f32[4096,128]{1,0:T(8,128)S(1)} %get-tuple-element.135.refs_1_, ...), custom_call_target="tpu_custom_call" | custom-call | flops 134217728 | bytes 4718592 | tf_op jit(solution)/shard_map/query/pallas_call | solution.py:201
  12.3 0.6 %key.7 = (bf16[4,128,128]{2,1,0:T(8,128)(2,1)S(1)}, bf16[4,256,128]{2,1,0:T(8,128)(2,1)S(1)}, bf16[4,256,128]{2,1,0:T(8,128)(2,1)S(1)}, f32[4,256,128]{2,1,0:T(8,128)S(1)}) custom-call(f32[4096,128]{1,0:T(8,128)S(1)} %get-tuple-element.144.refs_0_, f32[4096,128]{1,0:T(8,128)S(1)} %get-tuple-element.128.refs_1_), custom_call_target="tpu_custom_call" | custom-call | flops 33554432 | bytes 4194304 | tf_op jit(solution)/shard_map/key/pallas_call | solution.py:201
  13.1 2.6 %collective-permute-done.1.rest_0_ = bf16[4,128,128]{2,1,0:T(8,128)(2,1)S(1)} collective-permute-done((bf16[4,128,128]{2,1,0:T(8,128)(2,1)S(1)}, bf16[4,128,128]{2,1,0:T(8,128)(2,1)S(1)}, u32[]{:S(2)}, u32[]{:S(2)}) %collective-permute-start.1) | collective-permute-done | bytes 131104 | tf_op jit(solution)/shard_map/ppermute | solution.py:220
  16.4 1.6 %collective-permute-done.3.rest_0_ = bf16[4,128,128]{2,1,0:T(8,128)(2,1)S(1)} collective-permute-done((bf16[4,128,128]{2,1,0:T(8,128)(2,1)S(1)}, bf16[4,128,128]{2,1,0:T(8,128)(2,1)S(1)}, u32[]{:S(2)}, u32[]{:S(2)}) %collective-permute-start.3) | collective-permute-done | bytes 131104 | tf_op jit(solution)/shard_map/ppermute | solution.py:220
  18.2 0.8 %query.6 = (f32[4,256,128]{2,1,0:T(8,128)S(1)}, bf16[4,256,128]{2,1,0:T(8,128)(2,1)S(1)}, bf16[4,256,128]{2,1,0:T(8,128)(2,1)S(1)}, f32[4,256,128]{2,1,0:T(8,128)S(1)}, bf16[4,256,256]{2,1,0:T(8,128)(2,1)S(1)}) custom-call(f32[4096,128]{1,0:T(8,128)S(1)} %get-tuple-element.134.refs_0_, f32[4096,128]{1,0:T(8,128)S(1)} %get-tuple-element.135.refs_1_, ...), custom_call_target="tpu_custom_call" | custom-call | flops 134217728 | bytes 4718592 | tf_op jit(solution)/shard_map/query/pallas_call | solution.py:201
  19.1 0.6 %collective-permute-start.8 = (bf16[4,128,128]{2,1,0:T(8,128)(2,1)S(1)}, bf16[4,128,128]{2,1,0:T(8,128)(2,1)S(1)}, u32[]{:S(2)}, u32[]{:S(2)}) collective-permute-start(bf16[4,128,128]{2,1,0:T(8,128)(2,1)S(1)} %fusion.3), channel_id=1, source_target_pairs={{0,1},{1,0},{4,5},{5,4},{8,12},{9,13},{12,8},{13,9},{2,3},{3,2},{6... | collective-permute-start | bytes 393224 | tf_op jit(solution)/shard_map/ppermute | solution.py:220
  20.0 0.9 %norm.4 = (bf16[4,128,128]{2,1,0:T(8,128)(2,1)S(1)}, bf16[4,256,128]{2,1,0:T(8,128)(2,1)S(1)}, bf16[4,128,128]{2,1,0:T(8,128)(2,1)S(1)}, f32[4096,128]{1,0:T(8,128)S(1)}) custom-call(bf16[4,256,128]{2,1,0:T(8,128)(2,1)S(1)} %get-tuple-element.157.fq_ref, bf16[4,256,128]{2,1,0:T(8,128)(2,1)S(1)} %get-tuple-element.158.gh_ref, ...), custom_call_target="tpu_custom_call" | custom-call | flops 67108864 | bytes 1441792 | tf_op jit(solution)/shard_map/norm/pallas_call | solution.py:201
  21.5 0.8 %query.7 = (f32[4,256,128]{2,1,0:T(8,128)S(1)}, bf16[4,256,128]{2,1,0:T(8,128)(2,1)S(1)}, bf16[4,256,128]{2,1,0:T(8,128)(2,1)S(1)}, f32[4,256,128]{2,1,0:T(8,128)S(1)}, bf16[4,256,256]{2,1,0:T(8,128)(2,1)S(1)}) custom-call(f32[4096,128]{1,0:T(8,128)S(1)} %get-tuple-element.134.refs_0_, f32[4096,128]{1,0:T(8,128)S(1)} %get-tuple-element.135.refs_1_, ...), custom_call_target="tpu_custom_call" | custom-call | flops 134217728 | bytes 4718592 | tf_op jit(solution)/shard_map/query/pallas_call | solution.py:201
  22.4 0.9 %norm.5 = (bf16[4,128,128]{2,1,0:T(8,128)(2,1)S(1)}, bf16[4,256,128]{2,1,0:T(8,128)(2,1)S(1)}, bf16[4,128,128]{2,1,0:T(8,128)(2,1)S(1)}, f32[4096,128]{1,0:T(8,128)S(1)}) custom-call(bf16[4,256,128]{2,1,0:T(8,128)(2,1)S(1)} %get-tuple-element.169.fq_ref, bf16[4,256,128]{2,1,0:T(8,128)(2,1)S(1)} %get-tuple-element.172.gh_ref, ...), custom_call_target="tpu_custom_call", output_to_operand_aliasing={{3}: (6, {})} | custom-call | flops 67108864 | bytes 3538944 | tf_op jit(solution)/shard_map/norm/pallas_call | solution.py:201
  23.4 1.4 %back.4 = (f32[4,256,128]{2,1,0:T(8,128)S(1)}, f32[4,256,128]{2,1,0:T(8,128)S(1)}, f32[4096,128]{1,0:T(8,128)S(1)}) custom-call(bf16[4,256,128]{2,1,0:T(8,128)(2,1)S(1)} %get-tuple-element.169.fq_ref, bf16[4,256,128]{2,1,0:T(8,128)(2,1)S(1)} %get-tuple-element.140.refs_2_.fk_ref, bf16[4,256,128]{2,1,0:T(8,128)(2,1)S(1)} %get-tuple-element.141.refs_3_.vh_ref, ...), custom_call_target="tpu_custom_call" | custom-call | flops 301989888 | bytes 2228224 | tf_op jit(solution)/shard_map/back/pallas_call | solution.py:201
  25.4 0.9 %norm.6 = (bf16[4,128,128]{2,1,0:T(8,128)(2,1)S(1)}, bf16[4,256,128]{2,1,0:T(8,128)(2,1)S(1)}, bf16[4,128,128]{2,1,0:T(8,128)(2,1)S(1)}, f32[4096,128]{1,0:T(8,128)S(1)}) custom-call(bf16[4,256,128]{2,1,0:T(8,128)(2,1)S(1)} %get-tuple-element.166.fq_ref, bf16[4,256,128]{2,1,0:T(8,128)(2,1)S(1)} %get-tuple-element.167.gh_ref, ...), custom_call_target="tpu_custom_call", output_to_operand_aliasing={{3}: (6, {})} | custom-call | flops 67108864 | bytes 3538944 | tf_op jit(solution)/shard_map/norm/pallas_call | solution.py:201
  27.0 0.9 %norm.7 = (bf16[4,128,128]{2,1,0:T(8,128)(2,1)S(1)}, bf16[4,256,128]{2,1,0:T(8,128)(2,1)S(1)}, bf16[4,128,128]{2,1,0:T(8,128)(2,1)S(1)}, f32[4096,128]{1,0:T(8,128)S(1)}) custom-call(bf16[4,256,128]{2,1,0:T(8,128)(2,1)S(1)} %get-tuple-element.153.fq_ref, bf16[4,256,128]{2,1,0:T(8,128)(2,1)S(1)} %get-tuple-element.154.gh_ref, ...), custom_call_target="tpu_custom_call", output_to_operand_aliasing={{3}: (6, {})} | custom-call | flops 67108864 | bytes 3538944 | tf_op jit(solution)/shard_map/norm/pallas_call | solution.py:201
  28.0 6.8 %collective-permute-start.19 = (bf16[4,128,128]{2,1,0:T(8,128)(2,1)S(1)}, bf16[4,128,128]{2,1,0:T(8,128)(2,1)S(1)}, u32[]{:S(2)}, u32[]{:S(2)}) collective-permute-start(bf16[4,128,128]{2,1,0:T(8,128)(2,1)S(1)} %fusion.5), channel_id=1, source_target_pairs={{0,4},{1,5},{4,0},{5,1},{8,9},{9,8},{12,13},{13,12},{2,6},{3,7},{6... | collective-permute-start | bytes 393224 | tf_op jit(solution)/shard_map/ppermute | solution.py:220
  35.0 2.6 %collective-permute-start.18 = (bf16[4,128,128]{2,1,0:T(8,128)(2,1)S(1)}, bf16[4,128,128]{2,1,0:T(8,128)(2,1)S(1)}, u32[]{:S(2)}, u32[]{:S(2)}) collective-permute-start(bf16[4,128,128]{2,1,0:T(8,128)(2,1)S(1)} %fusion.7), channel_id=1, source_target_pairs={{0,4},{1,5},{4,0},{5,1},{8,9},{9,8},{12,13},{13,12},{2,6},{3,7},{6... | collective-permute-start | bytes 393224 | tf_op jit(solution)/shard_map/ppermute | solution.py:220
  37.6 1.1 %gather.2 = bf16[4096,128]{1,0:T(8,128)(2,1)} custom-call(f32[4096,128]{1,0:T(8,128)S(1)} %get-tuple-element.195.refs_0_), custom_call_target="tpu_custom_call" | custom-call | flops 134217728 | bytes 2097152 | tf_op jit(solution)/shard_map/gather/pallas_call | solution.py:201
  39.0 1.5 %collective-permute-start.20 = (bf16[4,128,128]{2,1,0:T(8,128)(2,1)S(1)}, bf16[4,128,128]{2,1,0:T(8,128)(2,1)S(1)}, u32[]{:S(2)}, u32[]{:S(2)}) collective-permute-start(bf16[4,128,128]{2,1,0:T(8,128)(2,1)S(1)} %fusion.9), channel_id=1, source_target_pairs={{0,4},{1,5},{4,0},{5,1},{8,9},{9,8},{12,13},{13,12},{2,6},{3,7},{6... | collective-permute-start | bytes 393224 | tf_op jit(solution)/shard_map/ppermute | solution.py:220
  40.5 1.4 %back.5 = (f32[4,256,128]{2,1,0:T(8,128)S(1)}, f32[4,256,128]{2,1,0:T(8,128)S(1)}, f32[4096,128]{1,0:T(8,128)S(1)}) custom-call(bf16[4,256,128]{2,1,0:T(8,128)(2,1)S(1)} %get-tuple-element.153.fq_ref, bf16[4,256,128]{2,1,0:T(8,128)(2,1)S(1)} %get-tuple-element.151.refs_2_.fk_ref.refs_0_, ...), custom_call_target="tpu_custom_call", output_to_operand_aliasing={{2}: (7, {})} | custom-call | flops 301989888 | bytes 4325376 | tf_op jit(solution)/shard_map/back/pallas_call | solution.py:201
  41.9 1.4 %back.6 = (f32[4,256,128]{2,1,0:T(8,128)S(1)}, f32[4,256,128]{2,1,0:T(8,128)S(1)}, f32[4096,128]{1,0:T(8,128)S(1)}) custom-call(bf16[4,256,128]{2,1,0:T(8,128)(2,1)S(1)} %get-tuple-element.157.fq_ref, bf16[4,256,128]{2,1,0:T(8,128)(2,1)S(1)} %get-tuple-element.132.refs_2_.fk_ref, ...), custom_call_target="tpu_custom_call", output_to_operand_aliasing={{2}: (7, {})} | custom-call | flops 301989888 | bytes 4325376 | tf_op jit(solution)/shard_map/back/pallas_call | solution.py:201
  43.3 0.8 %collective-permute-start.21 = (bf16[4,128,128]{2,1,0:T(8,128)(2,1)S(1)}, bf16[4,128,128]{2,1,0:T(8,128)(2,1)S(1)}, u32[]{:S(2)}, u32[]{:S(2)}) collective-permute-start(bf16[4,128,128]{2,1,0:T(8,128)(2,1)S(1)} %fusion.11), channel_id=1, source_target_pairs={{0,4},{1,5},{4,0},{5,1},{8,9},{9,8},{12,13},{13,12},{2,6},{3,7},{6... | collective-permute-start | bytes 393224 | tf_op jit(solution)/shard_map/ppermute | solution.py:220
  44.2 0.7 %later.3 = (f32[4096,128]{1,0:T(8,128)S(1)}, f32[4096,128]{1,0:T(8,128)S(1)}) custom-call(bf16[4,256,128]{2,1,0:T(8,128)(2,1)S(1)} %get-tuple-element.140.refs_2_.fk_ref, bf16[4,256,128]{2,1,0:T(8,128)(2,1)S(1)} %get-tuple-element.141.refs_3_.vh_ref, f32[4,256,128]{2,1,0:T(8,128)S(1)} %get-tuple-element.218.slope_ref, ...), custom_call_target="tpu_custom_call" | custom-call | flops 67108864 | bytes 2490368 | tf_op jit(solution)/shard_map/later/pallas_call | solution.py:201
  44.9 0.7 %later.4 = (f32[4096,128]{1,0:T(8,128)S(1)}, f32[4096,128]{1,0:T(8,128)S(1)}) custom-call(bf16[4,256,128]{2,1,0:T(8,128)(2,1)S(1)} %get-tuple-element.132.refs_2_.fk_ref, bf16[4,256,128]{2,1,0:T(8,128)(2,1)S(1)} %get-tuple-element.133.refs_3_.vh_ref, f32[4,256,128]{2,1,0:T(8,128)S(1)} %get-tuple-element.200.slope_ref, ...), custom_call_target="tpu_custom_call", output_to_operand_aliasing={{0}: (8, {}), {1}: (9, {})} | custom-call | flops 67108864 | bytes 6684672 | tf_op jit(solution)/shard_map/later/pallas_call | solution.py:201
  45.6 1.4 %back.7 = (f32[4,256,128]{2,1,0:T(8,128)S(1)}, f32[4,256,128]{2,1,0:T(8,128)S(1)}, f32[4096,128]{1,0:T(8,128)S(1)}) custom-call(bf16[4,256,128]{2,1,0:T(8,128)(2,1)S(1)} %get-tuple-element.166.fq_ref, bf16[4,256,128]{2,1,0:T(8,128)(2,1)S(1)} %get-tuple-element.164.refs_2_.fk_ref, ...), custom_call_target="tpu_custom_call", output_to_operand_aliasing={{2}: (7, {})} | custom-call | flops 301989888 | bytes 4325376 | tf_op jit(solution)/shard_map/back/pallas_call | solution.py:201
  47.0 1.1 %gather.3 = bf16[4096,128]{1,0:T(8,128)(2,1)} custom-call(f32[4096,128]{1,0:T(8,128)S(1)} %get-tuple-element.230.refs_0_), custom_call_target="tpu_custom_call" | custom-call | flops 134217728 | bytes 2097152 | tf_op jit(solution)/shard_map/gather/pallas_call | solution.py:201
  48.0 0.7 %later.5 = (f32[4096,128]{1,0:T(8,128)S(1)}, f32[4096,128]{1,0:T(8,128)S(1)}) custom-call(bf16[4,256,128]{2,1,0:T(8,128)(2,1)S(1)} %get-tuple-element.164.refs_2_.fk_ref, bf16[4,256,128]{2,1,0:T(8,128)(2,1)S(1)} %get-tuple-element.165.refs_3_.vh_ref, f32[4,256,128]{2,1,0:T(8,128)S(1)} %get-tuple-element.233.slope_ref, ...), custom_call_target="tpu_custom_call", output_to_operand_aliasing={{0}: (8, {}), {1}: (9, {})} | custom-call | flops 67108864 | bytes 6684672 | tf_op jit(solution)/shard_map/later/pallas_call | solution.py:201
  48.7 1.7 %last.1 = (bf16[4096,128]{1,0:T(8,128)(2,1)}, bf16[4096,128]{1,0:T(8,128)(2,1)}) custom-call(bf16[4,256,128]{2,1,0:T(8,128)(2,1)S(1)} %get-tuple-element.151.refs_2_.fk_ref.refs_0_, bf16[4,256,128]{2,1,0:T(8,128)(2,1)S(1)} %get-tuple-element.152.refs_3_.vh_ref.refs_1_, f32[4,256,128]{2,1,0:T(8,128)S(1)} %get-tuple-element.231.refs_2_, ...), custom_call_target="tpu_custom_call" | custom-call | flops 67108864 | bytes 6684672 | tf_op jit(solution)/shard_map/last/pallas_call | solution.py:201
  (54 shorter events, 4.6 us)
Async XLA Ops:
  3.0 9.2 %collective-permute-start = (bf16[4,128,128]{2,1,0:T(8,128)(2,1)S(1)}, bf16[4,128,128]{2,1,0:T(8,128)(2,1)S(1)}, u32[]{:S(2)}, u32[]{:S(2)}) collective-permute-start(bf16[4,128,128]{2,1,0:T(8,128)(2,1)S(1)} %get-tuple-element.126), channel_id=1, source_target_pairs={{0,4},{1,5},{4,0},{5,1},{8,9},{9,8},{12,13},{13,12},{2,6},{3,7},{6... | collective-permute-start | bytes 393224 | tf_op jit(solution)/shard_map/ppermute | solution.py:220
  6.6 1.2 %copy-start = (bf16[1,256,16,128]{3,2,1,0:T(8,128)(2,1)S(1)}, bf16[1,256,16,128]{3,2,1,0:T(8,128)(2,1)}, u32[]{:S(2)}) copy-start(bf16[1,256,16,128]{3,2,1,0:T(8,128)(2,1)} %param.4) | copy-start | bytes 3145732
  6.6 1.5 %copy-start.1 = (bf16[1,256,16,128]{3,2,1,0:T(8,128)(2,1)S(1)}, bf16[1,256,16,128]{3,2,1,0:T(8,128)(2,1)}, u32[]{:S(2)}) copy-start(bf16[1,256,16,128]{3,2,1,0:T(8,128)(2,1)} %param.7) | copy-start | bytes 3145732
  9.3 6.4 %collective-permute-start.1 = (bf16[4,128,128]{2,1,0:T(8,128)(2,1)S(1)}, bf16[4,128,128]{2,1,0:T(8,128)(2,1)S(1)}, u32[]{:S(2)}, u32[]{:S(2)}) collective-permute-start(bf16[4,128,128]{2,1,0:T(8,128)(2,1)S(1)} %get-tuple-element.138), channel_id=1, source_target_pairs={{0,4},{1,5},{4,0},{5,1},{8,9},{9,8},{12,13},{13,12},{2,6},{3,7},{6... | collective-permute-start | bytes 393224 | tf_op jit(solution)/shard_map/ppermute | solution.py:220
  9.3 8.7 %collective-permute-start.3 = (bf16[4,128,128]{2,1,0:T(8,128)(2,1)S(1)}, bf16[4,128,128]{2,1,0:T(8,128)(2,1)S(1)}, u32[]{:S(2)}, u32[]{:S(2)}) collective-permute-start(bf16[4,128,128]{2,1,0:T(8,128)(2,1)S(1)} %get-tuple-element.139.part_ref), channel_id=1, source_target_pairs={{0,4},{1,5},{4,0},{5,1},{8,9},{9,8},{12,13},{13,12},{2,6},{3,7},{6... | collective-permute-start | bytes 393224 | tf_op jit(solution)/shard_map/ppermute | solution.py:220
  12.2 3.6 %collective-permute-start.2 = (bf16[4,128,128]{2,1,0:T(8,128)(2,1)S(1)}, bf16[4,128,128]{2,1,0:T(8,128)(2,1)S(1)}, u32[]{:S(2)}, u32[]{:S(2)}) collective-permute-start(bf16[4,128,128]{2,1,0:T(8,128)(2,1)S(1)} %fusion), channel_id=1, source_target_pairs={{0,1},{1,0},{4,8},{5,9},{8,4},{9,5},{12,13},{13,12},{2,3},{3,2},{6... | collective-permute-start | bytes 393224 | tf_op jit(solution)/shard_map/ppermute | solution.py:220
  12.9 7.0 %collective-permute-start.4 = (bf16[4,128,128]{2,1,0:T(8,128)(2,1)S(1)}, bf16[4,128,128]{2,1,0:T(8,128)(2,1)S(1)}, u32[]{:S(2)}, u32[]{:S(2)}) collective-permute-start(bf16[4,128,128]{2,1,0:T(8,128)(2,1)S(1)} %get-tuple-element.147.part_ref), channel_id=1, source_target_pairs={{0,4},{1,5},{4,0},{5,1},{8,9},{9,8},{12,13},{13,12},{2,6},{3,7},{6... | collective-permute-start | bytes 393224 | tf_op jit(solution)/shard_map/ppermute | solution.py:220
  15.7 3.3 %collective-permute-start.6 = (bf16[4,128,128]{2,1,0:T(8,128)(2,1)S(1)}, bf16[4,128,128]{2,1,0:T(8,128)(2,1)S(1)}, u32[]{:S(2)}, u32[]{:S(2)}) collective-permute-start(bf16[4,128,128]{2,1,0:T(8,128)(2,1)S(1)} %fusion.2), channel_id=1, source_target_pairs={{0,1},{1,0},{4,8},{5,9},{8,4},{9,5},{12,13},{13,12},{2,3},{3,2},{6... | collective-permute-start | bytes 393224 | tf_op jit(solution)/shard_map/ppermute | solution.py:220
  15.9 4.2 %collective-permute-start.7 = (bf16[4,128,128]{2,1,0:T(8,128)(2,1)S(1)}, bf16[4,128,128]{2,1,0:T(8,128)(2,1)S(1)}, u32[]{:S(2)}, u32[]{:S(2)}) collective-permute-start(bf16[4,128,128]{2,1,0:T(8,128)(2,1)S(1)} %fusion.1), channel_id=1, source_target_pairs={{0,1},{1,0},{4,5},{5,4},{8,12},{9,13},{12,8},{13,9},{2,3},{3,2},{6... | collective-permute-start | bytes 393224 | tf_op jit(solution)/shard_map/ppermute | solution.py:220
  18.1 2.8 %collective-permute-start.5 = (bf16[4,128,128]{2,1,0:T(8,128)(2,1)S(1)}, bf16[4,128,128]{2,1,0:T(8,128)(2,1)S(1)}, u32[]{:S(2)}, u32[]{:S(2)}) collective-permute-start(bf16[4,128,128]{2,1,0:T(8,128)(2,1)S(1)} %add_convert_fusion.1), channel_id=1, source_target_pairs={{0,1},{1,0},{4,8},{5,9},{8,4},{9,5},{12,13},{13,12},{2,3},{3,2},{6... | collective-permute-start | bytes 393224 | tf_op jit(solution)/shard_map/ppermute | solution.py:220
  19.1 3.3 %collective-permute-start.8 = (bf16[4,128,128]{2,1,0:T(8,128)(2,1)S(1)}, bf16[4,128,128]{2,1,0:T(8,128)(2,1)S(1)}, u32[]{:S(2)}, u32[]{:S(2)}) collective-permute-start(bf16[4,128,128]{2,1,0:T(8,128)(2,1)S(1)} %fusion.3), channel_id=1, source_target_pairs={{0,1},{1,0},{4,5},{5,4},{8,12},{9,13},{12,8},{13,9},{2,3},{3,2},{6... | collective-permute-start | bytes 393224 | tf_op jit(solution)/shard_map/ppermute | solution.py:220
  19.9 3.4 %collective-permute-start.9 = (bf16[4,128,128]{2,1,0:T(8,128)(2,1)S(1)}, bf16[4,128,128]{2,1,0:T(8,128)(2,1)S(1)}, u32[]{:S(2)}, u32[]{:S(2)}) collective-permute-start(bf16[4,128,128]{2,1,0:T(8,128)(2,1)S(1)} %add_convert_fusion), channel_id=1, source_target_pairs={{0,1},{1,0},{4,8},{5,9},{8,4},{9,5},{12,13},{13,12},{2,3},{3,2},{6... | collective-permute-start | bytes 393224 | tf_op jit(solution)/shard_map/ppermute | solution.py:220
  21.0 3.8 %collective-permute-start.10 = (bf16[4,128,128]{2,1,0:T(8,128)(2,1)S(1)}, bf16[4,128,128]{2,1,0:T(8,128)(2,1)S(1)}, u32[]{:S(2)}, u32[]{:S(2)}) collective-permute-start(bf16[4,128,128]{2,1,0:T(8,128)(2,1)S(1)} %merge.2), channel_id=1, source_target_pairs={{0,1},{1,0},{4,5},{5,4},{8,12},{9,13},{12,8},{13,9},{2,3},{3,2},{6... | collective-permute-start | bytes 393224 | tf_op jit(solution)/shard_map/ppermute | solution.py:220
  23.4 3.0 %collective-permute-start.11 = (bf16[4,128,128]{2,1,0:T(8,128)(2,1)S(1)}, bf16[4,128,128]{2,1,0:T(8,128)(2,1)S(1)}, u32[]{:S(2)}, u32[]{:S(2)}) collective-permute-start(bf16[4,128,128]{2,1,0:T(8,128)(2,1)S(1)} %merge.3), channel_id=1, source_target_pairs={{0,1},{1,0},{4,5},{5,4},{8,12},{9,13},{12,8},{13,9},{2,3},{3,2},{6... | collective-permute-start | bytes 393224 | tf_op jit(solution)/shard_map/ppermute | solution.py:220
  24.9 3.1 %collective-permute-start.12 = (bf16[4,128,128]{2,1,0:T(8,128)(2,1)S(1)}, bf16[4,128,128]{2,1,0:T(8,128)(2,1)S(1)}, u32[]{:S(2)}, u32[]{:S(2)}) collective-permute-start(bf16[4,128,128]{2,1,0:T(8,128)(2,1)S(1)} %fusion.4), channel_id=1, source_target_pairs={{0,1},{1,0},{4,8},{5,9},{8,4},{9,5},{12,13},{13,12},{2,3},{3,2},{6... | collective-permute-start | bytes 393224 | tf_op jit(solution)/shard_map/ppermute | solution.py:220
  26.3 8.5 %collective-permute-start.13 = (bf16[4,128,128]{2,1,0:T(8,128)(2,1)S(1)}, bf16[4,128,128]{2,1,0:T(8,128)(2,1)S(1)}, u32[]{:S(2)}, u32[]{:S(2)}) collective-permute-start(bf16[4,128,128]{2,1,0:T(8,128)(2,1)S(1)} %get-tuple-element.185), channel_id=1, source_target_pairs={{0,1},{1,0},{4,5},{5,4},{8,12},{9,13},{12,8},{13,9},{2,3},{3,2},{6... | collective-permute-start | bytes 393224 | tf_op jit(solution)/shard_map/ppermute | solution.py:220
  26.5 8.5 %collective-permute-start.14 = (bf16[4,128,128]{2,1,0:T(8,128)(2,1)S(1)}, bf16[4,128,128]{2,1,0:T(8,128)(2,1)S(1)}, u32[]{:S(2)}, u32[]{:S(2)}) collective-permute-start(bf16[4,128,128]{2,1,0:T(8,128)(2,1)S(1)} %fusion.6), channel_id=1, source_target_pairs={{0,1},{1,0},{4,8},{5,9},{8,4},{9,5},{12,13},{13,12},{2,3},{3,2},{6... | collective-permute-start | bytes 393224 | tf_op jit(solution)/shard_map/ppermute | solution.py:220
  27.9 10.8 %collective-permute-start.15 = (bf16[4,128,128]{2,1,0:T(8,128)(2,1)S(1)}, bf16[4,128,128]{2,1,0:T(8,128)(2,1)S(1)}, u32[]{:S(2)}, u32[]{:S(2)}) collective-permute-start(bf16[4,128,128]{2,1,0:T(8,128)(2,1)S(1)} %get-tuple-element.191), channel_id=1, source_target_pairs={{0,1},{1,0},{4,5},{5,4},{8,12},{9,13},{12,8},{13,9},{2,3},{3,2},{6... | collective-permute-start | bytes 393224 | tf_op jit(solution)/shard_map/ppermute | solution.py:220
  28.0 16.8 %collective-permute-start.19 = (bf16[4,128,128]{2,1,0:T(8,128)(2,1)S(1)}, bf16[4,128,128]{2,1,0:T(8,128)(2,1)S(1)}, u32[]{:S(2)}, u32[]{:S(2)}) collective-permute-start(bf16[4,128,128]{2,1,0:T(8,128)(2,1)S(1)} %fusion.5), channel_id=1, source_target_pairs={{0,4},{1,5},{4,0},{5,1},{8,9},{9,8},{12,13},{13,12},{2,6},{3,7},{6... | collective-permute-start | bytes 393224 | tf_op jit(solution)/shard_map/ppermute | solution.py:220
  34.8 4.2 %collective-permute-start.16 = (bf16[4,128,128]{2,1,0:T(8,128)(2,1)S(1)}, bf16[4,128,128]{2,1,0:T(8,128)(2,1)S(1)}, u32[]{:S(2)}, u32[]{:S(2)}) collective-permute-start(bf16[4,128,128]{2,1,0:T(8,128)(2,1)S(1)} %fusion.8), channel_id=1, source_target_pairs={{0,1},{1,0},{4,8},{5,9},{8,4},{9,5},{12,13},{13,12},{2,3},{3,2},{6... | collective-permute-start | bytes 393224 | tf_op jit(solution)/shard_map/ppermute | solution.py:220
  35.0 9.2 %collective-permute-start.18 = (bf16[4,128,128]{2,1,0:T(8,128)(2,1)S(1)}, bf16[4,128,128]{2,1,0:T(8,128)(2,1)S(1)}, u32[]{:S(2)}, u32[]{:S(2)}) collective-permute-start(bf16[4,128,128]{2,1,0:T(8,128)(2,1)S(1)} %fusion.7), channel_id=1, source_target_pairs={{0,4},{1,5},{4,0},{5,1},{8,9},{9,8},{12,13},{13,12},{2,6},{3,7},{6... | collective-permute-start | bytes 393224 | tf_op jit(solution)/shard_map/ppermute | solution.py:220
  38.7 4.5 %collective-permute-start.17 = (bf16[4,128,128]{2,1,0:T(8,128)(2,1)S(1)}, bf16[4,128,128]{2,1,0:T(8,128)(2,1)S(1)}, u32[]{:S(2)}, u32[]{:S(2)}) collective-permute-start(bf16[4,128,128]{2,1,0:T(8,128)(2,1)S(1)} %fusion.10), channel_id=1, source_target_pairs={{0,1},{1,0},{4,8},{5,9},{8,4},{9,5},{12,13},{13,12},{2,3},{3,2},{6... | collective-permute-start | bytes 393224 | tf_op jit(solution)/shard_map/ppermute | solution.py:220
  39.0 9.0 %collective-permute-start.20 = (bf16[4,128,128]{2,1,0:T(8,128)(2,1)S(1)}, bf16[4,128,128]{2,1,0:T(8,128)(2,1)S(1)}, u32[]{:S(2)}, u32[]{:S(2)}) collective-permute-start(bf16[4,128,128]{2,1,0:T(8,128)(2,1)S(1)} %fusion.9), channel_id=1, source_target_pairs={{0,4},{1,5},{4,0},{5,1},{8,9},{9,8},{12,13},{13,12},{2,6},{3,7},{6... | collective-permute-start | bytes 393224 | tf_op jit(solution)/shard_map/ppermute | solution.py:220
  43.3 5.4 %collective-permute-start.21 = (bf16[4,128,128]{2,1,0:T(8,128)(2,1)S(1)}, bf16[4,128,128]{2,1,0:T(8,128)(2,1)S(1)}, u32[]{:S(2)}, u32[]{:S(2)}) collective-permute-start(bf16[4,128,128]{2,1,0:T(8,128)(2,1)S(1)} %fusion.11), channel_id=1, source_target_pairs={{0,4},{1,5},{4,0},{5,1},{8,9},{9,8},{12,13},{13,12},{2,6},{3,7},{6... | collective-permute-start | bytes 393224 | tf_op jit(solution)/shard_map/ppermute | solution.py:220

commit v6 on v5

--- a/solution.py
+++ b/solution.py
@@ -12,7 +12,7 @@
 SCOPED = 12 * MIB
 SIZES = [4, 4, 4, 4]
 UNROLL = 4
-BLOCKS = 4
+BLOCKS = 2
 ORDER = [
     "k0", "u0", "k2", "k1", "q0", "u1", "u2", "q1", "u0", "k3", "u3", "u1", "u0", "u2",
     "q3", "u1", "u3", "n0", "x20", "q2", "n1", "x31", "b1", "d0", "n2", "d2", "d1", "n3",

time: 50.8 us -> 50.5 us (level)
  transfers between devices with their start and end apart: 22 -> 22, of which waited for: 3 -> 4; matrix products, arithmetic and copies ran while one was open for 1% -> 1% of each run, Pallas kernels for 37% -> 37%
where the time goes in v6:
time: 50.5 us; the launch traced here: 50.4 us
  Pallas kernels  22.5 us (45%)
  starting transfers between devices  20.4 us (40%)
  waiting for transfers between devices  4.72 us (9%)
  between operations  1.24 us (2%)
  local copies, waits for them, and re-layouts  0.93 us (2%)
  other arithmetic  0.54 us (1%)
    pallas_call x24, Pallas kernels, call(): pl.pallas_call(body, out_shape=outs, in_specs=specs, out_specs=out_specs,...  22.5 us
    ppermute x22, starting transfers between devices, swap(): return lax.ppermute(x, ('ctx', 'rep'), pairs)  20.4 us
    ppermute x22, waiting for transfers between devices, swap(): return lax.ppermute(x, ('ctx', 'rep'), pairs)  4.72 us
  transfers between devices with their start and end apart: 22, of which 4 were waited for; matrix products, arithmetic and copies ran while one was open for 1% of the time, Pallas kernels for 37%

profile of v6, /device:TPU:0, one launch (start us, length us, event | category | flops | bytes accessed | tf_op | source)
XLA Modules:
  0.0 50.4 jit_solution(17034550603428362352)
XLA Ops:
  0.6 2.2 %key.4 = (bf16[4,128,128]{2,1,0:T(8,128)(2,1)S(1)}, bf16[4,256,128]{2,1,0:T(8,128)(2,1)S(1)}, bf16[4,256,128]{2,1,0:T(8,128)(2,1)S(1)}, f32[4,256,128]{2,1,0:T(8...) custom-call(bf16[4096,128]{1,0:T(8,128)(2,1)} %bitcast.12, bf16[4096,128]{1,0:T(8,128)(2,1)} %bitcast.13), custom_call_target="tpu_custom_call" | custom-call | flops 33554432 | bytes 2097152 | tf_op jit(solution)/shard_map/key/pallas_call | solution.py:201
  2.8 3.1 %collective-permute-start = (bf16[4,128,128]{2,1,0:T(8,128)(2,1)S(1)}, bf16[4,128,128]{2,1,0:T(8,128)(2,1)S(1)}, u32[]{:S(2)}, u32[]{:S(2)}) collective-permute-start(bf16[4,128,128]{2,1,0:T(8,128)(2,1)S(1)} %get-tuple-element.126), channel_id=1, source_target_pairs={{0,4},{1,5},{4,0},{5,1},{8,9},{9,8},{12,13},{13,12},{2,6},{3,7},{6... | collective-permute-start | bytes 393224 | tf_op jit(solution)/shard_map/ppermute | solution.py:220
  5.9 0.6 %key.5 = (bf16[4,128,128]{2,1,0:T(8,128)(2,1)S(1)}, bf16[4,256,128]{2,1,0:T(8,128)(2,1)S(1)}, bf16[4,256,128]{2,1,0:T(8,128)(2,1)S(1)}, f32[4,256,128]{2,1,0:T(8,128)S(1)}) custom-call(f32[4096,128]{1,0:T(8,128)S(1)} %get-tuple-element.144.refs_0_, f32[4096,128]{1,0:T(8,128)S(1)} %get-tuple-element.128.refs_1_), custom_call_target="tpu_custom_call" | custom-call | flops 33554432 | bytes 4194304 | tf_op jit(solution)/shard_map/key/pallas_call | solution.py:201
  6.5 0.6 %key.6 = (bf16[4,128,128]{2,1,0:T(8,128)(2,1)S(1)}, bf16[4,256,128]{2,1,0:T(8,128)(2,1)S(1)}, bf16[4,256,128]{2,1,0:T(8,128)(2,1)S(1)}, f32[4,256,128]{2,1,0:T(8,128)S(1)}) custom-call(f32[4096,128]{1,0:T(8,128)S(1)} %get-tuple-element.144.refs_0_, f32[4096,128]{1,0:T(8,128)S(1)} %get-tuple-element.128.refs_1_), custom_call_target="tpu_custom_call" | custom-call | flops 33554432 | bytes 4194304 | tf_op jit(solution)/shard_map/key/pallas_call | solution.py:201
  7.1 0.6 %copy-done = bf16[1,256,16,128]{3,2,1,0:T(8,128)(2,1)S(1)} copy-done((bf16[1,256,16,128]{3,2,1,0:T(8,128)(2,1)S(1)}, bf16[1,256,16,128]{3,2,1,0:T(8,128)(2,1)}, u32[]{:S(2)}) %copy-start) | copy-done | bytes 1048600
  8.1 1.1 %query.4 = (f32[4,256,128]{2,1,0:T(8,128)S(1)}, bf16[4,256,128]{2,1,0:T(8,128)(2,1)S(1)}, bf16[4,256,128]{2,1,0:T(8,128)(2,1)S(1)}, f32[4,256,128]{2,1,0:T(8,128...) custom-call(bf16[4096,128]{1,0:T(8,128)(2,1)S(1)} %bitcast.8, ...), custom_call_target="tpu_custom_call" | custom-call | flops 134217728 | bytes 2621440 | tf_op jit(solution)/shard_map/query/pallas_call | solution.py:201
  9.2 2.0 %collective-permute-start.3 = (bf16[4,128,128]{2,1,0:T(8,128)(2,1)S(1)}, bf16[4,128,128]{2,1,0:T(8,128)(2,1)S(1)}, u32[]{:S(2)}, u32[]{:S(2)}) collective-permute-start(bf16[4,128,128]{2,1,0:T(8,128)(2,1)S(1)} %get-tuple-element.139.part_ref), channel_id=1, source_target_pairs={{0,4},{1,5},{4,0},{5,1},{8,9},{9,8},{12,13},{13,12},{2,6},{3,7},{6... | collective-permute-start | bytes 393224 | tf_op jit(solution)/shard_map/ppermute | solution.py:220
  11.2 0.8 %query.5 = (f32[4,256,128]{2,1,0:T(8,128)S(1)}, bf16[4,256,128]{2,1,0:T(8,128)(2,1)S(1)}, bf16[4,256,128]{2,1,0:T(8,128)(2,1)S(1)}, f32[4,256,128]{2,1,0:T(8,128)S(1)}, bf16[4,256,256]{2,1,0:T(8,128)(2,1)S(1)}) custom-call(f32[4096,128]{1,0:T(8,128)S(1)} %get-tuple-element.134.refs_0_, f32[4096,128]{1,0:T(8,128)S(1)} %get-tuple-element.135.refs_1_, ...), custom_call_target="tpu_custom_call" | custom-call | flops 134217728 | bytes 4718592 | tf_op jit(solution)/shard_map/query/pallas_call | solution.py:201
  12.2 0.6 %key.7 = (bf16[4,128,128]{2,1,0:T(8,128)(2,1)S(1)}, bf16[4,256,128]{2,1,0:T(8,128)(2,1)S(1)}, bf16[4,256,128]{2,1,0:T(8,128)(2,1)S(1)}, f32[4,256,128]{2,1,0:T(8,128)S(1)}) custom-call(f32[4096,128]{1,0:T(8,128)S(1)} %get-tuple-element.144.refs_0_, f32[4096,128]{1,0:T(8,128)S(1)} %get-tuple-element.128.refs_1_), custom_call_target="tpu_custom_call" | custom-call | flops 33554432 | bytes 4194304 | tf_op jit(solution)/shard_map/key/pallas_call | solution.py:201
  13.0 2.6 %collective-permute-done.1.rest_0_ = bf16[4,128,128]{2,1,0:T(8,128)(2,1)S(1)} collective-permute-done((bf16[4,128,128]{2,1,0:T(8,128)(2,1)S(1)}, bf16[4,128,128]{2,1,0:T(8,128)(2,1)S(1)}, u32[]{:S(2)}, u32[]{:S(2)}) %collective-permute-start.1) | collective-permute-done | bytes 131104 | tf_op jit(solution)/shard_map/ppermute | solution.py:220
  16.3 1.6 %collective-permute-done.3.rest_0_ = bf16[4,128,128]{2,1,0:T(8,128)(2,1)S(1)} collective-permute-done((bf16[4,128,128]{2,1,0:T(8,128)(2,1)S(1)}, bf16[4,128,128]{2,1,0:T(8,128)(2,1)S(1)}, u32[]{:S(2)}, u32[]{:S(2)}) %collective-permute-start.3) | collective-permute-done | bytes 131104 | tf_op jit(solution)/shard_map/ppermute | solution.py:220
  18.1 0.8 %query.6 = (f32[4,256,128]{2,1,0:T(8,128)S(1)}, bf16[4,256,128]{2,1,0:T(8,128)(2,1)S(1)}, bf16[4,256,128]{2,1,0:T(8,128)(2,1)S(1)}, f32[4,256,128]{2,1,0:T(8,128)S(1)}, bf16[4,256,256]{2,1,0:T(8,128)(2,1)S(1)}) custom-call(f32[4096,128]{1,0:T(8,128)S(1)} %get-tuple-element.134.refs_0_, f32[4096,128]{1,0:T(8,128)S(1)} %get-tuple-element.135.refs_1_, ...), custom_call_target="tpu_custom_call" | custom-call | flops 134217728 | bytes 4718592 | tf_op jit(solution)/shard_map/query/pallas_call | solution.py:201
  19.0 0.6 %collective-permute-start.8 = (bf16[4,128,128]{2,1,0:T(8,128)(2,1)S(1)}, bf16[4,128,128]{2,1,0:T(8,128)(2,1)S(1)}, u32[]{:S(2)}, u32[]{:S(2)}) collective-permute-start(bf16[4,128,128]{2,1,0:T(8,128)(2,1)S(1)} %fusion.3), channel_id=1, source_target_pairs={{0,1},{1,0},{4,5},{5,4},{8,12},{9,13},{12,8},{13,9},{2,3},{3,2},{6... | collective-permute-start | bytes 393224 | tf_op jit(solution)/shard_map/ppermute | solution.py:220
  19.9 0.9 %norm.4 = (bf16[4,128,128]{2,1,0:T(8,128)(2,1)S(1)}, bf16[4,256,128]{2,1,0:T(8,128)(2,1)S(1)}, bf16[4,128,128]{2,1,0:T(8,128)(2,1)S(1)}, f32[4096,128]{1,0:T(8,128)S(1)}) custom-call(bf16[4,256,128]{2,1,0:T(8,128)(2,1)S(1)} %get-tuple-element.157.fq_ref, bf16[4,256,128]{2,1,0:T(8,128)(2,1)S(1)} %get-tuple-element.158.gh_ref, ...), custom_call_target="tpu_custom_call" | custom-call | flops 67108864 | bytes 1441792 | tf_op jit(solution)/shard_map/norm/pallas_call | solution.py:201
  21.4 0.8 %query.7 = (f32[4,256,128]{2,1,0:T(8,128)S(1)}, bf16[4,256,128]{2,1,0:T(8,128)(2,1)S(1)}, bf16[4,256,128]{2,1,0:T(8,128)(2,1)S(1)}, f32[4,256,128]{2,1,0:T(8,128)S(1)}, bf16[4,256,256]{2,1,0:T(8,128)(2,1)S(1)}) custom-call(f32[4096,128]{1,0:T(8,128)S(1)} %get-tuple-element.134.refs_0_, f32[4096,128]{1,0:T(8,128)S(1)} %get-tuple-element.135.refs_1_, ...), custom_call_target="tpu_custom_call" | custom-call | flops 134217728 | bytes 4718592 | tf_op jit(solution)/shard_map/query/pallas_call | solution.py:201
  22.3 0.9 %norm.5 = (bf16[4,128,128]{2,1,0:T(8,128)(2,1)S(1)}, bf16[4,256,128]{2,1,0:T(8,128)(2,1)S(1)}, bf16[4,128,128]{2,1,0:T(8,128)(2,1)S(1)}, f32[4096,128]{1,0:T(8,128)S(1)}) custom-call(bf16[4,256,128]{2,1,0:T(8,128)(2,1)S(1)} %get-tuple-element.169.fq_ref, bf16[4,256,128]{2,1,0:T(8,128)(2,1)S(1)} %get-tuple-element.172.gh_ref, ...), custom_call_target="tpu_custom_call", output_to_operand_aliasing={{3}: (6, {})} | custom-call | flops 67108864 | bytes 3538944 | tf_op jit(solution)/shard_map/norm/pallas_call | solution.py:201
  23.3 1.4 %back.4 = (f32[4,256,128]{2,1,0:T(8,128)S(1)}, f32[4,256,128]{2,1,0:T(8,128)S(1)}, f32[4096,128]{1,0:T(8,128)S(1)}) custom-call(bf16[4,256,128]{2,1,0:T(8,128)(2,1)S(1)} %get-tuple-element.169.fq_ref, bf16[4,256,128]{2,1,0:T(8,128)(2,1)S(1)} %get-tuple-element.140.refs_2_.fk_ref, bf16[4,256,128]{2,1,0:T(8,128)(2,1)S(1)} %get-tuple-element.141.refs_3_.vh_ref, ...), custom_call_target="tpu_custom_call" | custom-call | flops 301989888 | bytes 2228224 | tf_op jit(solution)/shard_map/back/pallas_call | solution.py:201
  25.3 0.9 %norm.6 = (bf16[4,128,128]{2,1,0:T(8,128)(2,1)S(1)}, bf16[4,256,128]{2,1,0:T(8,128)(2,1)S(1)}, bf16[4,128,128]{2,1,0:T(8,128)(2,1)S(1)}, f32[4096,128]{1,0:T(8,128)S(1)}) custom-call(bf16[4,256,128]{2,1,0:T(8,128)(2,1)S(1)} %get-tuple-element.166.fq_ref, bf16[4,256,128]{2,1,0:T(8,128)(2,1)S(1)} %get-tuple-element.167.gh_ref, ...), custom_call_target="tpu_custom_call", output_to_operand_aliasing={{3}: (6, {})} | custom-call | flops 67108864 | bytes 3538944 | tf_op jit(solution)/shard_map/norm/pallas_call | solution.py:201
  26.9 0.9 %norm.7 = (bf16[4,128,128]{2,1,0:T(8,128)(2,1)S(1)}, bf16[4,256,128]{2,1,0:T(8,128)(2,1)S(1)}, bf16[4,128,128]{2,1,0:T(8,128)(2,1)S(1)}, f32[4096,128]{1,0:T(8,128)S(1)}) custom-call(bf16[4,256,128]{2,1,0:T(8,128)(2,1)S(1)} %get-tuple-element.153.fq_ref, bf16[4,256,128]{2,1,0:T(8,128)(2,1)S(1)} %get-tuple-element.154.gh_ref, ...), custom_call_target="tpu_custom_call", output_to_operand_aliasing={{3}: (6, {})} | custom-call | flops 67108864 | bytes 3538944 | tf_op jit(solution)/shard_map/norm/pallas_call | solution.py:201
  27.9 6.7 %collective-permute-start.19 = (bf16[4,128,128]{2,1,0:T(8,128)(2,1)S(1)}, bf16[4,128,128]{2,1,0:T(8,128)(2,1)S(1)}, u32[]{:S(2)}, u32[]{:S(2)}) collective-permute-start(bf16[4,128,128]{2,1,0:T(8,128)(2,1)S(1)} %fusion.5), channel_id=1, source_target_pairs={{0,4},{1,5},{4,0},{5,1},{8,9},{9,8},{12,13},{13,12},{2,6},{3,7},{6... | collective-permute-start | bytes 393224 | tf_op jit(solution)/shard_map/ppermute | solution.py:220
  34.8 2.6 %collective-permute-start.18 = (bf16[4,128,128]{2,1,0:T(8,128)(2,1)S(1)}, bf16[4,128,128]{2,1,0:T(8,128)(2,1)S(1)}, u32[]{:S(2)}, u32[]{:S(2)}) collective-permute-start(bf16[4,128,128]{2,1,0:T(8,128)(2,1)S(1)} %fusion.7), channel_id=1, source_target_pairs={{0,4},{1,5},{4,0},{5,1},{8,9},{9,8},{12,13},{13,12},{2,6},{3,7},{6... | collective-permute-start | bytes 393224 | tf_op jit(solution)/shard_map/ppermute | solution.py:220
  37.5 1.1 %gather.2 = bf16[4096,128]{1,0:T(8,128)(2,1)} custom-call(f32[4096,128]{1,0:T(8,128)S(1)} %get-tuple-element.195.refs_0_), custom_call_target="tpu_custom_call" | custom-call | flops 134217728 | bytes 2097152 | tf_op jit(solution)/shard_map/gather/pallas_call | solution.py:201
  38.9 1.5 %collective-permute-start.20 = (bf16[4,128,128]{2,1,0:T(8,128)(2,1)S(1)}, bf16[4,128,128]{2,1,0:T(8,128)(2,1)S(1)}, u32[]{:S(2)}, u32[]{:S(2)}) collective-permute-start(bf16[4,128,128]{2,1,0:T(8,128)(2,1)S(1)} %fusion.9), channel_id=1, source_target_pairs={{0,4},{1,5},{4,0},{5,1},{8,9},{9,8},{12,13},{13,12},{2,6},{3,7},{6... | collective-permute-start | bytes 393224 | tf_op jit(solution)/shard_map/ppermute | solution.py:220
  40.4 1.4 %back.5 = (f32[4,256,128]{2,1,0:T(8,128)S(1)}, f32[4,256,128]{2,1,0:T(8,128)S(1)}, f32[4096,128]{1,0:T(8,128)S(1)}) custom-call(bf16[4,256,128]{2,1,0:T(8,128)(2,1)S(1)} %get-tuple-element.153.fq_ref, bf16[4,256,128]{2,1,0:T(8,128)(2,1)S(1)} %get-tuple-element.151.refs_2_.fk_ref.refs_0_, ...), custom_call_target="tpu_custom_call", output_to_operand_aliasing={{2}: (7, {})} | custom-call | flops 301989888 | bytes 4325376 | tf_op jit(solution)/shard_map/back/pallas_call | solution.py:201
  41.8 1.4 %back.6 = (f32[4,256,128]{2,1,0:T(8,128)S(1)}, f32[4,256,128]{2,1,0:T(8,128)S(1)}, f32[4096,128]{1,0:T(8,128)S(1)}) custom-call(bf16[4,256,128]{2,1,0:T(8,128)(2,1)S(1)} %get-tuple-element.157.fq_ref, bf16[4,256,128]{2,1,0:T(8,128)(2,1)S(1)} %get-tuple-element.132.refs_2_.fk_ref, ...), custom_call_target="tpu_custom_call", output_to_operand_aliasing={{2}: (7, {})} | custom-call | flops 301989888 | bytes 4325376 | tf_op jit(solution)/shard_map/back/pallas_call | solution.py:201
  43.2 0.7 %collective-permute-start.21 = (bf16[4,128,128]{2,1,0:T(8,128)(2,1)S(1)}, bf16[4,128,128]{2,1,0:T(8,128)(2,1)S(1)}, u32[]{:S(2)}, u32[]{:S(2)}) collective-permute-start(bf16[4,128,128]{2,1,0:T(8,128)(2,1)S(1)} %fusion.11), channel_id=1, source_target_pairs={{0,4},{1,5},{4,0},{5,1},{8,9},{9,8},{12,13},{13,12},{2,6},{3,7},{6... | collective-permute-start | bytes 393224 | tf_op jit(solution)/shard_map/ppermute | solution.py:220
  43.9 0.7 %later.3 = (f32[4096,128]{1,0:T(8,128)S(1)}, f32[4096,128]{1,0:T(8,128)S(1)}) custom-call(bf16[4,256,128]{2,1,0:T(8,128)(2,1)S(1)} %get-tuple-element.140.refs_2_.fk_ref, bf16[4,256,128]{2,1,0:T(8,128)(2,1)S(1)} %get-tuple-element.141.refs_3_.vh_ref, f32[4,256,128]{2,1,0:T(8,128)S(1)} %get-tuple-element.218.slope_ref, ...), custom_call_target="tpu_custom_call" | custom-call | flops 67108864 | bytes 2490368 | tf_op jit(solution)/shard_map/later/pallas_call | solution.py:201
  44.6 0.7 %later.4 = (f32[4096,128]{1,0:T(8,128)S(1)}, f32[4096,128]{1,0:T(8,128)S(1)}) custom-call(bf16[4,256,128]{2,1,0:T(8,128)(2,1)S(1)} %get-tuple-element.132.refs_2_.fk_ref, bf16[4,256,128]{2,1,0:T(8,128)(2,1)S(1)} %get-tuple-element.133.refs_3_.vh_ref, f32[4,256,128]{2,1,0:T(8,128)S(1)} %get-tuple-element.200.slope_ref, ...), custom_call_target="tpu_custom_call", output_to_operand_aliasing={{0}: (8, {}), {1}: (9, {})} | custom-call | flops 67108864 | bytes 6684672 | tf_op jit(solution)/shard_map/later/pallas_call | solution.py:201
  45.3 1.4 %back.7 = (f32[4,256,128]{2,1,0:T(8,128)S(1)}, f32[4,256,128]{2,1,0:T(8,128)S(1)}, f32[4096,128]{1,0:T(8,128)S(1)}) custom-call(bf16[4,256,128]{2,1,0:T(8,128)(2,1)S(1)} %get-tuple-element.166.fq_ref, bf16[4,256,128]{2,1,0:T(8,128)(2,1)S(1)} %get-tuple-element.164.refs_2_.fk_ref, ...), custom_call_target="tpu_custom_call", output_to_operand_aliasing={{2}: (7, {})} | custom-call | flops 301989888 | bytes 4325376 | tf_op jit(solution)/shard_map/back/pallas_call | solution.py:201
  46.6 1.1 %gather.3 = bf16[4096,128]{1,0:T(8,128)(2,1)} custom-call(f32[4096,128]{1,0:T(8,128)S(1)} %get-tuple-element.230.refs_0_), custom_call_target="tpu_custom_call" | custom-call | flops 134217728 | bytes 2097152 | tf_op jit(solution)/shard_map/gather/pallas_call | solution.py:201
  47.7 0.7 %later.5 = (f32[4096,128]{1,0:T(8,128)S(1)}, f32[4096,128]{1,0:T(8,128)S(1)}) custom-call(bf16[4,256,128]{2,1,0:T(8,128)(2,1)S(1)} %get-tuple-element.164.refs_2_.fk_ref, bf16[4,256,128]{2,1,0:T(8,128)(2,1)S(1)} %get-tuple-element.165.refs_3_.vh_ref, f32[4,256,128]{2,1,0:T(8,128)S(1)} %get-tuple-element.233.slope_ref, ...), custom_call_target="tpu_custom_call", output_to_operand_aliasing={{0}: (8, {}), {1}: (9, {})} | custom-call | flops 67108864 | bytes 6684672 | tf_op jit(solution)/shard_map/later/pallas_call | solution.py:201
  48.4 1.8 %last.1 = (bf16[4096,128]{1,0:T(8,128)(2,1)}, bf16[4096,128]{1,0:T(8,128)(2,1)}) custom-call(bf16[4,256,128]{2,1,0:T(8,128)(2,1)S(1)} %get-tuple-element.151.refs_2_.fk_ref.refs_0_, bf16[4,256,128]{2,1,0:T(8,128)(2,1)S(1)} %get-tuple-element.152.refs_3_.vh_ref.refs_1_, f32[4,256,128]{2,1,0:T(8,128)S(1)} %get-tuple-element.231.refs_2_, ...), custom_call_target="tpu_custom_call" | custom-call | flops 67108864 | bytes 6684672 | tf_op jit(solution)/shard_map/last/pallas_call | solution.py:201
  (54 shorter events, 4.6 us)
Async XLA Ops:
  2.8 9.2 %collective-permute-start = (bf16[4,128,128]{2,1,0:T(8,128)(2,1)S(1)}, bf16[4,128,128]{2,1,0:T(8,128)(2,1)S(1)}, u32[]{:S(2)}, u32[]{:S(2)}) collective-permute-start(bf16[4,128,128]{2,1,0:T(8,128)(2,1)S(1)} %get-tuple-element.126), channel_id=1, source_target_pairs={{0,4},{1,5},{4,0},{5,1},{8,9},{9,8},{12,13},{13,12},{2,6},{3,7},{6... | collective-permute-start | bytes 393224 | tf_op jit(solution)/shard_map/ppermute | solution.py:220
  6.5 1.2 %copy-start = (bf16[1,256,16,128]{3,2,1,0:T(8,128)(2,1)S(1)}, bf16[1,256,16,128]{3,2,1,0:T(8,128)(2,1)}, u32[]{:S(2)}) copy-start(bf16[1,256,16,128]{3,2,1,0:T(8,128)(2,1)} %param.4) | copy-start | bytes 3145732
  6.5 1.5 %copy-start.1 = (bf16[1,256,16,128]{3,2,1,0:T(8,128)(2,1)S(1)}, bf16[1,256,16,128]{3,2,1,0:T(8,128)(2,1)}, u32[]{:S(2)}) copy-start(bf16[1,256,16,128]{3,2,1,0:T(8,128)(2,1)} %param.7) | copy-start | bytes 3145732
  9.1 6.4 %collective-permute-start.1 = (bf16[4,128,128]{2,1,0:T(8,128)(2,1)S(1)}, bf16[4,128,128]{2,1,0:T(8,128)(2,1)S(1)}, u32[]{:S(2)}, u32[]{:S(2)}) collective-permute-start(bf16[4,128,128]{2,1,0:T(8,128)(2,1)S(1)} %get-tuple-element.138), channel_id=1, source_target_pairs={{0,4},{1,5},{4,0},{5,1},{8,9},{9,8},{12,13},{13,12},{2,6},{3,7},{6... | collective-permute-start | bytes 393224 | tf_op jit(solution)/shard_map/ppermute | solution.py:220
  9.2 8.7 %collective-permute-start.3 = (bf16[4,128,128]{2,1,0:T(8,128)(2,1)S(1)}, bf16[4,128,128]{2,1,0:T(8,128)(2,1)S(1)}, u32[]{:S(2)}, u32[]{:S(2)}) collective-permute-start(bf16[4,128,128]{2,1,0:T(8,128)(2,1)S(1)} %get-tuple-element.139.part_ref), channel_id=1, source_target_pairs={{0,4},{1,5},{4,0},{5,1},{8,9},{9,8},{12,13},{13,12},{2,6},{3,7},{6... | collective-permute-start | bytes 393224 | tf_op jit(solution)/shard_map/ppermute | solution.py:220
  12.1 3.6 %collective-permute-start.2 = (bf16[4,128,128]{2,1,0:T(8,128)(2,1)S(1)}, bf16[4,128,128]{2,1,0:T(8,128)(2,1)S(1)}, u32[]{:S(2)}, u32[]{:S(2)}) collective-permute-start(bf16[4,128,128]{2,1,0:T(8,128)(2,1)S(1)} %fusion), channel_id=1, source_target_pairs={{0,1},{1,0},{4,8},{5,9},{8,4},{9,5},{12,13},{13,12},{2,3},{3,2},{6... | collective-permute-start | bytes 393224 | tf_op jit(solution)/shard_map/ppermute | solution.py:220
  12.8 7.0 %collective-permute-start.4 = (bf16[4,128,128]{2,1,0:T(8,128)(2,1)S(1)}, bf16[4,128,128]{2,1,0:T(8,128)(2,1)S(1)}, u32[]{:S(2)}, u32[]{:S(2)}) collective-permute-start(bf16[4,128,128]{2,1,0:T(8,128)(2,1)S(1)} %get-tuple-element.147.part_ref), channel_id=1, source_target_pairs={{0,4},{1,5},{4,0},{5,1},{8,9},{9,8},{12,13},{13,12},{2,6},{3,7},{6... | collective-permute-start | bytes 393224 | tf_op jit(solution)/shard_map/ppermute | solution.py:220
  15.6 3.3 %collective-permute-start.6 = (bf16[4,128,128]{2,1,0:T(8,128)(2,1)S(1)}, bf16[4,128,128]{2,1,0:T(8,128)(2,1)S(1)}, u32[]{:S(2)}, u32[]{:S(2)}) collective-permute-start(bf16[4,128,128]{2,1,0:T(8,128)(2,1)S(1)} %fusion.2), channel_id=1, source_target_pairs={{0,1},{1,0},{4,8},{5,9},{8,4},{9,5},{12,13},{13,12},{2,3},{3,2},{6... | collective-permute-start | bytes 393224 | tf_op jit(solution)/shard_map/ppermute | solution.py:220
  15.8 4.2 %collective-permute-start.7 = (bf16[4,128,128]{2,1,0:T(8,128)(2,1)S(1)}, bf16[4,128,128]{2,1,0:T(8,128)(2,1)S(1)}, u32[]{:S(2)}, u32[]{:S(2)}) collective-permute-start(bf16[4,128,128]{2,1,0:T(8,128)(2,1)S(1)} %fusion.1), channel_id=1, source_target_pairs={{0,1},{1,0},{4,5},{5,4},{8,12},{9,13},{12,8},{13,9},{2,3},{3,2},{6... | collective-permute-start | bytes 393224 | tf_op jit(solution)/shard_map/ppermute | solution.py:220
  18.0 2.8 %collective-permute-start.5 = (bf16[4,128,128]{2,1,0:T(8,128)(2,1)S(1)}, bf16[4,128,128]{2,1,0:T(8,128)(2,1)S(1)}, u32[]{:S(2)}, u32[]{:S(2)}) collective-permute-start(bf16[4,128,128]{2,1,0:T(8,128)(2,1)S(1)} %add_convert_fusion.1), channel_id=1, source_target_pairs={{0,1},{1,0},{4,8},{5,9},{8,4},{9,5},{12,13},{13,12},{2,3},{3,2},{6... | collective-permute-start | bytes 393224 | tf_op jit(solution)/shard_map/ppermute | solution.py:220
  19.0 3.3 %collective-permute-start.8 = (bf16[4,128,128]{2,1,0:T(8,128)(2,1)S(1)}, bf16[4,128,128]{2,1,0:T(8,128)(2,1)S(1)}, u32[]{:S(2)}, u32[]{:S(2)}) collective-permute-start(bf16[4,128,128]{2,1,0:T(8,128)(2,1)S(1)} %fusion.3), channel_id=1, source_target_pairs={{0,1},{1,0},{4,5},{5,4},{8,12},{9,13},{12,8},{13,9},{2,3},{3,2},{6... | collective-permute-start | bytes 393224 | tf_op jit(solution)/shard_map/ppermute | solution.py:220
  19.8 3.4 %collective-permute-start.9 = (bf16[4,128,128]{2,1,0:T(8,128)(2,1)S(1)}, bf16[4,128,128]{2,1,0:T(8,128)(2,1)S(1)}, u32[]{:S(2)}, u32[]{:S(2)}) collective-permute-start(bf16[4,128,128]{2,1,0:T(8,128)(2,1)S(1)} %add_convert_fusion), channel_id=1, source_target_pairs={{0,1},{1,0},{4,8},{5,9},{8,4},{9,5},{12,13},{13,12},{2,3},{3,2},{6... | collective-permute-start | bytes 393224 | tf_op jit(solution)/shard_map/ppermute | solution.py:220
  20.9 3.8 %collective-permute-start.10 = (bf16[4,128,128]{2,1,0:T(8,128)(2,1)S(1)}, bf16[4,128,128]{2,1,0:T(8,128)(2,1)S(1)}, u32[]{:S(2)}, u32[]{:S(2)}) collective-permute-start(bf16[4,128,128]{2,1,0:T(8,128)(2,1)S(1)} %merge.2), channel_id=1, source_target_pairs={{0,1},{1,0},{4,5},{5,4},{8,12},{9,13},{12,8},{13,9},{2,3},{3,2},{6... | collective-permute-start | bytes 393224 | tf_op jit(solution)/shard_map/ppermute | solution.py:220
  23.2 3.0 %collective-permute-start.11 = (bf16[4,128,128]{2,1,0:T(8,128)(2,1)S(1)}, bf16[4,128,128]{2,1,0:T(8,128)(2,1)S(1)}, u32[]{:S(2)}, u32[]{:S(2)}) collective-permute-start(bf16[4,128,128]{2,1,0:T(8,128)(2,1)S(1)} %merge.3), channel_id=1, source_target_pairs={{0,1},{1,0},{4,5},{5,4},{8,12},{9,13},{12,8},{13,9},{2,3},{3,2},{6... | collective-permute-start | bytes 393224 | tf_op jit(solution)/shard_map/ppermute | solution.py:220
  24.7 3.1 %collective-permute-start.12 = (bf16[4,128,128]{2,1,0:T(8,128)(2,1)S(1)}, bf16[4,128,128]{2,1,0:T(8,128)(2,1)S(1)}, u32[]{:S(2)}, u32[]{:S(2)}) collective-permute-start(bf16[4,128,128]{2,1,0:T(8,128)(2,1)S(1)} %fusion.4), channel_id=1, source_target_pairs={{0,1},{1,0},{4,8},{5,9},{8,4},{9,5},{12,13},{13,12},{2,3},{3,2},{6... | collective-permute-start | bytes 393224 | tf_op jit(solution)/shard_map/ppermute | solution.py:220
  26.2 8.5 %collective-permute-start.13 = (bf16[4,128,128]{2,1,0:T(8,128)(2,1)S(1)}, bf16[4,128,128]{2,1,0:T(8,128)(2,1)S(1)}, u32[]{:S(2)}, u32[]{:S(2)}) collective-permute-start(bf16[4,128,128]{2,1,0:T(8,128)(2,1)S(1)} %get-tuple-element.185), channel_id=1, source_target_pairs={{0,1},{1,0},{4,5},{5,4},{8,12},{9,13},{12,8},{13,9},{2,3},{3,2},{6... | collective-permute-start | bytes 393224 | tf_op jit(solution)/shard_map/ppermute | solution.py:220
  26.3 8.4 %collective-permute-start.14 = (bf16[4,128,128]{2,1,0:T(8,128)(2,1)S(1)}, bf16[4,128,128]{2,1,0:T(8,128)(2,1)S(1)}, u32[]{:S(2)}, u32[]{:S(2)}) collective-permute-start(bf16[4,128,128]{2,1,0:T(8,128)(2,1)S(1)} %fusion.6), channel_id=1, source_target_pairs={{0,1},{1,0},{4,8},{5,9},{8,4},{9,5},{12,13},{13,12},{2,3},{3,2},{6... | collective-permute-start | bytes 393224 | tf_op jit(solution)/shard_map/ppermute | solution.py:220
  27.8 10.7 %collective-permute-start.15 = (bf16[4,128,128]{2,1,0:T(8,128)(2,1)S(1)}, bf16[4,128,128]{2,1,0:T(8,128)(2,1)S(1)}, u32[]{:S(2)}, u32[]{:S(2)}) collective-permute-start(bf16[4,128,128]{2,1,0:T(8,128)(2,1)S(1)} %get-tuple-element.191), channel_id=1, source_target_pairs={{0,1},{1,0},{4,5},{5,4},{8,12},{9,13},{12,8},{13,9},{2,3},{3,2},{6... | collective-permute-start | bytes 393224 | tf_op jit(solution)/shard_map/ppermute | solution.py:220
  27.9 16.6 %collective-permute-start.19 = (bf16[4,128,128]{2,1,0:T(8,128)(2,1)S(1)}, bf16[4,128,128]{2,1,0:T(8,128)(2,1)S(1)}, u32[]{:S(2)}, u32[]{:S(2)}) collective-permute-start(bf16[4,128,128]{2,1,0:T(8,128)(2,1)S(1)} %fusion.5), channel_id=1, source_target_pairs={{0,4},{1,5},{4,0},{5,1},{8,9},{9,8},{12,13},{13,12},{2,6},{3,7},{6... | collective-permute-start | bytes 393224 | tf_op jit(solution)/shard_map/ppermute | solution.py:220
  34.7 4.1 %collective-permute-start.16 = (bf16[4,128,128]{2,1,0:T(8,128)(2,1)S(1)}, bf16[4,128,128]{2,1,0:T(8,128)(2,1)S(1)}, u32[]{:S(2)}, u32[]{:S(2)}) collective-permute-start(bf16[4,128,128]{2,1,0:T(8,128)(2,1)S(1)} %fusion.8), channel_id=1, source_target_pairs={{0,1},{1,0},{4,8},{5,9},{8,4},{9,5},{12,13},{13,12},{2,3},{3,2},{6... | collective-permute-start | bytes 393224 | tf_op jit(solution)/shard_map/ppermute | solution.py:220
  34.8 9.0 %collective-permute-start.18 = (bf16[4,128,128]{2,1,0:T(8,128)(2,1)S(1)}, bf16[4,128,128]{2,1,0:T(8,128)(2,1)S(1)}, u32[]{:S(2)}, u32[]{:S(2)}) collective-permute-start(bf16[4,128,128]{2,1,0:T(8,128)(2,1)S(1)} %fusion.7), channel_id=1, source_target_pairs={{0,4},{1,5},{4,0},{5,1},{8,9},{9,8},{12,13},{13,12},{2,6},{3,7},{6... | collective-permute-start | bytes 393224 | tf_op jit(solution)/shard_map/ppermute | solution.py:220
  38.6 4.6 %collective-permute-start.17 = (bf16[4,128,128]{2,1,0:T(8,128)(2,1)S(1)}, bf16[4,128,128]{2,1,0:T(8,128)(2,1)S(1)}, u32[]{:S(2)}, u32[]{:S(2)}) collective-permute-start(bf16[4,128,128]{2,1,0:T(8,128)(2,1)S(1)} %fusion.10), channel_id=1, source_target_pairs={{0,1},{1,0},{4,8},{5,9},{8,4},{9,5},{12,13},{13,12},{2,3},{3,2},{6... | collective-permute-start | bytes 393224 | tf_op jit(solution)/shard_map/ppermute | solution.py:220
  38.9 8.8 %collective-permute-start.20 = (bf16[4,128,128]{2,1,0:T(8,128)(2,1)S(1)}, bf16[4,128,128]{2,1,0:T(8,128)(2,1)S(1)}, u32[]{:S(2)}, u32[]{:S(2)}) collective-permute-start(bf16[4,128,128]{2,1,0:T(8,128)(2,1)S(1)} %fusion.9), channel_id=1, source_target_pairs={{0,4},{1,5},{4,0},{5,1},{8,9},{9,8},{12,13},{13,12},{2,6},{3,7},{6... | collective-permute-start | bytes 393224 | tf_op jit(solution)/shard_map/ppermute | solution.py:220
  43.2 5.2 %collective-permute-start.21 = (bf16[4,128,128]{2,1,0:T(8,128)(2,1)S(1)}, bf16[4,128,128]{2,1,0:T(8,128)(2,1)S(1)}, u32[]{:S(2)}, u32[]{:S(2)}) collective-permute-start(bf16[4,128,128]{2,1,0:T(8,128)(2,1)S(1)} %fusion.11), channel_id=1, source_target_pairs={{0,4},{1,5},{4,0},{5,1},{8,9},{9,8},{12,13},{13,12},{2,6},{3,7},{6... | collective-permute-start | bytes 393224 | tf_op jit(solution)/shard_map/ppermute | solution.py:220
